TPU v7x, 32 devices: a whole 2x2x4 slice. The times are simulated.
32 devices in a mesh: ctx: 16 (over z, x, core), ep: 2 (over y).
Axes of the slice: x: 2, y: 2, z: 4, core: 2. Of those that a mesh axis runs over, the one named last changes fastest.
Arguments:
- resid_in: bfloat16 [4096, 1024], P(('ctx', 'ep')), may hold values from -6 to 6
- out_grad: bfloat16 [4096, 1024], P(('ctx', 'ep')), may hold values from -6 to 6
- attn_gain: float32 [1024], replicated, may hold values from 0.5 to 1.5
- q_weight: bfloat16 [1024, 1024], P(None, 'ep'), may hold values from -0.1875 to 0.1875
- key_value_weight: bfloat16 [2, 1024, 512], P(None, None, 'ep'), may hold values from -0.1875 to 0.1875
- o_weight: bfloat16 [1024, 1024], P('ep'), may hold values from -1.5 to 1.5
- moe_gain: float32 [1024], replicated, may hold values from 0.5 to 1.5
- router: bfloat16 [1024, 16], replicated, may hold values from -0.09375 to 0.09375
- expert_in: bfloat16 [16, 1024, 1024], P('ep'), may hold values from -0.1875 to 0.1875
- expert_out: bfloat16 [16, 512, 1024], P('ep'), may hold values from -1 to 1
- qkv_down: bfloat16 [1024, 96], replicated, may hold values from -0.1875 to 0.1875
- q_up: bfloat16 [32, 1024], P(None, 'ep'), may hold values from -0.75 to 0.75
- key_value_up_factor: bfloat16 [2, 32, 512], P(None, None, 'ep'), may hold values from -0.75 to 0.75
- o_down: bfloat16 [1024, 32], P('ep'), may hold values from -1.5 to 1.5
- o_up: bfloat16 [32, 1024], replicated, may hold values from -0.75 to 0.75
- expert_in_down: bfloat16 [16, 1024, 64], P('ep'), may hold values from -0.1875 to 0.1875
- expert_in_up: bfloat16 [16, 2, 32, 512], P('ep'), may hold values from -0.75 to 0.75
- expert_out_down: bfloat16 [16, 512, 32], P('ep'), may hold values from -0.5 to 0.5
- expert_out_up: bfloat16 [16, 32, 1024], P('ep'), may hold values from -0.75 to 0.75
- expert_ids: int32 [4096, 8], P(('ctx', 'ep')), may hold values from 0 to 15, all different within a row; in each aligned block of 128 rows (0 to 127, 128 to 255, ...) at most 96 rows name the same one
- doc_starts: int32 [8], replicated, may hold values from 0 to 4095, as said below
- doc_adapter: int32 [8], replicated, may hold values from 0 to 1
Outputs:
- block_out: bfloat16 [4096, 1024], P(('ctx', 'ep'))
- in_grad: bfloat16 [4096, 1024], P(('ctx', 'ep'))
- grad_qkv_down: float32 [1024, 96], replicated
- grad_q_up: float32 [32, 1024], P(None, 'ep')
- grad_kv_up: float32 [2, 32, 512], P(None, None, 'ep')
- grad_o_down: float32 [1024, 32], P('ep')
- grad_o_up: float32 [32, 1024], replicated
- grad_expert_in_down: float32 [16, 1024, 64], P('ep')
- grad_expert_in_up: float32 [16, 2, 32, 512], P('ep')
- grad_expert_out_down: float32 [16, 512, 32], P('ep')
- grad_expert_out_up: float32 [16, 32, 1024], P('ep')
Inputs may be any that keep to these rules, and one draw needn't show every extreme that they name: `expert_ids`: each row names 8 different experts; among the rows of one device no expert is named by more than 96 rows, and in every draw some device has an expert named by exactly 96 rows. `doc_starts`: strictly increasing, the first is 0; one document begins within the first 256 tokens and ends within the last 256 tokens.
All inputs are finite; a program needn't handle non-finite values.
Results may differ from a plain program's by a relative error of at most 0.035.
Values may be sent and summed in bfloat16 or wider, within the bound.
A program may use at most 128 MiB of HBM per device.

v0:
```python
import jax
import jax.numpy as jnp
from jax import lax
from jax.sharding import PartitionSpec as P

HEAD_WIDTH = 64
FF = 512
ADAPTER_RANK = 16
ADAPTER_CHOICES = 2


norm_eps = 1e-06
masked_score = -1e30
score_scale = 0.125


def shifted_2(value, axis, steps):
    count = lax.axis_size(axis)
    pairs = [(source, (source + steps) % count) for source in range(count)]
    return lax.ppermute(value, axis, pairs)


def matrix_product(left, right):
    return jnp.dot(left, right, preferred_element_type=jnp.float32)


def matmul_tn(left, right):
    return lax.dot_general(
        left, right, (((0,), (0,)), ((), ())), preferred_element_type=jnp.float32
    )


def matmul_nt(left, right):
    return lax.dot_general(
        left, right, (((1,), (1,)), ((), ())), preferred_element_type=jnp.float32
    )


def rms_scale(values, gain):
    return values * lax.rsqrt(jnp.mean(values * values, axis=-1, keepdims=True) + norm_eps) * gain


def rms_back(values, gain, upstream):
    factor = lax.rsqrt(jnp.mean(values * values, axis=-1, keepdims=True) + norm_eps)
    scaled = upstream * gain
    return factor * scaled - values * factor * factor * factor * jnp.mean(
        scaled * values, axis=-1, keepdims=True
    )


def rope_tables(in_doc, width):
    half_width = width // 2
    steps_index = jnp.arange(half_width, dtype=jnp.float32)
    freq_table = jnp.power(10000.0, -2.0 * steps_index / width)
    angles = in_doc.astype(jnp.float32)[:, None] * freq_table[None, :]
    cosine_table = jnp.cos(angles)
    sine_table = jnp.sin(angles)
    return (
        jnp.concatenate([cosine_table, cosine_table], axis=1),
        jnp.concatenate([sine_table, sine_table], axis=1),
    )


def rotary_apply(values, cosine_table, sine_table):
    half_width = values.shape[-1] // 2
    turned = jnp.concatenate([-values[..., half_width:], values[..., :half_width]], axis=-1)
    return values * cosine_table[:, None, :] + turned * sine_table[:, None, :]


def unrotate(upstream, cosine_table, sine_table):
    half_width = upstream.shape[-1] // 2
    shifted = upstream * sine_table[:, None, :]
    return upstream * cosine_table[:, None, :] + jnp.concatenate(
        [shifted[..., half_width:], -shifted[..., :half_width]], axis=-1
    )


def doc_number(positions, doc_starts):
    opened = doc_starts[None, :] <= positions[:, None]
    return jnp.sum(opened.astype(jnp.int32), axis=1) - 1


def doc_layout(positions, doc_starts, doc_adapter):
    opened = doc_starts[None, :] <= positions[:, None]
    own_start = jnp.max(jnp.where(opened, doc_starts[None, :], 0), axis=1)
    doc_index = jnp.sum(opened.astype(jnp.int32), axis=1) - 1
    picked = jnp.arange(doc_starts.shape[0], dtype=jnp.int32)[None, :] == doc_index[:, None]
    adapter = jnp.sum(jnp.where(picked, doc_adapter[None, :], 0), axis=1)
    return (doc_index, positions - own_start, adapter)


def block_scores(query_rows, key_rows):
    kv_count = key_rows.shape[1] // HEAD_WIDTH
    query_group_width = query_rows.shape[1] // key_rows.shape[1]
    query_four = query_rows.reshape(query_rows.shape[0], kv_count, query_group_width, HEAD_WIDTH)
    key_three = key_rows.reshape(key_rows.shape[0], kv_count, HEAD_WIDTH)
    return (
        jnp.einsum("qkgd,nkd->kgqn", query_four, key_three, preferred_element_type=jnp.float32)
        * score_scale
    )


def visible_mask(query_pos, query_doc, key_pos, key_doc):
    return (key_pos[None, :] <= query_pos[:, None]) & (key_doc[None, :] == query_doc[:, None])


def forward_step(carried, key_rows, value_rows, key_pos, key_doc, query_rows, query_pos, query_doc):
    running_max, total_mass, accum = carried
    visible = visible_mask(query_pos, query_doc, key_pos, key_doc)
    scores = jnp.where(visible, block_scores(query_rows, key_rows), masked_score)
    new_max = jnp.maximum(running_max, jnp.max(scores, axis=-1))
    weights = jnp.where(visible, jnp.exp(scores - new_max[..., None]), 0.0)
    decay_factor = jnp.exp(running_max - new_max)
    kv_count = key_rows.shape[1] // HEAD_WIDTH
    value_three = value_rows.reshape(value_rows.shape[0], kv_count, HEAD_WIDTH)
    added = jnp.einsum(
        "kgqn,nkd->kgqd",
        weights.astype(jnp.bfloat16),
        value_three,
        preferred_element_type=jnp.float32,
    )
    return (
        new_max,
        total_mass * decay_factor + jnp.sum(weights, axis=-1),
        accum * decay_factor[..., None] + added,
    )


def grad_step(
    query_rows,
    query_grad,
    log_mass,
    delta_sum,
    query_pos,
    query_doc,
    key_rows,
    value_rows,
    key_pos,
    key_doc,
):
    visible = visible_mask(query_pos, query_doc, key_pos, key_doc)
    scores = block_scores(query_rows, key_rows)
    weights = jnp.where(visible, jnp.exp(scores - log_mass[..., None]), 0.0)
    count_query = query_rows.shape[0]
    count_key = key_rows.shape[0]
    kv_count = key_rows.shape[1] // HEAD_WIDTH
    query_group_width = query_rows.shape[1] // key_rows.shape[1]
    grad_four = query_grad.reshape(count_query, kv_count, query_group_width, HEAD_WIDTH)
    query_four = query_rows.reshape(count_query, kv_count, query_group_width, HEAD_WIDTH)
    key_three = key_rows.reshape(count_key, kv_count, HEAD_WIDTH)
    value_three = value_rows.reshape(count_key, kv_count, HEAD_WIDTH)
    weight_grad = jnp.einsum(
        "qkgd,nkd->kgqn", grad_four, value_three, preferred_element_type=jnp.float32
    )
    score_grad = (weights * (weight_grad - delta_sum[..., None])).astype(jnp.bfloat16)
    query_add = (
        jnp.einsum(
            "kgqn,nkd->qkgd", score_grad, key_three, preferred_element_type=jnp.float32
        ).reshape(count_query, -1)
        * score_scale
    )
    key_add = (
        jnp.einsum(
            "kgqn,qkgd->nkd", score_grad, query_four, preferred_element_type=jnp.float32
        ).reshape(count_key, -1)
        * score_scale
    )
    value_add = jnp.einsum(
        "kgqn,qkgd->nkd",
        weights.astype(jnp.bfloat16),
        grad_four,
        preferred_element_type=jnp.float32,
    ).reshape(count_key, -1)
    return (query_add, key_add, value_add)


def dispatch_plan(expert_ids, expert_count, capacity):
    row_count, top_count = expert_ids.shape
    flat_ids = expert_ids.reshape(row_count * top_count)
    expert_hot = (flat_ids[:, None] == jnp.arange(expert_count, dtype=jnp.int32)[None, :]).astype(
        jnp.int32
    )
    earlier = jnp.cumsum(expert_hot, axis=0) - expert_hot
    place_index = jnp.sum(earlier * expert_hot, axis=1)
    slot_index = flat_ids * capacity + place_index
    owner_flat = (
        jnp.zeros((expert_count * capacity,), jnp.int32)
        .at[slot_index]
        .set(jnp.arange(row_count * top_count, dtype=jnp.int32))
    )
    filled = jnp.zeros((expert_count * capacity,), jnp.float32).at[slot_index].set(1.0)
    return (slot_index, owner_flat // top_count, owner_flat, filled)


def expert_forward(
    got_rows,
    got_pick,
    expert_in,
    expert_in_down,
    expert_in_up,
    expert_out,
    expert_out_down,
    expert_out_up,
):
    adapter_rank_span = ADAPTER_CHOICES * ADAPTER_RANK
    got_mask = jnp.repeat(got_pick, ADAPTER_RANK, axis=2)
    double_mask = jnp.concatenate([got_mask, got_mask], axis=2)
    mid_in = (
        jnp.einsum("end,edr->enr", got_rows, expert_in_down, preferred_element_type=jnp.float32)
        * double_mask
    ).astype(jnp.bfloat16)
    lifted = jnp.concatenate(
        [
            jnp.einsum(
                "enr,erf->enf",
                mid_in[:, :, :adapter_rank_span],
                expert_in_up[:, 0],
                preferred_element_type=jnp.float32,
            ),
            jnp.einsum(
                "enr,erf->enf",
                mid_in[:, :, adapter_rank_span:],
                expert_in_up[:, 1],
                preferred_element_type=jnp.float32,
            ),
        ],
        axis=2,
    )
    joint = (
        jnp.einsum("end,edf->enf", got_rows, expert_in, preferred_element_type=jnp.float32) + lifted
    )
    gate_part = joint[:, :, :FF]
    up_part = joint[:, :, FF:]
    hidden = (jax.nn.silu(gate_part) * up_part).astype(jnp.bfloat16)
    mid_out = (
        jnp.einsum("enf,efr->enr", hidden, expert_out_down, preferred_element_type=jnp.float32)
        * got_mask
    ).astype(jnp.bfloat16)
    result = (
        jnp.einsum("enf,efd->end", hidden, expert_out, preferred_element_type=jnp.float32)
        + jnp.einsum("enr,erd->end", mid_out, expert_out_up, preferred_element_type=jnp.float32)
    ).astype(jnp.bfloat16)
    return ((got_mask, double_mask, mid_in, gate_part, up_part, hidden, mid_out), result)


def expert_backward(
    got_rows,
    saved,
    result_grad,
    expert_in,
    expert_in_down,
    expert_in_up,
    expert_out,
    expert_out_down,
    expert_out_up,
):
    adapter_rank_span = ADAPTER_CHOICES * ADAPTER_RANK
    got_mask, double_mask, mid_in, gate_part, up_part, hidden, mid_out = saved
    grad_eout_up = jnp.einsum(
        "enr,end->erd", mid_out, result_grad, preferred_element_type=jnp.float32
    )
    mid_out_grad = (
        jnp.einsum(
            "end,erd->enr", result_grad, expert_out_up, preferred_element_type=jnp.float32
        ).astype(jnp.bfloat16)
        * got_mask
    )
    hidden_grad = jnp.einsum(
        "end,efd->enf", result_grad, expert_out, preferred_element_type=jnp.float32
    ) + jnp.einsum(
        "enr,efr->enf", mid_out_grad, expert_out_down, preferred_element_type=jnp.float32
    )
    grad_eout_down = jnp.einsum(
        "enf,enr->efr", hidden, mid_out_grad, preferred_element_type=jnp.float32
    )
    gate_sigmoid = jax.nn.sigmoid(gate_part)
    joint_grad = jnp.concatenate(
        [
            hidden_grad * up_part * gate_sigmoid * (1.0 + gate_part * (1.0 - gate_sigmoid)),
            hidden_grad * gate_part * gate_sigmoid,
        ],
        axis=2,
    ).astype(jnp.bfloat16)
    mid_in_grad = (
        jnp.concatenate(
            [
                jnp.einsum(
                    "enf,erf->enr",
                    joint_grad[:, :, :FF],
                    expert_in_up[:, 0],
                    preferred_element_type=jnp.float32,
                ),
                jnp.einsum(
                    "enf,erf->enr",
                    joint_grad[:, :, FF:],
                    expert_in_up[:, 1],
                    preferred_element_type=jnp.float32,
                ),
            ],
            axis=2,
        ).astype(jnp.bfloat16)
        * double_mask
    )
    grad_ein_up = jnp.stack(
        [
            jnp.einsum(
                "enr,enf->erf",
                mid_in[:, :, :adapter_rank_span],
                joint_grad[:, :, :FF],
                preferred_element_type=jnp.float32,
            ),
            jnp.einsum(
                "enr,enf->erf",
                mid_in[:, :, adapter_rank_span:],
                joint_grad[:, :, FF:],
                preferred_element_type=jnp.float32,
            ),
        ],
        axis=1,
    )
    grad_ein_down = jnp.einsum(
        "end,enr->edr", got_rows, mid_in_grad, preferred_element_type=jnp.float32
    )
    rows_grad = (
        jnp.einsum("enf,edf->end", joint_grad, expert_in, preferred_element_type=jnp.float32)
        + jnp.einsum(
            "enr,edr->end", mid_in_grad, expert_in_down, preferred_element_type=jnp.float32
        )
    ).astype(jnp.bfloat16)
    return (rows_grad, (grad_ein_down, grad_ein_up, grad_eout_down, grad_eout_up))


def per_device(
    resid_in,
    out_grad,
    attn_gain,
    q_weight,
    key_value_weight,
    o_weight,
    moe_gain,
    router,
    expert_in,
    expert_out,
    qkv_down,
    q_up,
    key_value_up_factor,
    o_down,
    o_up,
    expert_in_down,
    expert_in_up,
    expert_out_down,
    expert_out_up,
    expert_ids,
    doc_starts,
    doc_adapter,
):
    cycle_size = lax.axis_size("ctx")
    pair_size = lax.axis_size("ep")
    cycle_index = lax.axis_index("ctx")
    pair_index = lax.axis_index("ep")
    row_count = resid_in.shape[0]
    block_size = row_count * pair_size
    adapter_rank_span = ADAPTER_CHOICES * ADAPTER_RANK
    adapter_range = jnp.arange(ADAPTER_CHOICES, dtype=jnp.int32)
    block_pos = cycle_index * block_size + jnp.arange(block_size, dtype=jnp.int32)
    block_doc, block_in_doc, block_adapter = doc_layout(block_pos, doc_starts, doc_adapter)
    row_adapter = lax.dynamic_slice_in_dim(block_adapter, pair_index * row_count, row_count, 0)
    block_pick = (block_adapter[:, None] == adapter_range[None, :]).astype(jnp.bfloat16)
    block_mask = jnp.repeat(block_pick, ADAPTER_RANK, axis=1)
    row_pick = (row_adapter[:, None] == adapter_range[None, :]).astype(jnp.bfloat16)
    row_mask = jnp.repeat(row_pick, ADAPTER_RANK, axis=1)
    expert_weights = (
        expert_in,
        expert_in_down,
        expert_in_up,
        expert_out,
        expert_out_down,
        expert_out_up,
    )
    resid_rows = resid_in.astype(jnp.float32)
    normed_rows = rms_scale(resid_rows, attn_gain).astype(jnp.bfloat16)
    normed_input = lax.all_gather(normed_rows, "ep", axis=0, tiled=True)
    adapter_middles = (
        matrix_product(normed_input, qkv_down) * jnp.tile(block_mask, (1, 3))
    ).astype(jnp.bfloat16)
    q_linear = matrix_product(normed_input, q_weight) + matrix_product(
        adapter_middles[:, :adapter_rank_span], q_up
    )
    key_projected = matrix_product(normed_input, key_value_weight[0]) + matrix_product(
        adapter_middles[:, adapter_rank_span : 2 * adapter_rank_span], key_value_up_factor[0]
    )
    value_head_rows = (
        matrix_product(normed_input, key_value_weight[1])
        + matrix_product(adapter_middles[:, 2 * adapter_rank_span :], key_value_up_factor[1])
    ).astype(jnp.bfloat16)
    cosine_table, sine_table = rope_tables(block_in_doc, HEAD_WIDTH)
    query_heads_rows = (
        rotary_apply(q_linear.reshape(block_size, -1, HEAD_WIDTH), cosine_table, sine_table)
        .reshape(block_size, -1)
        .astype(jnp.bfloat16)
    )
    key_head_rows = (
        rotary_apply(key_projected.reshape(block_size, -1, HEAD_WIDTH), cosine_table, sine_table)
        .reshape(block_size, -1)
        .astype(jnp.bfloat16)
    )
    kv_count = key_head_rows.shape[1] // HEAD_WIDTH
    query_group_width = query_heads_rows.shape[1] // key_head_rows.shape[1]
    start_state = (
        jnp.full((kv_count, query_group_width, block_size), masked_score, jnp.float32),
        jnp.zeros((kv_count, query_group_width, block_size), jnp.float32),
        jnp.zeros((kv_count, query_group_width, block_size, HEAD_WIDTH), jnp.float32),
    )
    key_piece = lax.all_gather(key_head_rows, "ctx", axis=0, tiled=True)
    value_piece = lax.all_gather(value_head_rows, "ctx", axis=0, tiled=True)
    piece_rows = key_piece.shape[0]
    step_rows = 512

    def sub_block(turn_index, inner_state):
        offset = turn_index * step_rows
        key_rows = lax.dynamic_slice_in_dim(key_piece, offset, step_rows, 0)
        value_rows = lax.dynamic_slice_in_dim(value_piece, offset, step_rows, 0)
        key_pos = offset + jnp.arange(step_rows, dtype=jnp.int32)

        def attend_block(current):
            return forward_step(
                current,
                key_rows,
                value_rows,
                key_pos,
                doc_number(key_pos, doc_starts),
                query_heads_rows,
                block_pos,
                block_doc,
            )

        return lax.cond(
            key_pos[0] <= block_pos[block_size - 1],
            attend_block,
            lambda current: current,
            inner_state,
        )

    running_max, total_mass, accum = lax.fori_loop(
        0, piece_rows // step_rows, sub_block, start_state
    )
    log_mass = running_max + jnp.log(total_mass)
    attended = jnp.transpose(accum / total_mass[..., None], (2, 0, 1, 3)).reshape(block_size, -1)
    attended_low = attended.astype(jnp.bfloat16)
    attn_sum, mid_sum = (
        lax.psum_scatter(
            matrix_product(attended_low, o_weight).astype(jnp.bfloat16),
            "ep",
            scatter_dimension=0,
            tiled=True,
        ).astype(jnp.float32),
        lax.psum_scatter(
            matrix_product(attended_low, o_down).astype(jnp.bfloat16),
            "ep",
            scatter_dimension=0,
            tiled=True,
        ).astype(jnp.float32),
    )
    mid_attn = (mid_sum * row_mask).astype(jnp.bfloat16)
    resid_mid = resid_rows + attn_sum + matrix_product(mid_attn, o_up)
    normed_moe = rms_scale(resid_mid, moe_gain).astype(jnp.bfloat16)
    logits = matrix_product(normed_moe, router)
    gate_probs = jax.nn.softmax(jnp.take_along_axis(logits, expert_ids, axis=1), axis=-1)
    expert_count = router.shape[1]
    local_experts = expert_in.shape[0]
    top_count = expert_ids.shape[1]
    capacity = 3 * row_count * top_count // (2 * expert_count)
    upstream = out_grad.astype(jnp.float32)
    slot_index, owner_row, owner_flat, filled = dispatch_plan(expert_ids, expert_count, capacity)
    live_slot = filled[:, None] > 0.0
    send_rows = jnp.where(
        live_slot, jnp.take(normed_moe, owner_row, axis=0), jnp.zeros((), jnp.bfloat16)
    ).reshape(pair_size, local_experts, capacity, -1)
    send_pick = jnp.where(
        live_slot, jnp.take(row_pick, owner_row, axis=0), jnp.zeros((), jnp.bfloat16)
    ).reshape(pair_size, local_experts, capacity, -1)
    got_rows, got_pick = (
        lax.all_to_all(send_rows, "ep", split_axis=0, concat_axis=2, tiled=True),
        lax.all_to_all(send_pick, "ep", split_axis=0, concat_axis=2, tiled=True),
    )
    got_rows = got_rows[0]
    saved, result = expert_forward(got_rows, got_pick[0], *expert_weights)
    returned = lax.all_to_all(result[None], "ep", split_axis=2, concat_axis=0, tiled=True).reshape(
        expert_count * capacity, -1
    )
    picked = (
        jnp.take(returned, slot_index, axis=0).reshape(row_count, top_count, -1).astype(jnp.float32)
    )
    block_out = (resid_mid + jnp.sum(gate_probs[:, :, None] * picked, axis=1)).astype(jnp.bfloat16)
    row_grads = (gate_probs[:, :, None] * upstream[:, None, :]).astype(jnp.bfloat16)
    gate_grads = jnp.sum(picked * upstream[:, None, :], axis=2)
    slot_grads = (
        jnp.zeros((expert_count * capacity, row_grads.shape[2]), jnp.bfloat16)
        .at[slot_index]
        .set(row_grads.reshape(row_count * top_count, -1))
    )
    result_grad = lax.all_to_all(
        slot_grads.reshape(pair_size, local_experts, capacity, -1),
        "ep",
        split_axis=0,
        concat_axis=2,
        tiled=True,
    )[0]
    rows_grad, expert_grads = expert_backward(got_rows, saved, result_grad, *expert_weights)
    back_grads = lax.all_to_all(
        rows_grad[None], "ep", split_axis=2, concat_axis=0, tiled=True
    ).reshape(expert_count * capacity, -1)
    token_moe_grad = jnp.sum(
        jnp.take(back_grads, slot_index, axis=0)
        .reshape(row_count, top_count, -1)
        .astype(jnp.float32),
        axis=1,
    )
    grad_ein_down, grad_ein_up, grad_eout_down, grad_eout_up = expert_grads
    logit_grads = (
        gate_probs * (gate_grads - jnp.sum(gate_probs * gate_grads, axis=1, keepdims=True))
    ).astype(jnp.bfloat16)
    expert_range = jnp.arange(expert_count, dtype=jnp.int32)
    full_logit_grads = jnp.sum(
        jnp.where(
            expert_ids[:, :, None] == expert_range[None, None, :],
            logit_grads[:, :, None],
            jnp.zeros((), jnp.bfloat16),
        ),
        axis=1,
    )
    moe_norm_grad = token_moe_grad + matmul_nt(full_logit_grads, router)
    mid_grad = upstream + rms_back(resid_mid, moe_gain, moe_norm_grad)
    attn_grad = mid_grad.astype(jnp.bfloat16)
    mid_attn_grad = matmul_nt(attn_grad, o_up).astype(jnp.bfloat16) * row_mask
    grad_o_up = matmul_tn(mid_attn, attn_grad)
    attn_grad_all, mid_grad_all = (
        lax.all_gather(attn_grad, "ep", axis=0, tiled=True),
        lax.all_gather(mid_attn_grad, "ep", axis=0, tiled=True),
    )
    attended_grad = (matmul_nt(attn_grad_all, o_weight) + matmul_nt(mid_grad_all, o_down)).astype(
        jnp.bfloat16
    )
    grad_o_down = matmul_tn(attended_low, mid_grad_all)
    delta_sum = jnp.transpose(
        jnp.sum(
            (attended_grad.astype(jnp.float32) * attended).reshape(
                block_size, kv_count, query_group_width, HEAD_WIDTH
            ),
            axis=3,
        ),
        (1, 2, 0),
    )

    def circle(turn_index, carried):
        key_float, value_float, key_total, value_total, query_total = carried
        anchor = (cycle_index - turn_index) % cycle_size
        key_pos = anchor * block_size + jnp.arange(block_size, dtype=jnp.int32)

        def add_block(current):
            added = grad_step(
                query_heads_rows,
                attended_grad,
                log_mass,
                delta_sum,
                block_pos,
                block_doc,
                key_float.astype(jnp.bfloat16),
                value_float.astype(jnp.bfloat16),
                key_pos,
                doc_number(key_pos, doc_starts),
            )
            return (current[0] + added[1], current[1] + added[2], current[2] + added[0])

        key_total, value_total, query_total = lax.cond(
            anchor <= cycle_index,
            add_block,
            lambda current: current,
            (key_total, value_total, query_total),
        )
        key_float, value_float, key_total, value_total = (
            shifted_2(key_float.astype(jnp.bfloat16), "ctx", 1).astype(key_float.dtype),
            shifted_2(value_float.astype(jnp.bfloat16), "ctx", 1).astype(value_float.dtype),
            shifted_2(key_total.astype(jnp.bfloat16), "ctx", 1).astype(key_total.dtype),
            shifted_2(value_total.astype(jnp.bfloat16), "ctx", 1).astype(value_total.dtype),
        )
        return (key_float, value_float, key_total, value_total, query_total)

    empty_keys = jnp.zeros((block_size, key_head_rows.shape[1]), jnp.float32)
    circle_start = (
        key_head_rows.astype(jnp.float32),
        value_head_rows.astype(jnp.float32),
        empty_keys,
        empty_keys,
        jnp.zeros((block_size, query_heads_rows.shape[1]), jnp.float32),
    )
    unused_keys, unused_values, key_grad, value_grad, query_grad = lax.fori_loop(
        0, cycle_size, circle, circle_start
    )
    query_low = query_grad.astype(jnp.bfloat16).astype(jnp.float32)
    key_low = key_grad.astype(jnp.bfloat16).astype(jnp.float32)
    value_low = value_grad.astype(jnp.bfloat16)
    q_lin_grad = (
        unrotate(query_low.reshape(block_size, -1, HEAD_WIDTH), cosine_table, sine_table)
        .reshape(block_size, -1)
        .astype(jnp.bfloat16)
    )
    k_lin_grad = (
        unrotate(key_low.reshape(block_size, -1, HEAD_WIDTH), cosine_table, sine_table)
        .reshape(block_size, -1)
        .astype(jnp.bfloat16)
    )
    grad_q_up = matmul_tn(adapter_middles[:, :adapter_rank_span], q_lin_grad)
    grad_kv_up = jnp.stack(
        [
            matmul_tn(adapter_middles[:, adapter_rank_span : 2 * adapter_rank_span], k_lin_grad),
            matmul_tn(adapter_middles[:, 2 * adapter_rank_span :], value_low),
        ],
        axis=0,
    )
    norm_part = (
        matmul_nt(q_lin_grad, q_weight)
        + matmul_nt(k_lin_grad, key_value_weight[0])
        + matmul_nt(value_low, key_value_weight[1])
    )
    mids_part = jnp.concatenate(
        [
            matmul_nt(q_lin_grad, q_up),
            matmul_nt(k_lin_grad, key_value_up_factor[0]),
            matmul_nt(value_low, key_value_up_factor[1]),
        ],
        axis=1,
    )
    norm_sum, mids_sum = (
        lax.psum_scatter(
            norm_part.astype(jnp.bfloat16), "ep", scatter_dimension=0, tiled=True
        ).astype(jnp.float32),
        lax.psum_scatter(
            mids_part.astype(jnp.bfloat16), "ep", scatter_dimension=0, tiled=True
        ).astype(jnp.float32),
    )
    mids_grad = mids_sum.astype(jnp.bfloat16) * jnp.tile(row_mask, (1, 3))
    norm_grad = norm_sum + matmul_nt(mids_grad, qkv_down)
    grad_qkv_down = matmul_tn(normed_rows, mids_grad)
    in_grad = (mid_grad + rms_back(resid_rows, attn_gain, norm_grad)).astype(jnp.bfloat16)
    grad_q_up, grad_kv_up, grad_o_down, grad_ein_down, grad_ein_up, grad_eout_down, grad_eout_up = (
        lax.psum(
            (
                grad_q_up,
                grad_kv_up,
                grad_o_down,
                grad_ein_down,
                grad_ein_up,
                grad_eout_down,
                grad_eout_up,
            ),
            "ctx",
        )
    )
    grad_qkv_down, grad_o_up = lax.psum((grad_qkv_down, grad_o_up), ("ctx", "ep"))
    return (
        block_out,
        in_grad,
        grad_qkv_down,
        grad_q_up,
        grad_kv_up,
        grad_o_down,
        grad_o_up,
        grad_ein_down,
        grad_ein_up,
        grad_eout_down,
        grad_eout_up,
    )


def solution(mesh):
    placed = (
        P(("ctx", "ep"), None),
        P(("ctx", "ep"), None),
        P(),
        P(None, "ep"),
        P(None, None, "ep"),
        P("ep", None),
        P(),
        P(),
        P("ep", None, None),
        P("ep", None, None),
        P(),
        P(None, "ep"),
        P(None, None, "ep"),
        P("ep", None),
        P(),
        P("ep", None, None),
        P("ep", None, None, None),
        P("ep", None, None),
        P("ep", None, None),
        P(("ctx", "ep"), None),
        P(),
        P(),
    )
    return jax.shard_map(
        per_device,
        mesh=mesh,
        in_specs=placed,
        out_specs=(
            P(("ctx", "ep"), None),
            P(("ctx", "ep"), None),
            P(),
            P(None, "ep"),
            P(None, None, "ep"),
            P("ep", None),
            P(),
            P("ep", None, None),
            P("ep", None, None, None),
            P("ep", None, None),
            P("ep", None, None),
        ),
        check_vma=False,
    )
```

profile of v0, /device:TPU:0, one launch (start us, length us, event | category | flops | bytes accessed | tf_op | source)
XLA Modules:
  0.0 1048.7 jit_solution(15662904749767576026)
XLA Ops:
  11.1 9.9 all_gather.15
  28.6 4.5 reduce-window.6
  33.8 32.9 %all-gather.5.cloned.1.call-done = bf16[4096,256]{1,0:T(8,128)(2,1)} async-done(((bf16[256,256]{1,0:T(8,128)(2,1)}), bf16[4096,256]{1,0:T(8,128)(2,1)}) %all-gather.5.cloned.1.call-update) | async-done | bytes 2097168 | tf_op jit(solution)/shard_map/all_gather | solution.py:415
  66.7 4.1 copy.183
  70.8 38.1 %all-gather.3.cloned.1.call-done = bf16[4096,256]{0,1:T(8,128)(2,1)} async-done(((bf16[256,256]{0,1:T(8,128)(2,1)}), bf16[4096,256]{0,1:T(8,128)(2,1)}) %all-gather.3.cloned.1.call-update) | async-done | bytes 2097168 | tf_op jit(solution)/shard_map/all_gather | solution.py:414
  109.0 24.0 %while.41 = (s32[]{:T(128)}, f32[4,2,256]{2,1,0:T(2,128)S(1)}, f32[4,2,256]{2,1,0:T(2,128)S(1)}, f32[4,2,256,64]{2,3,1,0:T(8,128)S(1)}, s32[256]{0:T(256)S(1)}, ...) while((s32[]{:T(128)}, f32[4,2,256]{2,1,0:T(2,128)S(1)}, ...), condition=%wide.region_10.11_spmd, body=%wide.region_4.10_spmd.sunk | while | flops 282739200 | bytes 16138617 | solution.py:444
  111.4 4.5 conditional.5
  136.3 4.3 scatter_custom_fusion.1
  140.8 4.3 scatter_custom_fusion
  152.6 22.6 %reduce-scatter.13.cloned.1.call-done = bf16[128,32]{1,0:T(8,128)(2,1)} async-done(((bf16[256,32]{1,0:T(8,128)(2,1)}), bf16[128,32]{1,0:T(8,128)(2,1)}) %reduce-scatter.13.cloned.1.call-update) | async-done | bytes 8208
  176.1 16.4 %reduce-scatter.9.cloned.1.call-done = bf16[128,1024]{1,0:T(8,128)(2,1)} async-done(((bf16[256,1024]{1,0:T(8,128)(2,1)}), bf16[128,1024]{1,0:T(8,128)(2,1)}) %reduce-scatter.9.cloned.1.call-update) | async-done | bytes 262160 | tf_op jit(solution)/shard_map/reduce_scatter | solution.py:451
  193.9 5.8 gather_fusion
  203.0 5.4 all-to-all-start
  208.5 36.3 %all-to-all-done = bf16[2,8,96,1024]{3,2,1,0:T(8,128)(2,1)} async-done(((bf16[2,8,96,1024]{3,2,1,0:T(8,128)(2,1)}), bf16[2,8,96,1024]{3,2,1,0:T(8,128)(2,1)}, u32[]{:S(2)}, u32[]{:S(2)}) %all-to-all-start) | async-done | bytes 3145760 | tf_op jit(solution)/shard_map/all_to_all | solution.py:483
  253.3 14.8 %maximum_add_fusion = f32[8,192,1024]{2,1,0:T(8,128)} fusion(f32[8,192,512]{2,1,0:T(8,128)} %fusion.72, f32[8,192,512]{2,1,0:T(8,128)} %fusion.75, bf16[8,192,1024]{2,1,0:T(8,128)(2,1)} %bitcast.324, bf16[8,1024,1024]{2,1,0:T(8,128)(2,1)} %param.40), kind=kOutput, calls=%fused_computation.49 | convolution fusion | flops 3224371200 | bytes 32505856 | tf_op jit(solution)/shard_map/end,edf->enf/dot_general | solution.py:230
  268.0 3.9 multiply_convert_fusion.2
  278.9 5.5 all-to-all-start.2
  285.0 7.0 gather_fusion.2
  292.2 27.8 %all-to-all-done.2 = bf16[1,8,192,1024]{3,1,0,2:T(8,128)(2,1)} async-done(((bf16[1,8,192,1024]{3,1,0,2:T(8,128)(2,1)}), bf16[1,8,192,1024]{3,1,0,2:T(8,128)(2,1)}, u32[]{:S(2)}, u32[]{:S(2)}) %all-to-all-start.2) | async-done | bytes 3145760 | tf_op jit(solution)/shard_map/all_to_all | solution.py:488
  320.0 5.3 copy.200
  325.3 8.3 gather_fusion.3
  336.9 7.9 scatter_custom_fusion.2
  344.8 5.7 all-to-all-start.3
  350.7 34.5 %all-to-all-done.3 = bf16[2,8,96,1024]{3,2,1,0:T(8,128)(2,1)} async-done(((bf16[2,8,96,1024]{3,2,1,0:T(8,128)(2,1)}), bf16[2,8,96,1024]{3,2,1,0:T(8,128)(2,1)}, u32[]{:S(2)}, u32[]{:S(2)}) %all-to-all-start.3) | async-done | bytes 3145760 | tf_op jit(solution)/shard_map/all_to_all | solution.py:502
  388.6 7.5 fusion.130
  400.3 11.9 %fusion.27 = f32[8,192,1024]{2,1,0:T(8,128)} fusion(bf16[8,1024,1024]{2,1,0:T(8,128)(2,1)} %param.40, bf16[8,192,512]{2,1,0:T(8,128)(2,1)} %copy-done.8, bf16[8,192,512]{2,1,0:T(8,128)(2,1)} %copy-done.7), kind=kOutput, calls=%fused_computation.62 | convolution fusion | flops 3227516928 | bytes 26214400 | tf_op jit(solution)/shard_map/enf,edf->end/dot_general | solution.py:325
  412.3 3.8 fusion.26
  416.1 3.4 copy.203
  419.5 5.3 all-to-all-start.4
  436.8 21.7 %all-to-all-done.4 = bf16[1,8,192,1024]{3,1,0,2:T(8,128)(2,1)} async-done(((bf16[1,8,192,1024]{3,1,0,2:T(8,128)(2,1)}), bf16[1,8,192,1024]{3,1,0,2:T(8,128)(2,1)}, u32[]{:S(2)}, u32[]{:S(2)}) %all-to-all-start.4) | async-done | bytes 3145760 | tf_op jit(solution)/shard_map/all_to_all | solution.py:510
  458.5 5.3 copy.204
  463.8 8.3 gather_fusion.4
  472.2 5.3 convert_reduce_fusion.2
  478.1 7.3 all_gather.18
  485.6 4.4 all_gather.19
  494.1 238.0 %while.42 = (s32[]{:T(128)}, bf16[256,256]{0,1:T(8,128)(2,1)}, bf16[256,256]{0,1:T(8,128)(2,1)S(1)}, f32[256,256]{0,1:T(8,128)}, f32[256,256]{0,1:T(8,128)S(1)},...) while((s32[]{:T(128)}, bf16[256,256]{0,1:T(8,128)(2,1)}, ...), condition=%wide.region_33.35_spmd.clone, body=%wide.region_29.34_spmd.clone.sunk | while | flops 340269568 | bytes 21001940 | solution.py:597
  495.8 3.7 conditional.6
  502.8 3.9 collective-permute-done.2
  527.7 3.6 collective-permute-start.3
  543.5 3.8 collective-permute-start
  559.5 7.1 collective-permute-start.1
  632.6 4.6 collective-permute-start.1
  704.3 3.6 collective-permute-start.1
  707.9 4.1 collective-permute-done.2
  723.6 4.4 collective-permute-done.2
  753.5 15.6 %reduce-scatter.11.cloned.1.call-done = bf16[128,1024]{1,0:T(8,128)(2,1)} async-done(((bf16[256,1024]{1,0:T(8,128)(2,1)}), bf16[128,1024]{1,0:T(8,128)(2,1)}) %reduce-scatter.11.cloned.1.call-update) | async-done | bytes 262160 | tf_op jit(solution)/shard_map/reduce_scatter | solution.py:635
  772.6 124.5 %all-reduce.7.cloned.1.call-done = (f32[32,512]{1,0:T(8,128)}, f32[2,32,256]{2,1,0:T(8,128)}, f32[512,32]{0,1:T(8,128)}, f32[8,1024,64]{1,2,0:T(8,128)}, f32[8,2...) async-done(((f32[32,512]{1,0:T(8,128)}, f32[2,32,256]{2,1,0:T(8,128)}, f32[512,32]{0,1:T(8,128)}, f32[8,1024,64]{1,2,0:T(8,128)}, ...) | async-done | bytes 4915216 | tf_op jit(solution)/shard_map/psum | solution.py:647
  899.5 131.9 %all-reduce.5.cloned.1.call-done = (f32[1024,96]{0,1:T(8,128)}, f32[32,1024]{1,0:T(8,128)}) async-done(((f32[1024,96]{0,1:T(8,128)}, f32[32,1024]{1,0:T(8,128)}), (f32[1024,96]{0,1:T(8,128)}, f32[32,1024]{1,0:T(8,128)})) %all-reduce.5.cloned.1.call-update) | async-done | bytes 524304 | tf_op jit(solution)/shard_map/psum | solution.py:660
  (711 shorter events, 324.2 us)
Async XLA Ops:
  7.2 59.5 %all-gather.5.cloned.1.call-start = ((), (), s32[]{:S(2)}) async-start(), calls=%async_computation.10 | async-start | bytes 2228224 | tf_op jit(solution)/shard_map/all_gather | solution.py:415
  23.7 85.2 %all-gather.3.cloned.1.call-start = ((), (), s32[]{:S(2)}) async-start(), calls=%async_computation.9 | async-start | bytes 2228224 | tf_op jit(solution)/shard_map/all_gather | solution.py:414
  26.4 148.8 %reduce-scatter.13.cloned.1.call-start = ((), (), s32[]{:S(2)}) async-start(), calls=%async_computation.13 | async-start | bytes 98304
  134.9 57.6 %reduce-scatter.9.cloned.1.call-start = ((), (), s32[]{:S(2)}) async-start(), calls=%async_computation.11 | async-start | bytes 786432 | tf_op jit(solution)/shard_map/reduce_scatter | solution.py:451
  149.4 53.6 %all-to-all-start.1 = ((bf16[2,8,96,2]{2,1,3,0:T(8,128)(2,1)}), bf16[2,8,96,2]{2,1,3,0:T(8,128)(2,1)S(1)}, u32[]{:S(2)}, u32[]{:S(2)}) async-start(bf16[2,8,96,2]{2,1,3,0:T(8,128)(2,1)} %select_select_fusion.1), calls=%async_computation.2 | async-start | bytes 16384 | tf_op jit(solution)/shard_map/all_to_all | solution.py:484
  203.0 41.8 %all-to-all-start = ((bf16[2,8,96,1024]{3,2,1,0:T(8,128)(2,1)}), bf16[2,8,96,1024]{3,2,1,0:T(8,128)(2,1)}, u32[]{:S(2)}, u32[]{:S(2)}) async-start(bf16[2,8,96,1024]{3,2,1,0:T(8,128)(2,1)} %select_select_fusion), calls=%async_computation.1 | async-start | bytes 6291456 | tf_op jit(solution)/shard_map/all_to_all | solution.py:483
  278.9 41.1 %all-to-all-start.2 = ((bf16[1,8,192,1024]{3,1,0,2:T(8,128)(2,1)}), bf16[1,8,192,1024]{3,1,0,2:T(8,128)(2,1)}, u32[]{:S(2)}, u32[]{:S(2)}) async-start(bf16[1,8,192,1024]{3,1,0,2:T(8,128)(2,1)} %copy.199), calls=%async_computation.3 | async-start | bytes 6291456 | tf_op jit(solution)/shard_map/all_to_all | solution.py:488
  344.8 40.4 %all-to-all-start.3 = ((bf16[2,8,96,1024]{3,2,1,0:T(8,128)(2,1)}), bf16[2,8,96,1024]{3,2,1,0:T(8,128)(2,1)}, u32[]{:S(2)}, u32[]{:S(2)}) async-start(bf16[2,8,96,1024]{3,2,1,0:T(8,128)(2,1)} %bitcast.332), calls=%async_computation.4 | async-start | bytes 6291456 | tf_op jit(solution)/shard_map/all_to_all | solution.py:502
  419.5 39.0 %all-to-all-start.4 = ((bf16[1,8,192,1024]{3,1,0,2:T(8,128)(2,1)}), bf16[1,8,192,1024]{3,1,0,2:T(8,128)(2,1)}, u32[]{:S(2)}, u32[]{:S(2)}) async-start(bf16[1,8,192,1024]{3,1,0,2:T(8,128)(2,1)} %copy.203), calls=%async_computation.5 | async-start | bytes 6291456 | tf_op jit(solution)/shard_map/all_to_all | solution.py:510
  424.8 326.8 %reduce-scatter.15.cloned.1.call-start = ((), (), s32[]{:S(2)}) async-start(), calls=%async_computation.14 | async-start | bytes 98304
  499.7 8.5 collective-permute-start.3
  501.3 9.6 collective-permute-start.1
  516.3 8.6 collective-permute-start.1
  527.7 8.5 collective-permute-start.3
  531.3 8.6 collective-permute-start.1
  542.7 8.6 collective-permute-start.3
  543.5 9.2 collective-permute-start
  557.0 9.6 collective-permute-start.2
  557.1 10.2 collective-permute-start.3
  559.5 8.9 collective-permute-start.1
  575.4 8.6 collective-permute-start.1
  586.8 8.5 collective-permute-start.3
  587.5 9.2 collective-permute-start
  588.5 9.5 collective-permute-start.1
  600.8 8.5 collective-permute-start.3
  601.9 8.8 collective-permute-start
  614.8 8.5 collective-permute-start.3
  628.7 8.5 collective-permute-start.2
  628.8 9.1 collective-permute-start.3
  642.7 9.2 collective-permute-start.2
  660.8 8.9 collective-permute-start.1
  672.4 9.1 collective-permute-start.3
  672.9 10.1 collective-permute-start
  687.0 9.1 collective-permute-start.2
  687.1 10.4 collective-permute-start.3
  688.3 10.7 %collective-permute-start = (bf16[256,256]{0,1:T(8,128)(2,1)}, bf16[256,256]{0,1:T(8,128)(2,1)}, u32[]{:S(2)}, u32[]{:S(2)}) collective-permute-start(bf16[256,256]{0,1:T(8,128)(2,1)} %copy.264), channel_id=1, source_target_pairs={{0,2},{2,4},{4,6},{6,8},{8,10},{10,12},{12,14},{14,16},{16,18},{18... | collective-permute-start | bytes 393224 | tf_op jit(solution)/shard_map/while/body/eval_jaxpr/ppermute | solution.py:20
  690.5 9.7 collective-permute-start.1
  702.9 9.1 collective-permute-start.2
  703.0 10.4 collective-permute-start.3
  703.1 11.8 %collective-permute-start = (bf16[256,256]{0,1:T(8,128)(2,1)}, bf16[256,256]{0,1:T(8,128)(2,1)}, u32[]{:S(2)}, u32[]{:S(2)}) collective-permute-start(bf16[256,256]{0,1:T(8,128)(2,1)} %copy.264), channel_id=1, source_target_pairs={{0,2},{2,4},{4,6},{6,8},{8,10},{10,12},{12,14},{14,16},{16,18},{18... | collective-permute-start | bytes 393224 | tf_op jit(solution)/shard_map/while/body/eval_jaxpr/ppermute | solution.py:20
  704.3 11.9 %collective-permute-start.1 = (bf16[256,256]{0,1:T(8,128)(2,1)S(1)}, bf16[256,256]{0,1:T(8,128)(2,1)S(1)}, u32[]{:S(2)}, u32[]{:S(2)}) collective-permute-start(bf16[256,256]{0,1:T(8,128)(2,1)S(1)} %copy.265), channel_id=1, source_target_pairs={{0,2},{2,4},{4,6},{6,8},{8,10},{10,12},{12,14},{14,16},{16,18},{18... | collective-permute-start | bytes 393224 | tf_op jit(solution)/shard_map/while/body/eval_jaxpr/ppermute | solution.py:20
  718.8 9.1 collective-permute-start.2
  718.9 10.4 collective-permute-start.3
  719.0 11.8 %collective-permute-start = (bf16[256,256]{0,1:T(8,128)(2,1)}, bf16[256,256]{0,1:T(8,128)(2,1)}, u32[]{:S(2)}, u32[]{:S(2)}) collective-permute-start(bf16[256,256]{0,1:T(8,128)(2,1)} %copy.264), channel_id=1, source_target_pairs={{0,2},{2,4},{4,6},{6,8},{8,10},{10,12},{12,14},{14,16},{16,18},{18... | collective-permute-start | bytes 393224 | tf_op jit(solution)/shard_map/while/body/eval_jaxpr/ppermute | solution.py:20
  720.2 11.9 %collective-permute-start.1 = (bf16[256,256]{0,1:T(8,128)(2,1)S(1)}, bf16[256,256]{0,1:T(8,128)(2,1)S(1)}, u32[]{:S(2)}, u32[]{:S(2)}) collective-permute-start(bf16[256,256]{0,1:T(8,128)(2,1)S(1)} %copy.265), channel_id=1, source_target_pairs={{0,2},{2,4},{4,6},{6,8},{8,10},{10,12},{12,14},{14,16},{16,18},{18... | collective-permute-start | bytes 393224 | tf_op jit(solution)/shard_map/while/body/eval_jaxpr/ppermute | solution.py:20
  737.7 31.4 %reduce-scatter.11.cloned.1.call-start = ((), (), s32[]{:S(2)}) async-start(), calls=%async_computation.12 | async-start | bytes 786432 | tf_op jit(solution)/shard_map/reduce_scatter | solution.py:635
  741.7 155.4 %all-reduce.7.cloned.1.call-start = ((), (), s32[]{:S(2)}) async-start(), calls=%async_computation.16 | async-start | bytes 9830400 | tf_op jit(solution)/shard_map/psum | solution.py:647
  749.8 281.7 %all-reduce.5.cloned.1.call-start = ((), (), s32[]{:S(2)}) async-start(), calls=%async_computation.15 | async-start | bytes 1048576 | tf_op jit(solution)/shard_map/psum | solution.py:660
  (131 other events, 2008.9 us)
Sparse Core Ops, SparseCore 0:
  23.8 42.8 all-gather.4
  68.8 39.9 all-gather.2
  135.0 40.1 reduce-scatter.12
  177.9 14.5 reduce-scatter.8
  737.8 13.7 reduce-scatter.14
  754.4 14.6 reduce-scatter.10
  774.8 122.2 all-reduce.6
  903.1 128.3 all-reduce.4
where the time goes:
time: 1060 us; the launch traced here: 1050 us
  waiting for transfers between devices  576 us (54%)
  starting transfers between devices  133 us (13%)
  local copies, waits for them, and re-layouts  128 us (12%)
  matrix products  90.2 us (9%)
  other arithmetic  71.2 us (7%)
  blocking collectives  21.6 us (2%)
  between operations  16.1 us (2%)
  loops' own time  12.3 us (1%)
    psum x1, waiting for transfers between devices, per_device(): lax.psum((grad_qkv_down, grad_o_up), ('ctx', 'ep'))  132 us
    psum x1, waiting for transfers between devices, per_device(): lax.psum((grad_q_up, grad_kv_up, grad_o_down, grad_ein_down, grad_ein_up,...  125 us
    ppermute x64, starting transfers between devices, shifted_2(): return lax.ppermute(value, axis, pairs)  108 us
    ppermute x64, waiting for transfers between devices, shifted_2(): return lax.ppermute(value, axis, pairs)  72.7 us
    all_gather x1, waiting for transfers between devices, per_device(): key_piece = lax.all_gather(key_head_rows, 'ctx', axis=0, tiled=True)  38.1 us
    all_to_all x1, waiting for transfers between devices, per_device(): lax.all_to_all(send_rows, 'ep', split_axis=0, concat_axis=2, tiled=True)  36.3 us
    all_to_all x1, waiting for transfers between devices, per_device(): lax.all_to_all(slot_grads.reshape(pair_size, local_experts, capacity, -1)...  34.5 us
    all_gather x1, waiting for transfers between devices, per_device(): value_piece = lax.all_gather(value_head_rows, 'ctx', axis=0, tiled=True)  32.9 us
  transfers between devices with their start and end apart: 77, of which 64 were waited for; matrix products, arithmetic and copies ran while one was open for 9% of the time, Pallas kernels for 0%

commit v1 on v0

v1 whole, which is shorter than its diff:
```python
import functools

import jax
import jax.numpy as jnp
from jax import lax
from jax.experimental import pallas as pl
from jax.experimental.pallas import tpu as pltpu
from jax.sharding import PartitionSpec as P

MESH = pl.DeviceIdType.MESH
VMEM = pl.BlockSpec(memory_space=pltpu.VMEM)
SMEM = pl.BlockSpec(memory_space=pltpu.SMEM)
HBM = pl.BlockSpec(memory_space=pl.ANY)
F32 = jnp.float32
BF16 = jnp.bfloat16

HEAD = 64
FF = 512
RANK = 16
SPAN = 32
EPS = 1e-06
LOW = -1e30
SCALE = 0.125

NN = (((1,), (0,)), ((), ()))
NT = (((1,), (1,)), ((), ()))
TN = (((0,), (0,)), ((), ()))


def dot(left, right, dims=NN):
    return lax.dot_general(left, right, dims, preferred_element_type=F32)


def iota(shape, dim):
    return lax.broadcasted_iota(jnp.int32, shape, dim)


def rms(values, gain):
    return values * lax.rsqrt(jnp.mean(values * values, axis=-1, keepdims=True) + EPS) * gain


def rms_back(values, gain, upstream):
    factor = lax.rsqrt(jnp.mean(values * values, axis=-1, keepdims=True) + EPS)
    scaled = upstream * gain
    return factor * scaled - values * factor * factor * factor * jnp.mean(
        scaled * values, axis=-1, keepdims=True
    )


def rotate(values, cosine, sine, sign):
    width = values.shape[1]
    copies = width // 128
    cosine = jnp.concatenate([cosine] * copies, axis=1)
    sine = jnp.concatenate([sine] * copies, axis=1)
    first = iota(values.shape, 1) % HEAD < HEAD // 2
    ahead = pltpu.roll(values, width - HEAD // 2, 1)
    behind = pltpu.roll(values, HEAD // 2, 1)
    return values * cosine + sign * jnp.where(first, -ahead, behind) * sine


def doc_scan(positions, starts_ref, adapters_ref):
    own_start = jnp.zeros(positions.shape, jnp.int32)
    adapter = jnp.zeros(positions.shape, jnp.int32)
    for number in range(starts_ref.shape[0]):
        opened = starts_ref[number] <= positions
        own_start = jnp.where(opened, starts_ref[number], own_start)
        adapter = jnp.where(opened, adapters_ref[number], adapter)
    return own_start, adapter


def place():
    me = lax.axis_index("ctx")
    ep = lax.axis_index("ep")
    return me, ep, me // 4, (me // 2) % 2, me % 2


def block_of(z, x, c):
    return (z * 2 + x) * 2 + c


def signal(device):
    pl.semaphore_signal(
        pltpu.get_barrier_semaphore(), inc=1, device_id=device, device_id_type=MESH
    )


def greet(planes, me, ep, z, x, c):
    signal({"ctx": me, "ep": 1 - ep})
    signal({"ctx": block_of(z, x, 1 - c), "ep": ep})
    signal({"ctx": block_of(z, 1 - x, c), "ep": ep})

    @pl.when(z > 0)
    def _():
        signal({"ctx": me - 4, "ep": ep})

    @pl.when(z < planes - 1)
    def _():
        signal({"ctx": me + 4, "ep": ep})

    count = 3 + jnp.where(z > 0, 1, 0) + jnp.where(z < planes - 1, 1, 0)
    pl.semaphore_wait(pltpu.get_barrier_semaphore(), count)


def remote(src, dst, send, recv, device):
    return pltpu.make_async_remote_copy(
        src_ref=src,
        dst_ref=dst,
        send_sem=send,
        recv_sem=recv,
        device_id=device,
        device_id_type=MESH,
    )


def rows_at(ref, start, count):
    return ref.at[pl.ds(pl.multiple_of(start, count), count)]


def pad_query(rows, target, lane_scale=None):
    count = rows.shape[0]
    upper = iota((count, 128), 1) >= HEAD
    for group in range(4):
        tile = rows[:, 128 * group : 128 * group + 128]
        turned = pltpu.roll(tile, HEAD, 1)
        keep = upper if group % 2 else jnp.logical_not(upper)
        low, high = (turned, tile) if group % 2 else (tile, turned)
        target[group, :count, :] = jnp.where(keep, low, 0.0).astype(BF16)
        target[group, count:, :] = jnp.where(keep, high, 0.0).astype(BF16)


def pad_query_t(columns, target):
    for group in range(4):
        both = jnp.concatenate(
            [
                columns[128 * group : 128 * group + 64],
                columns[128 * group + 64 : 128 * group + 128],
            ],
            axis=1,
        ).astype(BF16)
        blank = jnp.zeros(both.shape, BF16)
        own = HEAD * (group % 2)
        target[group, own : own + HEAD, :] = both
        target[group, HEAD - own : 2 * HEAD - own, :] = blank


def attend_kernel(
    planes,
    resid_ref, grad_ref, ids_ref, starts_ref, adapters_ref, attn_gain_ref, moe_gain_ref,
    q_w_ref, kv_w_ref, o_w_ref, qkv_down_ref, q_up_ref, kv_up_ref, o_down_ref, o_up_ref, router_ref,
    cos_ref, sin_ref,
    x_all, g_all, gates_ref, x2_ref, h2_ref, query_ref, kvall, mids_ref, lse_ref, att_ref, mid_o_ref, mask_ref,
    hot_all, ow_all, od_all, att_all, qt, m_s, l_s, acc,
    pair_send, pair_recv, ring_send, ring_recv,
):
    me, ep, z, x, c = place()
    pair = {"ctx": me, "ep": 1 - ep}
    up = {"ctx": jnp.minimum(me + 4, 4 * planes - 1), "ep": ep}
    across = {"ctx": block_of(z, 1 - x, c), "ep": ep}
    beside = {"ctx": block_of(z, x, 1 - c), "ep": ep}
    rows = resid_ref.shape[0]
    block = 2 * rows
    mine = ep * rows
    theirs = rows - mine
    greet(planes, me, ep, z, x, c)

    def swap(number, src, dst):
        return remote(src, dst, pair_send.at[number], pair_recv.at[number], pair)

    send_x = swap(0, resid_ref, rows_at(x_all, mine, rows))
    send_x.start()

    hot = jnp.zeros((rows, 128), F32)
    lanes = iota((rows, 128), 1)
    for choice in range(ids_ref.shape[1]):
        hot = hot + jnp.where(ids_ref[:, choice : choice + 1] == lanes, 1.0, 0.0)
    hot_all[pl.ds(pl.multiple_of(mine, rows), rows), :] = hot.astype(BF16)
    x_all[pl.ds(pl.multiple_of(mine, rows), rows), :] = resid_ref[...]
    g_all[pl.ds(pl.multiple_of(mine, rows), rows), :] = grad_ref[...]
    ow_all[ep] = o_w_ref[...]
    od_all[ep] = o_down_ref[...]

    position = me * block + iota((block, 128), 0)
    unused, adapter = doc_scan(position, starts_ref, adapters_ref)
    mask_ref[...] = jnp.where((iota((block, 128), 1) % SPAN) // RANK == adapter, 1.0, 0.0)
    row_pos = me * block + iota((8, 2 * block), 1) % block
    row_start, unused = doc_scan(row_pos, starts_ref, adapters_ref)

    def project(start):
        here = pl.ds(pl.multiple_of(start, rows), rows)
        h1 = rms(x_all[here, :].astype(F32), attn_gain_ref[...]).astype(BF16)
        mids = (dot(h1, qkv_down_ref[...]) * mask_ref[here, :96]).astype(BF16)
        mids_ref[here, :] = mids
        cosine, sine = cos_ref[here, :], sin_ref[here, :]
        q_lin = dot(h1, q_w_ref[...]) + dot(mids[:, :SPAN], q_up_ref[...])
        query_ref[here, :] = rotate(q_lin, cosine, sine, 1.0).astype(BF16)
        k_lin = dot(h1, kv_w_ref[0]) + dot(mids[:, SPAN : 2 * SPAN], kv_up_ref[0])
        kvall[me, 0, here, :] = rotate(k_lin, cosine, sine, 1.0).astype(BF16)
        kvall[me, 1, here, :] = (
            dot(h1, kv_w_ref[1]) + dot(mids[:, 2 * SPAN :], kv_up_ref[1])
        ).astype(BF16)

    project(mine)
    send_x.wait_recv()
    send_hot = swap(1, rows_at(hot_all, mine, rows), rows_at(hot_all, mine, rows))
    send_g = swap(2, grad_ref, rows_at(g_all, mine, rows))
    send_ow = swap(3, o_w_ref, ow_all.at[ep])
    send_od = swap(4, o_down_ref, od_all.at[ep])
    for copy in (send_hot, send_od, send_g, send_ow):
        copy.start()
    project(theirs)

    def ring(number, way, target):
        return remote(
            kvall.at[number], kvall.at[number], ring_send.at[way, number], ring_recv.at[number], target
        )

    def forward_own(p):
        number = block_of(p, x, c)

        @pl.when(z < planes - 1)
        def _():
            ring(number, 0, up).start()

        ring(number, 1, across).start()
        ring(number, 2, beside).start()

    def forward_across(p):
        number = block_of(p, 1 - x, c)
        ring(number, 1, across).wait_recv()
        ring(number, 2, beside).start()

    def arrive_beside(p):
        for column in (0, 1):
            ring(block_of(p, column, 1 - c), 2, beside).wait_recv()

    forward_own(z)
    pad_query_t((query_ref[...].astype(F32) * SCALE).T, qt)
    m_s[...] = jnp.full(m_s.shape, LOW, F32)
    l_s[...] = jnp.zeros(l_s.shape, F32)
    acc[...] = jnp.zeros(acc.shape, F32)
    forward_across(z)
    arrive_beside(z)

    start_row = row_start[:1]
    pos_row = row_pos[:1]

    def head_step(p, group, masked):
        tile = slice(128 * (group // 2), 128 * (group // 2) + 128)
        scores = []
        for b in range(4):
            s = dot(kvall[4 * p + b, 0, :, tile], qt[group])
            if masked:
                key = (4 * p + b) * block + iota(s.shape, 0)
                s = jnp.where((key <= pos_row) & (key >= start_row), s, LOW)
            scores.append(s)
        peak = functools.reduce(
            jnp.maximum, [jnp.max(s, axis=0, keepdims=True) for s in scores]
        )
        if not masked:
            sees = start_row <= 4 * p * block
            peak = jnp.where(sees, peak, LOW)
        old = m_s[group]
        new = jnp.maximum(old, peak)
        m_s[group] = new
        base = new if masked else jnp.where(sees, new, -LOW)
        decay = jnp.exp(old - new)
        total = l_s[group] * decay
        grown = acc[group] * decay
        for b in range(4):
            w = jnp.exp(scores[b] - base)
            total = total + jnp.sum(w, axis=0, keepdims=True)
            added = dot(kvall[4 * p + b, 1, :, tile], w.astype(BF16), TN)
            grown = grown + added[HEAD * (group % 2) : HEAD * (group % 2) + HEAD]
        l_s[group] = total
        acc[group] = grown

    def plane_step(turn, carry):
        p = z - turn
        edge = (turn == 0) | (p == 0)

        def heads(group):
            @pl.when(edge)
            def _():
                head_step(p, group, True)

            @pl.when(jnp.logical_not(edge))
            def _():
                head_step(p, group, False)

        heads(0)

        @pl.when(p > 0)
        def _():
            number = block_of(p - 1, x, c)
            ring(number, 0, up).wait_recv()
            forward_own(p - 1)

        heads(1)
        heads(2)

        @pl.when(p > 0)
        def _():
            forward_across(p - 1)

        heads(3)

        @pl.when(p > 0)
        def _():
            arrive_beside(p - 1)

        return carry

    lax.fori_loop(0, z + 1, plane_step, 0)

    columns = []
    for group in range(4):
        lse_ref[group] = m_s[group] + jnp.log(l_s[group])
        done = acc[group] / l_s[group]
        columns += [done[:, :block], done[:, block:]]
    attended = jnp.concatenate(columns, axis=0).T
    att_ref[...] = attended
    att_all[ep] = attended.astype(BF16)
    send_att = swap(5, att_all.at[ep], att_all.at[ep])
    send_att.start()
    for copy in (send_hot, send_od, send_g, send_ow):
        copy.wait_recv()
    send_att.wait_recv()
    left, right = att_all[0], att_all[1]
    mid_o = ((dot(left, od_all[0]) + dot(right, od_all[1])) * mask_ref[:, :SPAN]).astype(BF16)
    mid_o_ref[...] = mid_o
    x2 = (
        x_all[...].astype(F32)
        + (dot(left, ow_all[0]) + dot(right, ow_all[1]))
        + dot(mid_o, o_up_ref[...])
    )
    x2_ref[...] = x2
    h2 = rms(x2, moe_gain_ref[...]).astype(BF16)
    h2_ref[...] = h2
    logits = dot(h2, router_ref[...])
    chosen = hot_all[:, : logits.shape[1]].astype(F32) > 0.5
    logits = jnp.where(chosen, logits, LOW)
    grown = jnp.where(chosen, jnp.exp(logits - jnp.max(logits, axis=1, keepdims=True)), 0.0)
    gates_ref[...] = grown / jnp.sum(grown, axis=1, keepdims=True)

    for copy in (send_x, send_hot, send_g, send_ow, send_od, send_att):
        copy.wait_send()

    def drain(p, carry):
        @pl.when(z < planes - 1)
        def _():
            ring(block_of(p, x, c), 0, up).wait_send()

        ring(block_of(p, x, c), 1, across).wait_send()
        ring(block_of(p, x, c), 2, beside).wait_send()
        ring(block_of(p, 1 - x, c), 2, beside).wait_send()
        return carry

    lax.fori_loop(0, z + 1, drain, 0)


def expert_kernel(
    h2_ref, g_all, gates_ref, x2_ref, mask_ref, mid_o_ref, moe_gain_ref, router_ref, o_up_ref,
    in_hbm, out_hbm, in_down_hbm, in_up_hbm, out_down_hbm, out_up_hbm,
    block_out_ref, d_x2_ref, d_attn_ref, d_mid_o_ref, grads_ref, grad_o_up_ref,
    w_in, w_out, w_in_down, w_in_up, w_out_down, w_out_up, acc_out, acc_h2, dgates, trade, out_trade, dg_trade,
    load_sem, pair_send, pair_recv,
):
    me, ep, z, x, c = place()
    pair = {"ctx": me, "ep": 1 - ep}
    experts = in_hbm.shape[0]
    block = h2_ref.shape[0]
    rows = block // 2
    mine = ep * rows
    theirs = rows - mine
    halves = (
        (in_hbm, w_in), (out_hbm, w_out), (in_down_hbm, w_in_down),
        (in_up_hbm, w_in_up), (out_down_hbm, w_out_down), (out_up_hbm, w_out_up),
    )

    def loads(e):
        return [
            pltpu.make_async_copy(source.at[e], held.at[e], load_sem.at[e, number])
            for number, (source, held) in enumerate(halves)
        ]

    def begin(e, carry):
        for copy in loads(e):
            copy.start()
        return carry

    lax.fori_loop(0, experts, begin, 0)
    signal(pair)
    acc_out[...] = jnp.zeros(acc_out.shape, F32)
    acc_h2[...] = jnp.zeros(acc_h2.shape, F32)
    dgates[...] = jnp.zeros(dgates.shape, F32)
    pl.semaphore_wait(pltpu.get_barrier_semaphore(), 1)
    gates = gates_ref[...]
    own_gates = jnp.where(ep == 0, gates[:, :experts], gates[:, experts:])
    lanes = iota((block, experts), 1)

    def one(e, carry):
        for copy in loads(e):
            copy.wait()
        h2, g = h2_ref[...], g_all[...]
        mask = mask_ref[...]
        gate = jnp.sum(jnp.where(lanes == e, own_gates, 0.0), axis=1, keepdims=True)
        mid_in = (dot(h2, w_in_down[e]) * mask[:, : 2 * SPAN]).astype(BF16)
        gate_part = dot(h2, w_in[e, :, :FF]) + dot(mid_in[:, :SPAN], w_in_up[e, 0])
        up_part = dot(h2, w_in[e, :, FF:]) + dot(mid_in[:, SPAN:], w_in_up[e, 1])
        squash = 1.0 / (1.0 + jnp.exp(-gate_part))
        silu = gate_part * squash
        act_full = silu * up_part
        act = act_full.astype(BF16)
        mid_out = dot(act, w_out_down[e]) * mask[:, :SPAN]
        lifted = (dot(g, w_out_up[e], NT) * mask[:, :SPAN]).astype(BF16)
        d_act = dot(g, w_out[e], NT) + dot(lifted, w_out_down[e], NT)
        d_gate = jnp.sum(act.astype(F32) * d_act, axis=1, keepdims=True)
        dgates[...] += jnp.where(iota(dgates.shape, 1) == e, d_gate, 0.0)
        d_act = d_act * gate
        d_up = (d_act * silu).astype(BF16)
        d_gp = (d_act * up_part * squash * (1.0 + gate_part * (1.0 - squash))).astype(BF16)
        d_mid_in = (
            jnp.concatenate([dot(d_gp, w_in_up[e, 0], NT), dot(d_up, w_in_up[e, 1], NT)], axis=1)
            * mask[:, : 2 * SPAN]
        ).astype(BF16)
        scaled_mid = (mid_out * gate).astype(BF16)
        acc_out[...] += dot((act.astype(F32) * gate).astype(BF16), w_out[e]) + dot(scaled_mid, w_out_up[e])
        acc_h2[...] += (
            dot(d_gp, w_in[e, :, :FF], NT) + dot(d_up, w_in[e, :, FF:], NT) + dot(d_mid_in, w_in_down[e], NT)
        )
        grads_ref[e, 0:64, :] = dot(d_mid_in, h2, TN).astype(BF16)
        grads_ref[e, 64:96, :FF] = dot(mid_in[:, :SPAN], d_gp, TN).astype(BF16)
        grads_ref[e, 64:96, FF:] = dot(mid_in[:, SPAN:], d_up, TN).astype(BF16)
        down = dot((lifted.astype(F32) * gate).astype(BF16), act, TN).astype(BF16)
        grads_ref[e, 96:112, :FF] = down[:16]
        grads_ref[e, 96:112, FF:] = down[16:]
        grads_ref[e, 112:144, :] = dot(scaled_mid, g, TN).astype(BF16)
        return carry

    lax.fori_loop(0, experts, one, 0)

    def swap(number, src, dst):
        return remote(src, dst, pair_send.at[number], pair_recv.at[number], pair)

    dg_trade[ep] = dgates[...].T[:8]
    send_dg = swap(0, dg_trade.at[ep], dg_trade.at[ep])
    send_dg.start()
    trade[ep] = acc_h2[...].astype(BF16)
    send_h2 = swap(1, trade.at[ep], trade.at[ep])
    send_h2.start()
    out_trade[0] = acc_out[pl.ds(pl.multiple_of(theirs, rows), rows), :].astype(BF16)
    send_out = swap(2, out_trade.at[0], out_trade.at[1])
    send_out.start()
    send_dg.wait_recv()
    table = jnp.concatenate([dg_trade[0], dg_trade[1], jnp.zeros((112, block), F32)], axis=0).T
    d_gates = table[:, : 2 * experts]
    d_logits = (gates * (d_gates - jnp.sum(gates * d_gates, axis=1, keepdims=True))).astype(BF16)
    from_router = dot(d_logits, router_ref[...], NT)
    send_h2.wait_recv()
    d_h2 = trade[0].astype(F32) + trade[1].astype(F32) + from_router
    d_x2 = g_all[...].astype(F32) + rms_back(x2_ref[...], moe_gain_ref[...], d_h2)
    d_attn = d_x2.astype(BF16)
    d_attn_ref[...] = d_attn
    d_x2_ref[...] = d_x2
    d_mid_o = (dot(d_attn, o_up_ref[...], NT) * mask_ref[:, :SPAN]).astype(BF16)
    d_mid_o_ref[...] = d_mid_o
    grad_o_up_ref[...] = dot(mid_o_ref[...], d_attn, TN)
    send_out.wait_recv()
    here = pl.ds(pl.multiple_of(mine, rows), rows)
    block_out_ref[...] = (x2_ref[here, :] + (acc_out[here, :] + out_trade[1].astype(F32))).astype(BF16)
    for copy in (send_dg, send_h2, send_out):
        copy.wait_send()


def back_kernel(
    planes,
    x_all, query_ref, kv_hbm, mids_ref, lse_ref, att_ref, d_attn_ref, d_mid_o_ref, d_x2_ref, mask_ref,
    starts_ref, adapters_ref, attn_gain_ref,
    q_w_ref, kv_w_ref, o_w_ref, qkv_down_ref, q_up_ref, kv_up_ref, o_down_ref, cos_ref, sin_ref,
    in_grad_ref, grad_down_ref, grad_q_up_ref, grad_kv_up_ref, grad_o_down_ref,
    kvall, qt, qn, dt, dn, dqt, delta, from_beside, from_across, from_up, to_across, to_down, trade, mid_trade,
    kv_sem, pair_send, pair_recv, beside_send, beside_recv, across_send, across_recv, down_send, down_recv,
):
    me, ep, z, x, c = place()
    pair = {"ctx": me, "ep": 1 - ep}
    down = {"ctx": jnp.maximum(me - 4, 0), "ep": ep}
    across = {"ctx": block_of(z, 1 - x, c), "ep": ep}
    beside = {"ctx": block_of(z, x, 1 - c), "ep": ep}
    block = x_all.shape[0]
    rows = block // 2
    mine = ep * rows
    theirs = rows - mine
    load = pltpu.make_async_copy(kv_hbm, kvall, kv_sem)
    load.start()
    greet(planes, me, ep, z, x, c)

    pad_query(query_ref[...].astype(F32), qn)
    pad_query_t((query_ref[...].astype(F32) * SCALE).T, qt)
    d_att = (
        dot(d_attn_ref[...], o_w_ref[...], NT) + dot(d_mid_o_ref[...], o_down_ref[...], NT)
    ).astype(BF16)
    d_att_full = d_att.astype(F32)
    pad_query(d_att_full, dn)
    pad_query_t(d_att_full.T, dt)
    product = (d_att_full * att_ref[...]).T
    for group in range(4):
        for half in (0, 1):
            start = 128 * group + 64 * half
            delta[group, :, half * block : half * block + block] = jnp.sum(
                product[start : start + 64], axis=0, keepdims=True
            )
    grad_o_down_ref[...] = dot(d_mid_o_ref[...], att_ref[...].astype(BF16), TN)
    dqt[...] = jnp.zeros(dqt.shape, F32)
    row_pos = me * block + iota((8, 2 * block), 1) % block
    row_start, unused = doc_scan(row_pos, starts_ref, adapters_ref)
    start_row, pos_row = row_start[:1], row_pos[:1]
    load.wait()

    def block_step(number, masked):
        new_k, new_v = [], []
        for group in range(4):
            tile = slice(128 * (group // 2), 128 * (group // 2) + 128)
            keys = kvall[number, 0, :, tile]
            s = dot(keys, qt[group])
            base = lse_ref[group]
            if masked:
                key = number * block + iota(s.shape, 0)
                w = jnp.where((key <= pos_row) & (key >= start_row), jnp.exp(s - base), 0.0)
            else:
                w = jnp.exp(s - jnp.where(start_row <= number * block, base, -LOW))
            d_w = dot(kvall[number, 1, :, tile], dt[group])
            d_s = (w * (d_w - delta[group])).astype(BF16)
            new_k.append(dot(d_s, qn[group]))
            new_v.append(dot(w.astype(BF16), dn[group]))
            dqt[group] += dot(keys, d_s, TN)[HEAD * (group % 2) : HEAD * (group % 2) + HEAD]
        for half in (0, 1):
            tile = slice(128 * half, 128 * half + 128)
            kvall[number, 0, :, tile] = ((new_k[2 * half] + new_k[2 * half + 1]) * SCALE).astype(BF16)
            kvall[number, 1, :, tile] = (new_v[2 * half] + new_v[2 * half + 1]).astype(BF16)

    def compute(number):
        edge = (number == 0) | (number == me)

        @pl.when(edge)
        def _():
            block_step(number, True)

        @pl.when((number < me) & jnp.logical_not(edge))
        def _():
            block_step(number, False)

        @pl.when(number > me)
        def _():
            kvall[number] = jnp.zeros(kvall.shape[1:], BF16)

    def to_beside(p, column):
        return remote(
            kvall.at[block_of(p, column, 1 - c)], from_beside.at[p, column],
            beside_send.at[p, column], beside_recv.at[p, column], beside,
        )

    def over(p):
        return remote(to_across.at[p], from_across.at[p], across_send.at[p], across_recv.at[p], across)

    def lower(p):
        return remote(to_down.at[p], from_up.at[p], down_send.at[p], down_recv.at[p], down)

    def finish(p):
        over(p).wait_recv()
        total = (
            kvall[block_of(p, x, c)].astype(F32)
            + from_beside[p, x].astype(F32)
            + from_across[p].astype(F32)
        )
        to_down[p] = total.astype(BF16)

        @pl.when(z < planes - 1)
        def _():
            lower(p).wait_recv()
            to_down[p] = (total + from_up[p].astype(F32)).astype(BF16)

        @pl.when(p < z)
        def _():
            lower(p).start()

    def plane_step(p, carry):
        compute(block_of(p, 1 - x, 1 - c))
        to_beside(p, 1 - x).start()
        compute(block_of(p, x, 1 - c))
        to_beside(p, x).start()

        @pl.when(p > 0)
        def _():
            finish(p - 1)

        compute(block_of(p, 1 - x, c))
        to_beside(p, 1 - x).wait_recv()
        to_across[p] = (
            kvall[block_of(p, 1 - x, c)].astype(F32) + from_beside[p, 1 - x].astype(F32)
        ).astype(BF16)
        over(p).start()
        compute(block_of(p, x, c))
        to_beside(p, x).wait_recv()
        return carry

    lax.fori_loop(0, z + 1, plane_step, 0)
    finish(z)
    d_key = to_down[z, 0].astype(F32)
    d_value = to_down[z, 1]

    cosine, sine = cos_ref[...], sin_ref[...]
    parts = []
    for group in range(4):
        both = dqt[group]
        parts += [both[:, :block], both[:, block:]]
    d_query = jnp.concatenate(parts, axis=0).T * SCALE
    d_q = rotate(d_query.astype(BF16).astype(F32), cosine, sine, -1.0).astype(BF16)
    d_k = rotate(d_key, cosine, sine, -1.0).astype(BF16)
    mids_part = jnp.concatenate(
        [dot(d_q, q_up_ref[...], NT), dot(d_k, kv_up_ref[0], NT), dot(d_value, kv_up_ref[1], NT)], axis=1
    )

    def swap(number, src, dst):
        return remote(src, dst, pair_send.at[number], pair_recv.at[number], pair)

    mid_trade[ep] = mids_part.astype(BF16)
    send_mid = swap(0, mid_trade.at[ep], mid_trade.at[ep])
    send_mid.start()

    def norm_part(start):
        here = pl.ds(pl.multiple_of(start, rows), rows)
        return here

    here, there = norm_part(mine), norm_part(theirs)
    full = dot(d_q, q_w_ref[...], NT) + dot(d_k, kv_w_ref[0], NT) + dot(d_value, kv_w_ref[1], NT)
    first, second = full[:rows], full[rows:]
    trade[0] = jnp.where(ep == 0, second, first).astype(BF16)
    send_norm = swap(1, trade.at[0], trade.at[1])
    send_norm.start()
    grad_q_up_ref[...] = dot(mids_ref[:, :SPAN], d_q, TN)
    grad_kv_up_ref[0] = dot(mids_ref[:, SPAN : 2 * SPAN], d_k, TN)
    grad_kv_up_ref[1] = dot(mids_ref[:, 2 * SPAN :], d_value, TN)
    h1 = rms(x_all[...].astype(F32), attn_gain_ref[...]).astype(BF16)
    send_mid.wait_recv()
    d_mids = (
        (mid_trade[0].astype(F32) + mid_trade[1].astype(F32)) * mask_ref[:, : 3 * SPAN]
    ).astype(BF16)
    grad_down_ref[...] = dot(d_mids, h1, TN)
    from_mids = dot(d_mids, qkv_down_ref[...], NT)
    own = jnp.where(ep == 0, first + from_mids[:rows], second + from_mids[rows:])
    send_norm.wait_recv()
    own = own + trade[1].astype(F32)
    in_grad_ref[...] = (
        d_x2_ref[here, :] + rms_back(x_all[here, :].astype(F32), attn_gain_ref[...], own)
    ).astype(BF16)
    send_mid.wait_send()
    send_norm.wait_send()

    def drain(p, carry):
        to_beside(p, 0).wait_send()
        to_beside(p, 1).wait_send()
        over(p).wait_send()

        @pl.when(p < z)
        def _():
            lower(p).wait_send()

        return carry

    lax.fori_loop(0, z + 1, drain, 0)


def per_device(
    resid_in, out_grad, attn_gain, q_weight, key_value_weight, o_weight, moe_gain, router, expert_in,
    expert_out, qkv_down, q_up, key_value_up_factor, o_down, o_up, expert_in_down, expert_in_up,
    expert_out_down, expert_out_up, expert_ids, doc_starts, doc_adapter,
):
    blocks = lax.axis_size("ctx")
    planes = blocks // 4
    rows, width = resid_in.shape
    block = 2 * rows
    me, ep = lax.axis_index("ctx"), lax.axis_index("ep")
    positions = me * block + jnp.arange(block, dtype=jnp.int32)
    opened = doc_starts[None, :] <= positions[:, None]
    in_doc = positions - jnp.max(jnp.where(opened, doc_starts[None, :], 0), axis=1)
    steps = jnp.arange(HEAD // 2, dtype=F32)
    angles = in_doc.astype(F32)[:, None] * jnp.power(10000.0, -2.0 * steps / HEAD)[None, :]
    cosine, sine = jnp.tile(jnp.cos(angles), (1, 4)), jnp.tile(jnp.sin(angles), (1, 4))
    attn_gain, moe_gain = attn_gain[None, :], moe_gain[None, :]
    heads = q_weight.shape[1]
    kv = key_value_weight.shape[2]
    experts = expert_in.shape[0]

    def shape(dims, kind=F32):
        return jax.ShapeDtypeStruct(dims, kind)

    def dma(*dims):
        return pltpu.SemaphoreType.DMA(dims)

    x_all, g_all, gates, x2, h2, query, kvall, mids, lse, att, mid_o, mask = pl.pallas_call(
        functools.partial(attend_kernel, planes),
        out_shape=[
            shape((block, width), BF16), shape((block, width), BF16), shape((block, 2 * experts)),
            shape((block, width)), shape((block, width), BF16), shape((block, heads), BF16),
            shape((blocks, 2, block, kv), BF16), shape((block, 3 * SPAN), BF16), shape((4, 1, 2 * block)),
            shape((block, heads)), shape((block, SPAN), BF16), shape((block, 128)),
        ],
        in_specs=[VMEM] * 3 + [SMEM] * 2 + [VMEM] * 13,
        out_specs=[VMEM] * 12,
        scratch_shapes=[
            pltpu.VMEM((block, 128), BF16), pltpu.VMEM((2, heads, width), BF16),
            pltpu.VMEM((2, heads, SPAN), BF16), pltpu.VMEM((2, block, heads), BF16),
            pltpu.VMEM((4, 128, 2 * block), BF16), pltpu.VMEM((4, 1, 2 * block), F32),
            pltpu.VMEM((4, 1, 2 * block), F32), pltpu.VMEM((4, HEAD, 2 * block), F32),
            dma(6), dma(6), dma(3, blocks), dma(blocks),
        ],
        compiler_params=pltpu.CompilerParams(
            collective_id=1, has_side_effects=True, vmem_limit_bytes=60 << 20
        ),
        name="attend",
    )(
        resid_in, out_grad, expert_ids, doc_starts, doc_adapter, attn_gain, moe_gain, q_weight,
        key_value_weight, o_weight, qkv_down, q_up, key_value_up_factor, o_down, o_up, router, cosine, sine,
    )

    block_out, d_x2, d_attn, d_mid_o, grads, grad_o_up = pl.pallas_call(
        expert_kernel,
        out_shape=[
            shape((rows, width), BF16), shape((block, width)), shape((block, width), BF16),
            shape((block, SPAN), BF16), shape((experts, 144, width), BF16), shape((SPAN, width)),
        ],
        in_specs=[VMEM] * 9 + [HBM] * 6,
        out_specs=[VMEM] * 6,
        scratch_shapes=[
            pltpu.VMEM(expert_in.shape, BF16), pltpu.VMEM(expert_out.shape, BF16),
            pltpu.VMEM(expert_in_down.shape, BF16), pltpu.VMEM(expert_in_up.shape, BF16),
            pltpu.VMEM(expert_out_down.shape, BF16), pltpu.VMEM(expert_out_up.shape, BF16),
            pltpu.VMEM((block, width), F32), pltpu.VMEM((block, width), F32), pltpu.VMEM((block, 128), F32),
            pltpu.VMEM((2, block, width), BF16), pltpu.VMEM((2, rows, width), BF16),
            pltpu.VMEM((2, 8, block), F32), dma(experts, 6), dma(3), dma(3),
        ],
        compiler_params=pltpu.CompilerParams(
            collective_id=2, has_side_effects=True, vmem_limit_bytes=60 << 20
        ),
        name="experts",
    )(
        h2, g_all, gates, x2, mask, mid_o, moe_gain, router, o_up, expert_in, expert_out,
        expert_in_down, expert_in_up, expert_out_down, expert_out_up,
    )

    in_grad, grad_down, grad_q_up, grad_kv_up, grad_o_down = pl.pallas_call(
        functools.partial(back_kernel, planes),
        out_shape=[
            shape((rows, width), BF16), shape((3 * SPAN, width)), shape((SPAN, heads)),
            shape((2, SPAN, kv)), shape((SPAN, heads)),
        ],
        in_specs=[VMEM] * 2 + [HBM] + [VMEM] * 7 + [SMEM] * 2 + [VMEM] * 10,
        out_specs=[VMEM] * 5,
        scratch_shapes=[
            pltpu.VMEM((blocks, 2, block, kv), BF16), pltpu.VMEM((4, 128, 2 * block), BF16),
            pltpu.VMEM((4, 2 * block, 128), BF16), pltpu.VMEM((4, 128, 2 * block), BF16),
            pltpu.VMEM((4, 2 * block, 128), BF16), pltpu.VMEM((4, HEAD, 2 * block), F32),
            pltpu.VMEM((4, 1, 2 * block), F32), pltpu.VMEM((planes, 2, 2, block, kv), BF16),
            pltpu.VMEM((planes, 2, block, kv), BF16), pltpu.VMEM((planes, 2, block, kv), BF16),
            pltpu.VMEM((planes, 2, block, kv), BF16), pltpu.VMEM((planes, 2, block, kv), BF16),
            pltpu.VMEM((2, rows, width), BF16), pltpu.VMEM((2, block, 3 * SPAN), BF16),
            pltpu.SemaphoreType.DMA, dma(2), dma(2), dma(planes, 2), dma(planes, 2),
            dma(planes), dma(planes), dma(planes), dma(planes),
        ],
        compiler_params=pltpu.CompilerParams(
            collective_id=3, has_side_effects=True, vmem_limit_bytes=60 << 20
        ),
        name="back",
    )(
        x_all, query, kvall, mids, lse, att, d_attn, d_mid_o, d_x2, mask, doc_starts, doc_adapter,
        attn_gain, q_weight, key_value_weight, o_weight, qkv_down, q_up, key_value_up_factor, o_down,
        cosine, sine,
    )

    grads, grad_q_up, grad_kv_up, grad_o_down = lax.psum((grads, grad_q_up, grad_kv_up, grad_o_down), "ctx")
    grad_o_up, grad_down = lax.psum(
        (jnp.where(ep == 0, grad_o_up, 0.0), jnp.where(ep == 0, grad_down, 0.0)), ("ctx", "ep")
    )
    grads = grads.astype(F32)
    ein_down = jnp.swapaxes(grads[:, :64], 1, 2)
    ein_up = jnp.stack([grads[:, 64:96, :FF], grads[:, 64:96, FF:]], axis=1)
    eout_down = jnp.swapaxes(
        jnp.concatenate([grads[:, 96:112, :FF], grads[:, 96:112, FF:]], axis=1), 1, 2
    )
    eout_up = grads[:, 112:144]
    return (
        block_out, in_grad, grad_down.T, grad_q_up, grad_kv_up, grad_o_down.T, grad_o_up,
        ein_down, ein_up, eout_down, eout_up,
    )


def solution(mesh):
    placed = (
        P(("ctx", "ep"), None),
        P(("ctx", "ep"), None),
        P(),
        P(None, "ep"),
        P(None, None, "ep"),
        P("ep", None),
        P(),
        P(),
        P("ep", None, None),
        P("ep", None, None),
        P(),
        P(None, "ep"),
        P(None, None, "ep"),
        P("ep", None),
        P(),
        P("ep", None, None),
        P("ep", None, None, None),
        P("ep", None, None),
        P("ep", None, None),
        P(("ctx", "ep"), None),
        P(),
        P(),
    )
    return jax.shard_map(
        per_device,
        mesh=mesh,
        in_specs=placed,
        out_specs=(
            P(("ctx", "ep"), None),
            P(("ctx", "ep"), None),
            P(),
            P(None, "ep"),
            P(None, None, "ep"),
            P("ep", None),
            P(),
            P("ep", None, None),
            P("ep", None, None, None),
            P("ep", None, None),
            P("ep", None, None),
        ),
        check_vma=False,
    )
```

time: 1060 us -> 536 us (0.51); the launches traced: 1050 us -> 535 us
  waiting for transfers between devices: 576 us -> 321 us
  Pallas kernels: 0 us -> 170 us
  starting transfers between devices: 133 us -> 0.12 us
  local copies, waits for them, and re-layouts: 128 us -> 24 us
  matrix products: 90.2 us -> 0 us
  other arithmetic: 71.2 us -> 6.5 us
  blocking collectives: 21.6 us -> 0 us
  loops' own time: 12.3 us -> 0 us
    pallas_call x0 -> x3, Pallas kernels: none -> 170 us  [the longest x1 59.2 us: per_device(): pl.pallas_call(functools.partial(back_kernel, planes), out_shape=[shape((...]
    all_to_all x5 -> x0, waiting for transfers between devices: 120 us -> none  [the longest x1 36.3 us: per_device(): lax.all_to_all(send_rows, 'ep', split_axis=0, concat_axis=2, tiled=True)]
    ppermute x64 -> x0, starting transfers between devices: 108 us -> none  [shifted_2(): return lax.ppermute(value, axis, pairs)]
    dot_general x54 -> x0, matrix products: 90.2 us -> none  [the longest x1 14.8 us: expert_forward(): jnp.einsum('end,edf->enf', got_rows, expert_in, preferred_element_type=jn...]
    ppermute x64 -> x0, waiting for transfers between devices: 72.7 us -> none  [shifted_2(): return lax.ppermute(value, axis, pairs)]
    all_gather x2 -> x0, waiting for transfers between devices: 71 us -> none  [the longest x1 38.1 us: per_device(): key_piece = lax.all_gather(key_head_rows, 'ctx', axis=0, tiled=True)]
    psum x2 -> x3, waiting for transfers between devices: 256 us -> 320 us  [the longest x2 194 us: per_device(): lax.psum((grads, grad_q_up, grad_kv_up, grad_o_down), 'ctx')]
    gather x10 -> x0, local copies, waits for them, and re-layouts: 33.2 us -> none  [the longest x1 8.32 us: per_device(): jnp.take(back_grads, slot_index, axis=0).reshape(row_count, top_count, -1)]
  transfers between devices with their start and end apart: 77 -> 3, of which waited for: 64 -> 3; matrix products, arithmetic and copies ran while one was open for 9% -> 2% of each run, Pallas kernels for 0% -> 0%
where the time goes in v1:
time: 536 us; the launch traced here: 535 us
  waiting for transfers between devices  321 us (60%)
  Pallas kernels  170 us (32%)
  local copies, waits for them, and re-layouts  24 us (4%)
  between operations  13.9 us (3%)
  other arithmetic  6.5 us (1%)
    psum x2, waiting for transfers between devices, per_device(): lax.psum((grads, grad_q_up, grad_kv_up, grad_o_down), 'ctx')  194 us
    psum x1, waiting for transfers between devices, per_device(): lax.psum((jnp.where(ep == 0, grad_o_up, 0.0), jnp.where(ep == 0, grad_dow...  126 us
    pallas_call x1, Pallas kernels, per_device(): pl.pallas_call(functools.partial(back_kernel, planes), out_shape=[shape((...  59.2 us
    pallas_call x1, Pallas kernels, per_device(): pl.pallas_call(functools.partial(attend_kernel, planes), out_shape=[shape...  55.8 us
    pallas_call x1, Pallas kernels, per_device(): pl.pallas_call(expert_kernel, out_shape=[shape((rows, width), BF16), shap...  55.1 us
    unnamed x28, local copies, waits for them, and re-layouts  19.8 us
  transfers between devices with their start and end apart: 3, of which 3 were waited for; matrix products, arithmetic and copies ran while one was open for 2% of the time, Pallas kernels for 0%

profile of v1, /device:TPU:0, one launch (start us, length us, event | category | flops | bytes accessed | tf_op | source)
XLA Modules:
  0.0 535.3 jit_solution(14116723143026329705)
XLA Ops:
  7.2 0.0 all-reduce.10.cloned.1.call-start
  7.3 0.7 select_reduce_fusion
  8.0 1.4 copy.57.ids_ref
  9.4 0.2 multiply_sine_fusion
  9.6 0.8 copy.62.sin_ref
  10.4 1.5 copy.59.o_down_ref
  11.9 0.8 copy.61.cos_ref
  12.7 1.6 copy.60.router_ref
  14.3 1.8 copy.58.qkv_down_ref
  16.0 2.3 copy.65.out_down_hbm
  18.3 2.7 copy.64.in_down_hbm
  21.0 55.8 %attend.1 = (bf16[256,1024]{1,0:T(8,128)(2,1)}, bf16[256,1024]{1,0:T(8,128)(2,1)}, f32[256,16]{1,0:T(8,128)}, f32[256,1024]{1,0:T(8,128)}, bf16[256,1024]{1,0:T(...) custom-call(bf16[128,1024]{1,0:T(8,128)(2,1)} %resid_ref.1, ...), custom_call_target="tpu_custom_call" | custom-call | tf_op jit(solution)/shard_map/attend/pallas_call | solution.py:700
  76.8 55.1 %experts.1 = (bf16[128,1024]{1,0:T(8,128)(2,1)}, f32[256,1024]{1,0:T(8,128)}, bf16[256,1024]{1,0:T(8,128)(2,1)}, bf16[256,32]{1,0:T(8,128)(2,1)}, bf16[8,144,1024]{2,1,0:T(8,128)(2,1)}, /*index=5*/f32[32,1024]{1,0:T(8,128)}) custom-call(bf16[256,1024]{1,0:T(8,128)(2,1)} %get-tuple-element.34.h2_ref, bf16[256,1024]{1,0:T(8,128)(2,1)} %get-tuple-element.35.g_all, ...), custom_call_target="tpu_custom_call" | custom-call | tf_op jit(solution)/shard_map/experts/pallas_call | solution.py:726
  131.9 0.0 copy-start.3
  131.9 59.2 %back.1 = (bf16[128,1024]{1,0:T(8,128)(2,1)}, f32[96,1024]{1,0:T(8,128)}, f32[32,512]{1,0:T(8,128)}, f32[2,32,256]{2,1,0:T(8,128)}, f32[32,512]{1,0:T(8,128)}) custom-call(bf16[256,1024]{1,0:T(8,128)(2,1)} %get-tuple-element.41.x_all, bf16[256,512]{1,0:T(8,128)(2,1)} %get-tuple-element.42.query_ref, bf16[16,2,256,256]{3,2,1,0:T(8,128)(2,1)} %get-tuple-element.43.kv_hbm, ...), custom_call_target="tpu_custom_call" | custom-call | tf_op jit(solution)/shard_map/back/pallas_call | solution.py:751
  191.1 0.0 all-reduce.10.cloned.1.call-update
  191.1 0.0 all-reduce.6.cloned.1.call-start
  191.2 0.7 all-reduce.6.cloned.1.call-update
  191.9 0.0 all-reduce.8.cloned.1.call-start
  191.9 0.0 copy-done.3
  192.0 0.7 broadcast_select_fusion
  192.6 1.8 select_bitcast_fusion
  194.4 0.0 all-reduce.8.cloned.1.call-update
  194.4 92.5 %all-reduce.10.cloned.1.call-done = (f32[32,512]{1,0:T(8,128)}, f32[2,32,256]{2,1,0:T(8,128)}, f32[512,32]{0,1:T(8,128)}) async-done(((f32[32,512]{1,0:T(8,128)}, f32[2,32,256]{2,1,0:T(8,128)}, f32[512,32]{0,1:T(8,128)}), (f32[32,512]{1,0:T(8,128)}, f32[2,32,256]{2,1,0:T(8,128)}, f32[512,32]{0,1:T(8,128)})) %all-reduce.10.cloned.1.call-update) | async-done | bytes 196624 | tf_op jit(solution)/shard_map/psum | solution.py:780
  286.9 101.8 %all-reduce.6.cloned.1.call-done = bf16[8,144,1024]{2,1,0:T(8,128)(2,1)} async-done(((bf16[8,144,1024]{2,1,0:T(8,128)(2,1)}), bf16[8,144,1024]{2,1,0:T(8,128)(2,1)}) %all-reduce.6.cloned.1.call-update) | async-done | bytes 2359312 | tf_op jit(solution)/shard_map/psum | solution.py:780
  388.8 2.2 convert_element_type.11
  391.0 0.0 copy-start
  391.0 0.1 slice_bitcast_fusion.2
  391.1 0.1 pad_maximum_fusion
  391.2 1.1 copy.70
  392.2 0.8 copy-done
  393.1 0.0 copy-start.2
  393.1 0.8 maximum_bitcast_fusion
  393.9 1.1 slice.29
  395.0 1.5 slice_bitcast_fusion
  396.5 125.7 %all-reduce.8.cloned.1.call-done = (f32[1024,96]{0,1:T(8,128)}, f32[32,1024]{1,0:T(8,128)}) async-done(((f32[1024,96]{0,1:T(8,128)}, f32[32,1024]{1,0:T(8,128)}), (f32[1024,96]{0,1:T(8,128)}, f32[32,1024]{1,0:T(8,128)})) %all-reduce.8.cloned.1.call-update) | async-done | bytes 524304 | tf_op jit(solution)/shard_map/psum | solution.py:781
  522.2 0.0 copy-done.1
  522.2 0.7 copy.82
  522.9 0.0 copy-done.2
  522.9 0.7 copy.83
  523.6 1.8 copy.84
  525.3 0.0 copy-done.6
  525.3 0.6 copy.85
  526.0 0.0 copy-done.5
  526.0 0.6 copy.86
  526.6 0.0 copy-done.4
  526.6 0.6 copy.87
  527.2 1.6 copy.88
  (10 shorter events, 0.1 us)
Async XLA Ops:
  7.2 279.8 %all-reduce.10.cloned.1.call-start = ((), (), s32[]{:S(2)}) async-start(), calls=%async_computation.2 | async-start | bytes 393216 | tf_op jit(solution)/shard_map/psum | solution.py:780
  131.9 60.1 %copy-start.3 = (f32[32,1024]{1,0:T(8,128)S(1)}, f32[32,1024]{1,0:T(8,128)}, u32[]{:S(2)}) copy-start(f32[32,1024]{1,0:T(8,128)} %get-tuple-element.55) | copy-start | bytes 393220
  191.1 197.6 %all-reduce.6.cloned.1.call-start = ((), (), s32[]{:S(2)}) async-start(), calls=%async_computation | async-start | bytes 4718592 | tf_op jit(solution)/shard_map/psum | solution.py:780
  191.9 330.3 %all-reduce.8.cloned.1.call-start = ((), (), s32[]{:S(2)}) async-start(), calls=%async_computation.1 | async-start | bytes 1048576 | tf_op jit(solution)/shard_map/psum | solution.py:781
  391.0 2.0 copy-start
  393.0 129.1 %copy-start.1 = (bf16[128,1024]{1,0:T(8,128)(2,1)S(1)}, bf16[128,1024]{1,0:T(8,128)(2,1)}, u32[]{:S(2)}) copy-start(bf16[128,1024]{1,0:T(8,128)(2,1)} %get-tuple-element.112) | copy-start | bytes 786436
  393.1 129.8 %copy-start.2 = (bf16[128,1024]{1,0:T(8,128)(2,1)S(1)}, bf16[128,1024]{1,0:T(8,128)(2,1)}, u32[]{:S(2)}) copy-start(bf16[128,1024]{1,0:T(8,128)(2,1)} %get-tuple-element.113) | copy-start | bytes 786436
  393.9 131.4 %copy-start.6 = (f32[32,512]{1,0:T(8,128)S(1)}, f32[32,512]{1,0:T(8,128)}, u32[]{:S(2)}) copy-start(f32[32,512]{1,0:T(8,128)} %get-tuple-element.115) | copy-start | bytes 196612
  393.9 132.0 %copy-start.5 = (f32[2,32,256]{2,1,0:T(8,128)S(1)}, f32[2,32,256]{2,1,0:T(8,128)}, u32[]{:S(2)}) copy-start(f32[2,32,256]{2,1,0:T(8,128)} %get-tuple-element.116) | copy-start | bytes 196612
  393.9 132.7 %copy-start.4 = (f32[512,32]{0,1:T(8,128)S(1)}, f32[512,32]{0,1:T(8,128)}, u32[]{:S(2)}) copy-start(f32[512,32]{0,1:T(8,128)} %get-tuple-element.117) | copy-start | bytes 196612
Sparse Core Ops, SparseCore 0:
  191.3 95.6 all-reduce.9
  290.5 98.2 all-reduce.5
  394.8 127.2 all-reduce.7

commit v2 on v1

v2 whole, which is shorter than its diff:
```python
import functools

import jax
import jax.numpy as jnp
import numpy as np
from jax import lax
from jax.experimental import pallas as pl
from jax.experimental.pallas import tpu as pltpu
from jax.sharding import PartitionSpec as P

MESH = pl.DeviceIdType.MESH
VMEM = pl.BlockSpec(memory_space=pltpu.VMEM)
SMEM = pl.BlockSpec(memory_space=pltpu.SMEM)
HBM = pl.BlockSpec(memory_space=pl.ANY)
F32 = jnp.float32
BF16 = jnp.bfloat16

HEAD = 64
FF = 512
RANK = 16
SPAN = 32
EPS = 1e-06
LOW = -1e30
SCALE = 0.125

NN = (((1,), (0,)), ((), ()))
NT = (((1,), (1,)), ((), ()))
TN = (((0,), (0,)), ((), ()))


def dot(left, right, dims=NN):
    return lax.dot_general(left, right, dims, preferred_element_type=F32)


def iota(shape, dim):
    return lax.broadcasted_iota(jnp.int32, shape, dim)


def rms(values, gain):
    return values * lax.rsqrt(jnp.mean(values * values, axis=-1, keepdims=True) + EPS) * gain


def rms_back(values, gain, upstream):
    factor = lax.rsqrt(jnp.mean(values * values, axis=-1, keepdims=True) + EPS)
    scaled = upstream * gain
    return factor * scaled - values * factor * factor * factor * jnp.mean(
        scaled * values, axis=-1, keepdims=True
    )


def rotate(values, cosine, sine, sign):
    width = values.shape[1]
    copies = width // 128
    cosine = jnp.concatenate([cosine] * copies, axis=1)
    sine = jnp.concatenate([sine] * copies, axis=1)
    first = iota(values.shape, 1) % HEAD < HEAD // 2
    ahead = pltpu.roll(values, width - HEAD // 2, 1)
    behind = pltpu.roll(values, HEAD // 2, 1)
    return values * cosine + sign * jnp.where(first, -ahead, behind) * sine


def doc_scan(positions, starts_ref, adapters_ref):
    own_start = jnp.zeros(positions.shape, jnp.int32)
    adapter = jnp.zeros(positions.shape, jnp.int32)
    for number in range(starts_ref.shape[0]):
        opened = starts_ref[number] <= positions
        own_start = jnp.where(opened, starts_ref[number], own_start)
        adapter = jnp.where(opened, adapters_ref[number], adapter)
    return own_start, adapter


def place():
    me = lax.axis_index("ctx")
    ep = lax.axis_index("ep")
    return me, ep, me // 4, (me // 2) % 2, me % 2


def block_of(z, x, c):
    return (z * 2 + x) * 2 + c


def signal(device):
    pl.semaphore_signal(
        pltpu.get_barrier_semaphore(), inc=1, device_id=device, device_id_type=MESH
    )


def remote(src, dst, send, recv, device):
    return pltpu.make_async_remote_copy(
        src_ref=src,
        dst_ref=dst,
        send_sem=send,
        recv_sem=recv,
        device_id=device,
        device_id_type=MESH,
    )


def span(start, count):
    return pl.ds(pl.multiple_of(start, count), count)


def pad_query(rows, target):
    count = rows.shape[0]
    upper = iota((count, 128), 1) >= HEAD
    for group in range(4):
        tile = rows[:, 128 * group : 128 * group + 128]
        turned = pltpu.roll(tile, HEAD, 1)
        keep = upper if group % 2 else jnp.logical_not(upper)
        low, high = (turned, tile) if group % 2 else (tile, turned)
        target[group, :count, :] = jnp.where(keep, low, 0.0).astype(BF16)
        target[group, count:, :] = jnp.where(keep, high, 0.0).astype(BF16)


def pad_query_t(columns, target):
    for group in range(4):
        both = jnp.concatenate(
            [
                columns[128 * group : 128 * group + 64],
                columns[128 * group + 64 : 128 * group + 128],
            ],
            axis=1,
        ).astype(BF16)
        blank = jnp.zeros(both.shape, BF16)
        own = HEAD * (group % 2)
        target[group, own : own + HEAD, :] = both
        target[group, HEAD - own : 2 * HEAD - own, :] = blank


def fold(wide):
    count = wide.shape[0] // 2
    return jnp.concatenate([wide[:count], wide[count:]], axis=1)


INPUTS = (
    "resid", "grad", "ids", "starts", "adapters", "attn_gain", "moe_gain", "freq",
    "qkv_down", "q_up", "kv_up", "o_down", "o_up", "router",
    "q_hbm", "kv_hbm", "o_hbm", "in_hbm", "out_hbm", "in_down_hbm", "in_up_hbm", "out_down_hbm", "out_up_hbm",
)
OUTPUTS = ("block_out", "in_grad", "final", "early_out", "late_out")


def layer_kernel(planes, slots, names, *refs):
    r = dict(zip(names, refs))
    r = type("Refs", (), r)
    r.acc_out, r.acc_h2 = r.halves.at[0], r.halves.at[1]
    me, ep, z, x, c = place()
    blocks = 4 * planes
    pair = {"ctx": me, "ep": 1 - ep}
    up = {"ctx": jnp.minimum(me + 4, blocks - 1), "ep": ep}
    down = {"ctx": jnp.maximum(me - 4, 0), "ep": ep}
    across = {"ctx": block_of(z, 1 - x, c), "ep": ep}
    beside = {"ctx": block_of(z, x, 1 - c), "ep": ep}
    rows = r.resid.shape[0]
    block = 2 * rows
    mine = span(ep * rows, rows)
    theirs = span(rows - ep * rows, rows)
    experts = r.in_hbm.shape[0]
    quarter_rows = r.pack.shape[1]
    piece_rows = quarter_rows // planes
    kept = r.from_across.shape[0]

    load_q = pltpu.make_async_copy(r.q_hbm, r.q_w, r.load_sem.at[0])
    load_kv = pltpu.make_async_copy(r.kv_hbm, r.kv_w, r.load_sem.at[1])
    load_o = pltpu.make_async_copy(r.o_hbm, r.ow_all.at[ep], r.load_sem.at[2])
    load_kv.start()
    load_q.start()
    load_o.start()
    weights = (
        (r.in_hbm, r.w_in), (r.out_hbm, r.w_out), (r.in_down_hbm, r.w_in_down),
        (r.in_up_hbm, r.w_in_up), (r.out_down_hbm, r.w_out_down), (r.out_up_hbm, r.w_out_up),
    )

    def quarter_at(turn):
        return jnp.where(turn % 2 == 0, 1 - x, x) * 2 + jnp.where(turn < 2, 1 - c, c)

    def expert_at(turn):
        return 2 * quarter_at(turn // 2) + turn % 2

    def expert_loads(turn):
        e, slot = expert_at(turn), turn % slots
        return [
            pltpu.make_async_copy(source.at[e], held.at[slot], r.expert_sem.at[slot, number])
            for number, (source, held) in enumerate(weights)
        ]

    def begin(turn, carry):
        for copy in expert_loads(turn):
            copy.start()
        return carry

    lax.fori_loop(0, slots, begin, 0)

    signal(pair)

    def greet(step, carry):
        signal({"ctx": lax.rem(me + step, blocks), "ep": ep})
        return carry

    lax.fori_loop(1, blocks, greet, 0)
    pl.semaphore_wait(pltpu.get_barrier_semaphore(), blocks)

    def swap(number, src, dst):
        return remote(src, dst, r.pair_send.at[number], r.pair_recv.at[number], pair)

    send_x = swap(0, r.resid, r.x_all.at[mine])
    send_x.start()

    hot = jnp.zeros((r.ids.shape[0], rows), F32)
    hot = jnp.zeros((128, rows), F32)
    numbers = iota((128, rows), 0)
    for choice in range(r.ids.shape[0]):
        hot = hot + jnp.where(r.ids[choice : choice + 1, :] == numbers, 1.0, 0.0)
    r.hot_all[mine, :] = hot.T.astype(BF16)
    r.x_all[mine, :] = r.resid[...]
    r.g_all[mine, :] = r.grad[...]
    r.od_all[ep] = r.o_down[...]
    position = me * block + iota((block, 128), 0)
    own_start, adapter = doc_scan(position, r.starts, r.adapters)
    r.mask[...] = jnp.where((iota((block, 128), 1) % SPAN) // RANK == adapter, 1.0, 0.0)
    angles = (position - own_start).astype(F32) * r.freq[...]
    r.cosine[...] = jnp.cos(angles)
    r.sine[...] = jnp.sin(angles)
    row_pos = me * block + iota((8, 2 * block), 1) % block
    row_start, unused = doc_scan(row_pos, r.starts, r.adapters)
    start_row, pos_row = row_start[:1], row_pos[:1]

    def ring(number, half, way, target):
        part = r.kvall.at[number, :, mine if half == 0 else theirs, :]
        return remote(part, part, r.ring_send.at[way, number, half], r.ring_recv.at[number, half], target)

    def forward_own(p, half):
        number = block_of(p, x, c)

        @pl.when(z < planes - 1)
        def _():
            ring(number, half, 0, up).start()

        ring(number, half, 1, across).start()
        ring(number, half, 2, beside).start()

    def forward_across(p, half):
        number = block_of(p, 1 - x, c)
        ring(number, half, 1, across).wait_recv()
        ring(number, half, 2, beside).start()

    def arrive_beside(p):
        for column in (0, 1):
            for half in (0, 1):
                ring(block_of(p, column, 1 - c), half, 2, beside).wait_recv()

    def project(here):
        h1 = rms(r.x_all[here, :].astype(F32), r.attn_gain[...]).astype(BF16)
        r.h1[here, :] = h1
        mids = (dot(h1, r.qkv_down[...], NT) * r.mask[here, : 3 * SPAN]).astype(BF16)
        r.mids[here, :] = mids
        k_lin = dot(h1, r.kv_w[0]) + dot(mids[:, SPAN : 2 * SPAN], r.kv_up[0])
        r.kvall[me, 0, here, :] = rotate(k_lin, r.cosine[here, :], r.sine[here, :], 1.0).astype(BF16)
        r.kvall[me, 1, here, :] = (dot(h1, r.kv_w[1]) + dot(mids[:, 2 * SPAN :], r.kv_up[1])).astype(BF16)

    load_kv.wait()
    project(mine)
    forward_own(z, 0)
    send_x.wait_recv()
    load_o.wait()
    send_ow = swap(3, r.ow_all.at[ep], r.ow_all.at[ep])
    send_od = swap(4, r.od_all.at[ep], r.od_all.at[ep])
    send_hot = swap(1, r.hot_all.at[mine], r.hot_all.at[mine])
    send_g = swap(2, r.grad, r.g_all.at[mine])
    for copy in (send_ow, send_od, send_hot, send_g):
        copy.start()
    project(theirs)
    forward_own(z, 1)
    load_q.wait()
    q_lin = dot(r.h1[...], r.q_w[...]) + dot(r.mids[:, :SPAN], r.q_up[...])
    query = rotate(q_lin, r.cosine[...], r.sine[...], 1.0).astype(BF16).astype(F32)
    pad_query(query, r.qn)
    pad_query_t((query * SCALE).T, r.qt)
    r.m_s[...] = jnp.full(r.m_s.shape, LOW, F32)
    r.l_s[...] = jnp.zeros(r.l_s.shape, F32)
    r.acc[...] = jnp.zeros(r.acc.shape, F32)
    forward_across(z, 0)
    forward_across(z, 1)
    arrive_beside(z)

    def head_step(p, group, masked):
        tile = slice(128 * (group // 2), 128 * (group // 2) + 128)
        scores, peak = [], None
        sees = start_row <= (4 * p + 1) * block
        for b in range(4):
            s = dot(r.kvall[4 * p + b, 0, :, tile], r.qt[group])
            if masked[b]:
                key = (4 * p + b) * block + iota(s.shape, 0)
                s = jnp.where((key <= pos_row) & (key >= start_row), s, LOW)
            scores.append(s)
            highest = jnp.max(s, axis=0, keepdims=True)
            if not masked[b]:
                highest = jnp.where(sees, highest, LOW)
            peak = highest if peak is None else jnp.maximum(peak, highest)
        old = r.m_s[group]
        new = jnp.maximum(old, peak)
        r.m_s[group] = new
        blind = jnp.where(sees, new, -LOW)
        decay = jnp.exp(old - new)
        total = r.l_s[group] * decay
        grown = r.acc[group] * decay
        for b in range(4):
            w = jnp.exp(scores[b] - (new if masked[b] else blind))
            total = total + jnp.sum(w, axis=0, keepdims=True)
            added = dot(r.kvall[4 * p + b, 1, :, tile], w.astype(BF16), TN)
            grown = grown + added[HEAD * (group % 2) : HEAD * (group % 2) + HEAD]
        r.l_s[group] = total
        r.acc[group] = grown

    def send_att(group):
        part = r.att_all.at[ep, :, pl.ds(128 * group, 128)]
        return swap(5 + group, part, part)

    def settle(group):
        r.lse[group] = r.m_s[group] + jnp.log(r.l_s[group])
        done = r.acc[group] / r.l_s[group]
        attended = jnp.concatenate([done[:, :block], done[:, block:]], axis=0).T
        tile = slice(128 * group, 128 * group + 128)
        r.att[:, tile] = attended
        r.att_all[ep, :, tile] = attended.astype(BF16)
        send_att(group).start()

    def plane_forward(turn, carry):
        p = z - turn

        def heads(group):
            @pl.when(turn == 0)
            def _():
                head_step(p, group, (True,) * 4)

            @pl.when((turn > 0) & (p > 0))
            def _():
                head_step(p, group, (False,) * 4)

            @pl.when((turn > 0) & (p == 0))
            def _():
                head_step(p, group, (True, False, False, False))

            @pl.when(p == 0)
            def _():
                settle(group)

        heads(0)

        @pl.when(p > 0)
        def _():
            ring(block_of(p - 1, x, c), 0, 0, up).wait_recv()
            forward_own(p - 1, 0)

        heads(1)

        @pl.when(p > 0)
        def _():
            ring(block_of(p - 1, x, c), 1, 0, up).wait_recv()
            forward_own(p - 1, 1)

        heads(2)

        @pl.when(p > 0)
        def _():
            forward_across(p - 1, 0)

        heads(3)

        @pl.when(p > 0)
        def _():
            forward_across(p - 1, 1)
            arrive_beside(p - 1)

        return carry

    lax.fori_loop(0, z + 1, plane_forward, 0)

    def ring_drain(p, carry):
        for side in (0, 1):

            @pl.when(z < planes - 1)
            def _():
                ring(block_of(p, x, c), side, 0, up).wait_send()

            ring(block_of(p, x, c), side, 1, across).wait_send()
            ring(block_of(p, x, c), side, 2, beside).wait_send()
            ring(block_of(p, 1 - x, c), side, 2, beside).wait_send()
        return carry

    send_ow.wait_recv()
    send_od.wait_recv()

    def half_product(index, carry):
        which = jnp.where(index == 0, ep, 1 - ep)

        @pl.when(index == 1)
        def _():
            for group in range(4):
                send_att(group).wait_recv()

        r.halves[which] = dot(r.att_all[which], r.ow_all[which])
        r.half_mid[which] = dot(r.att_all[which], r.od_all[which], NT)
        return carry

    lax.fori_loop(0, 2, half_product, 0)
    mid_o = ((r.half_mid[0] + r.half_mid[1]) * r.mask[:, :SPAN]).astype(BF16)
    r.mid_o[...] = mid_o
    x2 = r.x_all[...].astype(F32) + (r.halves[0] + r.halves[1]) + dot(mid_o, r.o_up[...])
    r.x2[...] = x2
    h2 = rms(x2, r.moe_gain[...]).astype(BF16)
    r.h2[...] = h2
    send_hot.wait_recv()
    logits = dot(h2, r.router[...], NT)
    chosen = r.hot_all[:, : 2 * experts].astype(F32) > 0.5
    logits = jnp.where(chosen, logits, LOW)
    grown = jnp.where(chosen, jnp.exp(logits - jnp.max(logits, axis=1, keepdims=True)), 0.0)
    gates = grown / jnp.sum(grown, axis=1, keepdims=True)
    r.gates[...] = gates
    r.acc_out[...] = jnp.zeros(r.acc_out.shape, F32)
    r.acc_h2[...] = jnp.zeros(r.acc_h2.shape, F32)
    r.dgates[...] = jnp.zeros(r.dgates.shape, F32)
    r.pack[:, 288:, :] = jnp.zeros((4, quarter_rows - 288, r.pack.shape[2]), BF16)
    send_g.wait_recv()

    def to_core(column):
        return remote(
            r.pack.at[2 * column + 1 - c], r.core_recv.at[column],
            r.core_send_sem.at[column], r.core_recv_sem.at[column], beside,
        )

    to_column = remote(r.pack.at[2 * (1 - x) + c], r.x_recv, r.x_sem.at[0], r.x_sem.at[1], across)
    quarter = 2 * x + c

    def one(turn, carry):
        slot = turn % slots
        e = expert_at(turn)
        for copy in expert_loads(turn):
            copy.wait()
        h2, g = r.h2[...], r.g_all[...]
        mask = r.mask[...]
        gate = jnp.sum(
            jnp.where(iota((block, 2 * experts), 1) == e + ep * experts, r.gates[...], 0.0), axis=1, keepdims=True
        )
        mid_in = (dot(h2, r.w_in_down[slot], NT) * mask[:, : 2 * SPAN]).astype(BF16)
        gate_part = dot(h2, r.w_in[slot, :, :FF]) + dot(mid_in[:, :SPAN], r.w_in_up[slot, 0])
        up_part = dot(h2, r.w_in[slot, :, FF:]) + dot(mid_in[:, SPAN:], r.w_in_up[slot, 1])
        squash = 1.0 / (1.0 + jnp.exp(-gate_part))
        silu = gate_part * squash
        act = (silu * up_part).astype(BF16)
        mid_out = dot(act, r.w_out_down[slot], NT) * mask[:, :SPAN]
        lifted = (dot(g, r.w_out_up[slot], NT) * mask[:, :SPAN]).astype(BF16)
        d_act = dot(g, r.w_out[slot], NT) + dot(lifted, r.w_out_down[slot])
        d_gate = jnp.sum(act.astype(F32) * d_act, axis=1, keepdims=True)
        r.dgates[...] += jnp.where(iota(r.dgates.shape, 1) == e, d_gate, 0.0)
        d_act = d_act * gate
        d_up = (d_act * silu).astype(BF16)
        d_gp = (d_act * up_part * squash * (1.0 + gate_part * (1.0 - squash))).astype(BF16)
        d_mid_in = (
            jnp.concatenate([dot(d_gp, r.w_in_up[slot, 0], NT), dot(d_up, r.w_in_up[slot, 1], NT)], axis=1)
            * mask[:, : 2 * SPAN]
        ).astype(BF16)
        scaled_mid = (mid_out * gate).astype(BF16)
        r.acc_out[...] += dot((act.astype(F32) * gate).astype(BF16), r.w_out[slot]) + dot(
            scaled_mid, r.w_out_up[slot]
        )
        r.acc_h2[...] += (
            dot(d_gp, r.w_in[slot, :, :FF], NT)
            + dot(d_up, r.w_in[slot, :, FF:], NT)
            + dot(d_mid_in, r.w_in_down[slot])
        )
        q = quarter_at(turn // 2)
        first = 144 * (turn % 2)

        def at(offset, count):
            return pl.ds(pl.multiple_of(first + offset, 16), count)

        r.pack[q, at(0, 64), :] = dot(d_mid_in, h2, TN).astype(BF16)
        r.pack[q, at(64, 32), :FF] = dot(mid_in[:, :SPAN], d_gp, TN).astype(BF16)
        r.pack[q, at(64, 32), FF:] = dot(mid_in[:, SPAN:], d_up, TN).astype(BF16)
        r.pack[q, at(96, 16), :] = fold(
            dot((lifted.astype(F32) * gate).astype(BF16), act, TN)
        ).astype(BF16)
        r.pack[q, at(112, 32), :] = dot(scaled_mid, g, TN).astype(BF16)

        @pl.when(turn + slots < experts)
        def _():
            for copy in expert_loads(turn + slots):
                copy.start()

        @pl.when(turn == 1)
        def _():
            to_core(1 - x).start()

        @pl.when(turn == 3)
        def _():
            to_core(x).start()

        def add_core(column):
            to_core(column).wait_recv()
            number = 2 * column + c
            r.pack[number] = (r.pack[number].astype(F32) + r.core_recv[column].astype(F32)).astype(BF16)

        @pl.when(turn == 5)
        def _():
            add_core(1 - x)
            to_column.start()

        @pl.when(turn == 7)
        def _():
            add_core(x)

        return carry

    lax.fori_loop(0, experts, one, 0)

    r.dg_trade[ep] = r.dgates[...].T[:8]
    send_dg = swap(9, r.dg_trade.at[ep], r.dg_trade.at[ep])
    send_dg.start()
    r.trade[ep] = r.acc_h2[...].astype(BF16)
    send_h2 = swap(10, r.trade.at[ep], r.trade.at[ep])
    send_h2.start()
    r.out_trade[0] = r.acc_out[theirs, :].astype(BF16)
    send_out = swap(11, r.out_trade.at[0], r.out_trade.at[1])
    send_out.start()

    to_column.wait_recv()
    r.pack[quarter] = (r.pack[quarter].astype(F32) + r.x_recv[...].astype(F32)).astype(BF16)

    def plane_of(step):
        return lax.rem(z + step, planes)

    def give(step):
        other = plane_of(step)
        return remote(
            r.pack.at[quarter, span(other * piece_rows, piece_rows), :], r.z_recv.at[z],
            r.z_send_sem.at[0, other], r.z_recv_sem.at[0, z], {"ctx": block_of(other, x, c), "ep": ep},
        )

    def take(step):
        other = plane_of(step)
        return remote(
            r.pack.at[quarter, span(other * piece_rows, piece_rows), :], r.z_recv.at[other],
            r.z_send_sem.at[0, other], r.z_recv_sem.at[0, other], {"ctx": block_of(other, x, c), "ep": ep},
        )

    def spread(step):
        other = plane_of(step)
        part = r.final.at[quarter, span(z * piece_rows, piece_rows), :]
        return remote(
            part, part, r.z_send_sem.at[1, other], r.z_recv_sem.at[1, z], {"ctx": block_of(other, x, c), "ep": ep}
        )

    def gather(step):
        other = plane_of(step)
        part = r.final.at[quarter, span(other * piece_rows, piece_rows), :]
        return remote(
            part, part, r.z_send_sem.at[1, other], r.z_recv_sem.at[1, other], {"ctx": block_of(other, x, c), "ep": ep}
        )

    def each_plane(act):
        def step(number, carry):
            act(number)
            return carry

        lax.fori_loop(1, planes, step, 0)

    each_plane(lambda step: give(step).start())

    def stage_own():
        each_plane(lambda step: take(step).wait_recv())
        r.z_recv[z] = r.pack[quarter, span(z * piece_rows, piece_rows), :]

        def add(p, total):
            return total + r.z_recv[p].astype(F32)

        total = lax.fori_loop(0, planes, add, jnp.zeros(r.z_recv.shape[1:], F32))
        r.final[quarter, span(z * piece_rows, piece_rows), :] = total.astype(BF16)
        each_plane(lambda step: spread(step).start())

    def over_final(number, way, target):
        part = r.final.at[number]
        return remote(part, part, r.last_send.at[way, number], r.last_recv.at[number], target)

    def stage_column():
        each_plane(lambda step: gather(step).wait_recv())
        over_final(quarter, 0, across).start()
        over_final(quarter, 1, beside).start()

    def stage_core():
        over_final(2 * (1 - x) + c, 0, across).wait_recv()
        over_final(2 * (1 - x) + c, 1, beside).start()

    def stage_end():
        over_final(2 * x + 1 - c, 1, beside).wait_recv()
        over_final(2 * (1 - x) + 1 - c, 1, beside).wait_recv()
        each_plane(lambda step: give(step).wait_send())
        each_plane(lambda step: spread(step).wait_send())
        over_final(quarter, 0, across).wait_send()
        over_final(quarter, 1, beside).wait_send()
        over_final(2 * (1 - x) + c, 1, beside).wait_send()
        to_core(0).wait_send()
        to_core(1).wait_send()
        to_column.wait_send()

    def small_sum(number, source, landing, result):
        tiles = source.shape[0] // 16
        width = landing.shape[2]
        each = source.shape[1] // width
        owners = tiles * each

        def region(ref, owner):
            return ref.at[span(owner // each * 16, 16), span(owner % each * width, width)]

        def other(step):
            return lax.rem(me + step, blocks)

        def to_owner(step):
            owner = other(step)
            return remote(
                region(source, owner), landing.at[me], r.small_send.at[number, 0, owner],
                r.small_recv.at[number, 0, me], {"ctx": owner, "ep": ep},
            )

        def from_all(step):
            device = other(step)
            return remote(
                region(source, me % owners), landing.at[device], r.small_send.at[number, 0, device],
                r.small_recv.at[number, 0, device], {"ctx": device, "ep": ep},
            )

        def to_all(step):
            device = other(step)
            part = region(result, me % owners)
            return remote(
                part, part, r.small_send.at[number, 1, device], r.small_recv.at[number, 1, me],
                {"ctx": device, "ep": ep},
            )

        def from_owner(step):
            owner = other(step)
            part = region(result, owner)
            return remote(
                part, part, r.small_send.at[number, 1, owner], r.small_recv.at[number, 1, owner],
                {"ctx": owner, "ep": ep},
            )

        def loop(act, mine_too):
            def step(index, carry):
                if mine_too:
                    act(index)
                else:

                    @pl.when(other(index) < owners)
                    def _():
                        act(index)

                return carry

            lax.fori_loop(1, blocks, step, 0)

        def scatter():
            loop(lambda step: to_owner(step).start(), False)

        def total():
            @pl.when(me < owners)
            def _():
                loop(lambda step: from_all(step).wait_recv(), True)
                landing[me] = region(source, me % owners)[...]

                def add(p, sums):
                    return sums + landing[p].astype(F32)

                sums = lax.fori_loop(0, blocks, add, jnp.zeros(landing.shape[1:], F32))
                region(result, me % owners)[...] = sums.astype(BF16)
                loop(lambda step: to_all(step).start(), True)

        def finish():
            loop(lambda step: from_owner(step).wait_recv(), False)
            loop(lambda step: to_owner(step).wait_send(), False)

            @pl.when(me < owners)
            def _():
                loop(lambda step: to_all(step).wait_send(), True)

        return scatter, total, finish

    early_scatter, early_total, early_finish = small_sum(0, r.early, r.early_land, r.early_out)
    late_scatter, late_total, late_finish = small_sum(1, r.late, r.late_land, r.late_out)

    lax.fori_loop(0, z + 1, ring_drain, 0)

    send_dg.wait_recv()
    blank = jnp.zeros((112, block), F32)
    table = jnp.concatenate([r.dg_trade[0], r.dg_trade[1], blank], axis=0).T
    d_gates = table[:, : 2 * experts]
    gates = r.gates[...]
    d_logits = (gates * (d_gates - jnp.sum(gates * d_gates, axis=1, keepdims=True))).astype(BF16)
    from_router = dot(d_logits, r.router[...])
    send_h2.wait_recv()
    d_h2 = r.trade[0].astype(F32) + r.trade[1].astype(F32) + from_router
    d_x2 = r.g_all[...].astype(F32) + rms_back(r.x2[...], r.moe_gain[...], d_h2)
    d_attn = d_x2.astype(BF16)
    r.acc_h2[...] = d_x2
    d_mid_o = (dot(d_attn, r.o_up[...], NT) * r.mask[:, :SPAN]).astype(BF16)

    d_att = (dot(d_attn, r.ow_all[ep], NT) + dot(d_mid_o, r.od_all[ep])).astype(BF16).astype(F32)
    pad_query(d_att, r.dn)
    pad_query_t(d_att.T, r.dt)
    product = (d_att * r.att[...]).T
    for group in range(4):
        for side in (0, 1):
            first = 128 * group + 64 * side
            r.delta[group, :, side * block : side * block + block] = jnp.sum(
                product[first : first + 64], axis=0, keepdims=True
            )
    r.dqt[...] = jnp.zeros(r.dqt.shape, F32)
    r.early[:32, :] = dot(r.mid_o[...], d_attn, TN).astype(BF16)
    r.early[32:48, :] = fold(dot(d_mid_o, r.att_all[ep], TN)).astype(BF16)
    r.early[48:, :] = jnp.zeros((16, r.early.shape[1]), BF16)
    early_scatter()

    def block_step(number, masked):
        new_k, new_v = [], []
        for group in range(4):
            tile = slice(128 * (group // 2), 128 * (group // 2) + 128)
            keys = r.kvall[number, 0, :, tile]
            s = dot(keys, r.qt[group])
            base = r.lse[group]
            if masked:
                key = number * block + iota(s.shape, 0)
                w = jnp.where((key <= pos_row) & (key >= start_row), jnp.exp(s - base), 0.0)
            else:
                w = jnp.exp(s - jnp.where(start_row <= number * block, base, -LOW))
            d_w = dot(r.kvall[number, 1, :, tile], r.dt[group])
            d_s = (w * (d_w - r.delta[group])).astype(BF16)
            new_k.append(dot(d_s, r.qn[group]))
            new_v.append(dot(w.astype(BF16), r.dn[group]))
            r.dqt[group] += dot(keys, d_s, TN)[HEAD * (group % 2) : HEAD * (group % 2) + HEAD]
        for side in (0, 1):
            tile = slice(128 * side, 128 * side + 128)
            r.kvall[number, 0, :, tile] = ((new_k[2 * side] + new_k[2 * side + 1]) * SCALE).astype(BF16)
            r.kvall[number, 1, :, tile] = (new_v[2 * side] + new_v[2 * side + 1]).astype(BF16)

    def compute(number):
        edge = (number == 0) | (number == me)

        @pl.when(edge)
        def _():
            block_step(number, True)

        @pl.when((number < me) & jnp.logical_not(edge))
        def _():
            block_step(number, False)

        @pl.when(number > me)
        def _():
            r.kvall[number] = jnp.zeros(r.kvall.shape[1:], BF16)

    def to_beside(p, column):
        return remote(
            r.kvall.at[block_of(p, column, 1 - c)], r.from_beside.at[p % kept, column],
            r.beside_send.at[p, column], r.beside_recv.at[p, column], beside,
        )

    def over(p):
        return remote(
            r.kvall.at[block_of(p, 1 - x, c)], r.from_across.at[p % kept], r.across_send.at[p], r.across_recv.at[p], across
        )

    def lower(p):
        return remote(r.kvall.at[block_of(p, x, c)], r.from_up.at[p % kept], r.down_send.at[p], r.down_recv.at[p], down)

    def claim(p, number):
        if planes > kept:

            @pl.when(p >= kept)
            def _():
                pl.semaphore_wait(r.credit.at[number], 1)

    def release(p):
        if planes > kept:

            @pl.when(p + kept <= z)
            def _():
                pl.semaphore_signal(r.credit.at[0], inc=1, device_id=beside, device_id_type=MESH)
                pl.semaphore_signal(r.credit.at[1], inc=1, device_id=across, device_id_type=MESH)

            @pl.when((p + kept <= z) & (z < planes - 1))
            def _():
                pl.semaphore_signal(r.credit.at[2], inc=1, device_id=up, device_id_type=MESH)

    def finish(p):
        number = block_of(p, x, c)
        over(p).wait_recv()
        total = (
            r.kvall[number].astype(F32) + r.from_beside[p % kept, x].astype(F32) + r.from_across[p % kept].astype(F32)
        )
        r.kvall[number] = total.astype(BF16)

        @pl.when(z < planes - 1)
        def _():
            lower(p).wait_recv()
            r.kvall[number] = (total + r.from_up[p % kept].astype(F32)).astype(BF16)

        release(p)

        @pl.when(p < z)
        def _():
            claim(p, 2)
            lower(p).start()

    def plane_back(p, carry):
        @pl.when(p <= z)
        def _():
            compute(block_of(p, 1 - x, 1 - c))
            claim(p, 0)
            to_beside(p, 1 - x).start()
            compute(block_of(p, x, 1 - c))
            to_beside(p, x).start()

            @pl.when(p > 0)
            def _():
                finish(p - 1)

            compute(block_of(p, 1 - x, c))
            to_beside(p, 1 - x).wait_recv()
            number = block_of(p, 1 - x, c)
            r.kvall[number] = (r.kvall[number].astype(F32) + r.from_beside[p % kept, 1 - x].astype(F32)).astype(BF16)
            claim(p, 1)
            over(p).start()
            compute(block_of(p, x, c))
            to_beside(p, x).wait_recv()

        @pl.when(p == 0)
        def _():
            stage_own()

        @pl.when(p == 1)
        def _():
            early_total()

        @pl.when(p == 2)
        def _():
            stage_column()

        @pl.when(p == planes - 1)
        def _():
            stage_core()

        return carry

    lax.fori_loop(0, planes, plane_back, 0)
    finish(z)

    cosine, sine = r.cosine[...], r.sine[...]
    parts = []
    for group in range(4):
        both = r.dqt[group]
        parts += [both[:, :block], both[:, block:]]
    d_query = jnp.concatenate(parts, axis=0).T * SCALE
    d_q = rotate(d_query.astype(BF16).astype(F32), cosine, sine, -1.0).astype(BF16)
    d_k = rotate(r.kvall[me, 0].astype(F32), cosine, sine, -1.0).astype(BF16)
    d_value = r.kvall[me, 1]
    r.mid_trade[ep] = jnp.concatenate(
        [dot(d_q, r.q_up[...], NT), dot(d_k, r.kv_up[0], NT), dot(d_value, r.kv_up[1], NT)], axis=1
    ).astype(BF16)
    send_mid = swap(12, r.mid_trade.at[ep], r.mid_trade.at[ep])
    send_mid.start()
    full = dot(d_q, r.q_w[...], NT) + dot(d_k, r.kv_w[0], NT) + dot(d_value, r.kv_w[1], NT)
    first, second = full[:rows], full[rows:]
    r.norm_trade[0] = jnp.where(ep == 0, second, first).astype(BF16)
    send_norm = swap(13, r.norm_trade.at[0], r.norm_trade.at[1])
    send_norm.start()
    r.late[96:112, :] = fold(dot(r.mids[:, :SPAN], d_q, TN)).astype(BF16)
    r.late[112:, :] = fold(
        jnp.concatenate(
            [dot(r.mids[:, SPAN : 2 * SPAN], d_k, TN), dot(r.mids[:, 2 * SPAN :], d_value, TN)], axis=1
        )
    ).astype(BF16)
    send_mid.wait_recv()
    d_mids = (
        (r.mid_trade[0].astype(F32) + r.mid_trade[1].astype(F32)) * r.mask[:, : 3 * SPAN]
    ).astype(BF16)
    r.late[:96, :] = dot(d_mids, r.h1[...], TN).astype(BF16)
    late_scatter()
    send_out.wait_recv()
    r.block_out[...] = (r.x2[mine, :] + (r.acc_out[mine, :] + r.out_trade[1].astype(F32))).astype(BF16)
    from_mids = dot(d_mids, r.qkv_down[...])
    own = jnp.where(ep == 0, first + from_mids[:rows], second + from_mids[rows:])
    send_norm.wait_recv()
    own = own + r.norm_trade[1].astype(F32)
    r.in_grad[...] = (
        r.acc_h2[mine, :] + rms_back(r.x_all[mine, :].astype(F32), r.attn_gain[...], own)
    ).astype(BF16)
    late_total()
    early_finish()
    stage_end()

    for copy in (send_x, send_ow, send_od, send_hot, send_g, send_dg, send_h2, send_out, send_mid, send_norm):
        copy.wait_send()
    for group in range(4):
        send_att(group).wait_send()

    def drain(p, carry):
        for side in (0, 1):
            to_beside(p, side).wait_send()
        over(p).wait_send()

        @pl.when(p < z)
        def _():
            lower(p).wait_send()

        return carry

    lax.fori_loop(0, z + 1, drain, 0)
    late_finish()


def unpack_kernel(
    final, early, late, block_in, grad_in,
    ein_down, ein_up, eout_down, eout_up, block_out, in_grad, g_down, g_q, g_kv, g_od, g_ou,
):
    for number in range(2):
        part = final[0, 144 * number : 144 * number + 144, :].astype(F32)
        ein_down[number] = part[:64]
        ein_up[number, 0] = part[64:96, :FF]
        ein_up[number, 1] = part[64:96, FF:]
        eout_down[number, :16] = part[96:112, :FF]
        eout_down[number, 16:] = part[96:112, FF:]
        eout_up[number] = part[112:]

    @pl.when(pl.program_id(0) == 0)
    def _():
        block_out[...] = block_in[...]
        in_grad[...] = grad_in[...]
        g_down[...] = late[:96, :].astype(F32)
        g_q[:16, :] = late[96:112, :FF].astype(F32)
        g_q[16:, :] = late[96:112, FF:].astype(F32)
        both = late[112:, :].astype(F32)
        kv = FF // 2
        g_kv[0, :16, :] = both[:, :kv]
        g_kv[1, :16, :] = both[:, kv : 2 * kv]
        g_kv[0, 16:, :] = both[:, 2 * kv : 3 * kv]
        g_kv[1, 16:, :] = both[:, 3 * kv :]
        g_od[:16, :] = early[32:48, :FF].astype(F32)
        g_od[16:, :] = early[32:48, FF:].astype(F32)
        g_ou[...] = early[:32, :].astype(F32)


def per_device(
    resid_in, out_grad, attn_gain, q_weight, key_value_weight, o_weight, moe_gain, router, expert_in,
    expert_out, qkv_down, q_up, key_value_up_factor, o_down, o_up, expert_in_down, expert_in_up,
    expert_out_down, expert_out_up, expert_ids, doc_starts, doc_adapter,
):
    blocks = lax.axis_size("ctx")
    planes = blocks // 4
    rows, width = resid_in.shape
    block = 2 * rows
    heads = q_weight.shape[1]
    kv = key_value_weight.shape[2]
    experts = expert_in.shape[0]
    slots = 4 if planes <= 4 else 2
    kept = planes if planes <= 4 else 2
    piece_rows = -(-288 // (16 * planes)) * 16
    quarter_rows = piece_rows * planes
    early_width = max(128, 4 * width // blocks)
    late_width = max(128, 8 * width // blocks)
    freq = np.tile(np.power(10000.0, -2.0 * np.arange(HEAD // 2) / HEAD).astype(np.float32), 4)[None, :]

    def shape(dims, kind=BF16):
        return jax.ShapeDtypeStruct(dims, kind)

    def dma(*dims):
        return pltpu.SemaphoreType.DMA(dims)

    def low(*dims):
        return pltpu.VMEM(dims, BF16)

    def full(*dims):
        return pltpu.VMEM(dims, F32)

    operands = dict(
        resid=resid_in, grad=out_grad, ids=expert_ids.T, starts=doc_starts, adapters=doc_adapter,
        attn_gain=attn_gain[None, :], moe_gain=moe_gain[None, :], freq=jnp.asarray(freq), qkv_down=qkv_down.T,
        q_up=q_up, kv_up=key_value_up_factor, o_down=o_down.T, o_up=o_up, router=router.T, q_hbm=q_weight,
        kv_hbm=key_value_weight, o_hbm=o_weight, in_hbm=expert_in, out_hbm=expert_out,
        in_down_hbm=jnp.swapaxes(expert_in_down, 1, 2), in_up_hbm=expert_in_up,
        out_down_hbm=jnp.swapaxes(expert_out_down, 1, 2), out_up_hbm=expert_out_up,
    )
    results = dict(
        block_out=shape((rows, width)), in_grad=shape((rows, width)), final=shape((4, quarter_rows, width)),
        early_out=shape((64, width)), late_out=shape((128, width)),
    )
    scratch = dict(
        q_w=low(*q_weight.shape), kv_w=low(*key_value_weight.shape), ow_all=low(2, heads, width),
        od_all=low(2, SPAN, heads), w_in=low(slots, *expert_in.shape[1:]), w_out=low(slots, *expert_out.shape[1:]),
        w_in_down=low(slots, 2 * SPAN, width), w_in_up=low(slots, *expert_in_up.shape[1:]),
        w_out_down=low(slots, SPAN, FF), w_out_up=low(slots, *expert_out_up.shape[1:]),
        x_all=low(block, width), g_all=low(block, width), h1=low(block, width), h2=low(block, width),
        hot_all=low(block, 128), mask=full(block, 128), cosine=full(block, 128), sine=full(block, 128),
        mids=low(block, 3 * SPAN), kvall=low(blocks, 2, block, kv), qt=low(4, 128, 2 * block),
        qn=low(4, 2 * block, 128), dt=low(4, 128, 2 * block), dn=low(4, 2 * block, 128),
        m_s=full(4, 1, 2 * block), l_s=full(4, 1, 2 * block), lse=full(4, 1, 2 * block),
        delta=full(4, 1, 2 * block), acc=full(4, HEAD, 2 * block), dqt=full(4, HEAD, 2 * block),
        att=full(block, heads), att_all=low(2, block, heads), halves=full(2, block, width), half_mid=full(2, block, SPAN), mid_o=low(block, SPAN), x2=full(block, width),
        gates=full(block, 2 * experts), dgates=full(block, 128), trade=low(2, block, width), out_trade=low(2, rows, width),
        norm_trade=low(2, rows, width), mid_trade=low(2, block, 3 * SPAN), dg_trade=full(2, 8, block),
        pack=low(4, quarter_rows, width), core_recv=low(2, quarter_rows, width), x_recv=low(quarter_rows, width),
        z_recv=low(planes, piece_rows, width), early=low(64, width), late=low(128, width),
        early_land=low(blocks, 16, early_width), late_land=low(blocks, 16, late_width),
        from_beside=low(kept, 2, 2, block, kv), from_across=low(kept, 2, block, kv),
        from_up=low(kept, 2, block, kv), credit=pltpu.SemaphoreType.REGULAR((3,)),
        load_sem=dma(3), expert_sem=dma(slots, 6), pair_send=dma(14), pair_recv=dma(14),
        ring_send=dma(3, blocks, 2), ring_recv=dma(blocks, 2), core_send_sem=dma(2), core_recv_sem=dma(2),
        x_sem=dma(2), z_send_sem=dma(2, planes), z_recv_sem=dma(2, planes), last_send=dma(2, 4), last_recv=dma(4),
        small_send=dma(2, 2, blocks), small_recv=dma(2, 2, blocks), beside_send=dma(planes, 2),
        beside_recv=dma(planes, 2), across_send=dma(planes), across_recv=dma(planes), down_send=dma(planes),
        down_recv=dma(planes),
    )
    block_out, in_grad, final, early, late = pl.pallas_call(
        functools.partial(layer_kernel, planes, slots, INPUTS + OUTPUTS + tuple(scratch)),
        out_shape=[results[name] for name in OUTPUTS],
        in_specs=[
            SMEM if name in ("starts", "adapters") else HBM if name.endswith("hbm") else VMEM for name in INPUTS
        ],
        out_specs=[VMEM] * len(OUTPUTS),
        scratch_shapes=list(scratch.values()),
        compiler_params=pltpu.CompilerParams(
            collective_id=1, has_side_effects=True, vmem_limit_bytes=62 << 20
        ),
        name="layer",
    )(*[operands[name] for name in INPUTS])

    def whole(*dims):
        return pl.BlockSpec(dims, lambda step: (0,) * len(dims))

    def two(*dims):
        return pl.BlockSpec((2, *dims), lambda step: (step,) + (0,) * len(dims))

    small = [(96, width), (SPAN, heads), (2, SPAN, kv), (SPAN, heads), (SPAN, width)]
    ein_down, ein_up, eout_down, eout_up, block_out, in_grad, g_down, g_q, g_kv, g_od, g_ou = pl.pallas_call(
        unpack_kernel,
        grid=(4,),
        out_shape=[
            shape((experts, 2 * SPAN, width), F32), shape((experts, 2, SPAN, FF), F32),
            shape((experts, SPAN, FF), F32), shape((experts, SPAN, width), F32),
            shape((rows, width)), shape((rows, width)), *[shape(dims, F32) for dims in small],
        ],
        in_specs=[
            pl.BlockSpec((1, quarter_rows, width), lambda step: (step, 0, 0)), whole(64, width), whole(128, width),
            whole(rows, width), whole(rows, width),
        ],
        out_specs=[
            two(2 * SPAN, width), two(2, SPAN, FF), two(SPAN, FF), two(SPAN, width), whole(rows, width),
            whole(rows, width), *[whole(*dims) for dims in small],
        ],
        compiler_params=pltpu.CompilerParams(vmem_limit_bytes=40 << 20),
        name="unpack",
    )(final, early, late, block_out, in_grad)
    return (
        block_out, in_grad, g_down.T, g_q, g_kv, g_od.T, g_ou, jnp.swapaxes(ein_down, 1, 2), ein_up,
        jnp.swapaxes(eout_down, 1, 2), eout_up,
    )


def solution(mesh):
    placed = (
        P(("ctx", "ep"), None),
        P(("ctx", "ep"), None),
        P(),
        P(None, "ep"),
        P(None, None, "ep"),
        P("ep", None),
        P(),
        P(),
        P("ep", None, None),
        P("ep", None, None),
        P(),
        P(None, "ep"),
        P(None, None, "ep"),
        P("ep", None),
        P(),
        P("ep", None, None),
        P("ep", None, None, None),
        P("ep", None, None),
        P("ep", None, None),
        P(("ctx", "ep"), None),
        P(),
        P(),
    )
    return jax.shard_map(
        per_device,
        mesh=mesh,
        in_specs=placed,
        out_specs=(
            P(("ctx", "ep"), None),
            P(("ctx", "ep"), None),
            P(),
            P(None, "ep"),
            P(None, None, "ep"),
            P("ep", None),
            P(),
            P("ep", None, None),
            P("ep", None, None, None),
            P("ep", None, None),
            P("ep", None, None),
        ),
        check_vma=False,
    )
```

time: 536 us -> 195 us (0.36)
  waiting for transfers between devices: 321 us -> 0 us
  local copies, waits for them, and re-layouts: 24 us -> 5.49 us
  Pallas kernels: 170 us -> 185 us
  between operations: 13.9 us -> 0.96 us
  other arithmetic: 6.5 us -> 0 us
    psum x3 -> x0, waiting for transfers between devices: 320 us -> none  [the longest x2 194 us: per_device(): lax.psum((grads, grad_q_up, grad_kv_up, grad_o_down), 'ctx')]
    pallas_call x3 -> x2, Pallas kernels: 170 us -> 185 us  [the longest x1 182 us: per_device(): pl.pallas_call(functools.partial(layer_kernel, planes, slots, INPUTS + OU...]
    unnamed x28 -> x10, local copies, waits for them, and re-layouts: 19.8 us -> 5.49 us
  transfers between devices with their start and end apart: 3 -> 0, of which waited for: 3 -> 0; matrix products, arithmetic and copies ran while one was open for 2% -> 0% of each run, Pallas kernels for 0% -> 0%
where the time goes in v2:
time: 195 us; the launch traced here: 192 us
  Pallas kernels  185 us (95%)
  local copies, waits for them, and re-layouts  5.49 us (3%)
    pallas_call x1, Pallas kernels, per_device(): pl.pallas_call(functools.partial(layer_kernel, planes, slots, INPUTS + OU...  182 us
    unnamed x10, local copies, waits for them, and re-layouts  5.49 us

profile of v2, /device:TPU:0, one launch (start us, length us, event | category | flops | bytes accessed | tf_op | source)
XLA Modules:
  0.0 191.9 jit_solution(6467495337995433122)
XLA Ops:
  0.7 182.5 %layer.1 = (bf16[128,1024]{1,0:T(8,128)(2,1)}, bf16[128,1024]{1,0:T(8,128)(2,1)}, bf16[4,320,1024]{2,1,0:T(8,128)(2,1)}, bf16[64,1024]{1,0:T(8,128)(2,1)}, bf16[128,1024]{1,0:T(8,128)(2,1)}) custom-call(bf16[128,1024]{1,0:T(8,128)(2,1)} %refs_0_.1, bf16[128,1024]{1,0:T(8,128)(2,1)} %refs_1_.1, s32[8,128]{1,0:T(8,128)} %bitcast.17, s32[8]{0:T(128)} %refs_3_.1, ...), custom_call_target="tpu_custom_call" | custom-call | tf_op jit(solution)/shard_map/layer/pallas_call | solution.py:1021
  183.2 0.0 copy-start
  183.2 1.7 copy-done
  184.9 0.0 copy-start.1
  184.9 0.9 copy-done.1
  185.8 0.0 copy-start.2
  185.8 0.9 copy-done.2
  186.8 0.0 copy-start.3
  186.8 0.9 copy-done.3
  187.7 0.0 copy-start.4
  187.7 0.9 copy-done.4
  188.7 3.0 %unpack.1 = (f32[8,64,1024]{2,1,0:T(8,128)}, f32[8,2,32,512]{3,2,1,0:T(8,128)}, f32[8,32,512]{2,1,0:T(8,128)}, f32[8,32,1024]{2,1,0:T(8,128)}, bf16[128,1024]{1,...) custom-call(bf16[4,320,1024]{2,1,0:T(8,128)(2,1)S(1)} %copy-done, ...), custom_call_target="tpu_custom_call" | custom-call | tf_op jit(solution)/shard_map/unpack/pallas_call | solution.py:1042
Async XLA Ops:
  183.2 1.7 copy-start
  184.9 0.9 copy-start.1
  185.8 0.9 copy-start.2
  186.8 0.9 copy-start.3
  187.7 0.9 copy-start.4

commit v3 on v2

--- a/solution.py
+++ b/solution.py
@@ -137,13 +137,19 @@
     "qkv_down", "q_up", "kv_up", "o_down", "o_up", "router",
     "q_hbm", "kv_hbm", "o_hbm", "in_hbm", "out_hbm", "in_down_hbm", "in_up_hbm", "out_down_hbm", "out_up_hbm",
 )
-OUTPUTS = ("block_out", "in_grad", "final", "early_out", "late_out")
+OUTPUTS = ("out",)
 
 
 def layer_kernel(planes, slots, names, *refs):
     r = dict(zip(names, refs))
     r = type("Refs", (), r)
     r.acc_out, r.acc_h2 = r.halves.at[0], r.halves.at[1]
+    grad_rows = r.pack.shape[2]
+    base = r.in_hbm.shape[0] * grad_rows
+    r.late_out = r.out.at[pl.ds(base, 128)]
+    r.block_out = r.out.at[pl.ds(base + 128, 128)]
+    r.in_grad = r.out.at[pl.ds(base + 256, 128)]
+    r.early_out = r.out.at[pl.ds(base + 384, 64)]
     me, ep, z, x, c = place()
     blocks = 4 * planes
     pair = {"ctx": me, "ep": 1 - ep}
@@ -156,8 +162,9 @@
     mine = span(ep * rows, rows)
     theirs = span(rows - ep * rows, rows)
     experts = r.in_hbm.shape[0]
-    quarter_rows = r.pack.shape[1]
-    piece_rows = quarter_rows // planes
+    groups = 3 if planes >= 12 else 1
+    owners = 4 * groups
+    piece = (grad_rows // groups, r.pack.shape[3] // 4)
     kept = r.from_across.shape[0]
 
     load_q = pltpu.make_async_copy(r.q_hbm, r.q_w, r.load_sem.at[0])
@@ -166,16 +173,19 @@
     load_kv.start()
     load_q.start()
     load_o.start()
+    load_in_down = pltpu.make_async_copy(r.in_down_hbm, r.in_down, r.load_sem.at[3])
+    load_out_up = pltpu.make_async_copy(r.out_up_hbm, r.out_up, r.load_sem.at[4])
+    load_in_down.start()
+    load_out_up.start()
     weights = (
-        (r.in_hbm, r.w_in), (r.out_hbm, r.w_out), (r.in_down_hbm, r.w_in_down),
-        (r.in_up_hbm, r.w_in_up), (r.out_down_hbm, r.w_out_down), (r.out_up_hbm, r.w_out_up),
+        (r.in_hbm, r.w_in), (r.out_hbm, r.w_out), (r.in_up_hbm, r.w_in_up), (r.out_down_hbm, r.w_out_down),
     )
 
     def quarter_at(turn):
         return jnp.where(turn % 2 == 0, 1 - x, x) * 2 + jnp.where(turn < 2, 1 - c, c)
 
     def expert_at(turn):
-        return 2 * quarter_at(turn // 2) + turn % 2
+        return 2 * quarter_at(turn % 4) + turn // 4
 
     def expert_loads(turn):
         e, slot = expert_at(turn), turn % slots
@@ -420,37 +430,173 @@
     r.acc_out[...] = jnp.zeros(r.acc_out.shape, F32)
     r.acc_h2[...] = jnp.zeros(r.acc_h2.shape, F32)
     r.dgates[...] = jnp.zeros(r.dgates.shape, F32)
-    r.pack[:, 288:, :] = jnp.zeros((4, quarter_rows - 288, r.pack.shape[2]), BF16)
+    lanes = 2 * SPAN
+    load_in_down.wait()
+    load_out_up.wait()
     send_g.wait_recv()
-
-    def to_core(column):
+    in_down = r.in_down[...].reshape(experts * lanes, -1)
+    out_up = r.out_up[...].reshape(experts * SPAN, -1)
+    all_mids = dot(h2, in_down, NT)
+    all_lifted = dot(r.g_all[...], out_up, NT)
+    for e in range(experts):
+        r.mid_in[e] = (all_mids[:, lanes * e : lanes * e + lanes] * r.mask[:, :lanes]).astype(BF16)
+        r.lifted[e] = (all_lifted[:, SPAN * e : SPAN * e + SPAN] * r.mask[:, :SPAN]).astype(BF16)
+
+    quarter = 2 * x + c
+
+    def to_core(half, column):
         return remote(
-            r.pack.at[2 * column + 1 - c], r.core_recv.at[column],
-            r.core_send_sem.at[column], r.core_recv_sem.at[column], beside,
-        )
-
-    to_column = remote(r.pack.at[2 * (1 - x) + c], r.x_recv, r.x_sem.at[0], r.x_sem.at[1], across)
-    quarter = 2 * x + c
+            r.pack.at[half, 2 * column + 1 - c], r.core_land.at[half, column],
+            r.core_send.at[half, column], r.core_recv.at[half, column], beside,
+        )
+
+    def to_column(half):
+        return remote(
+            r.pack.at[half, 2 * (1 - x) + c], r.x_land.at[half], r.x_send.at[half], r.x_recv.at[half], across
+        )
+
+    def add_core(half, column):
+        to_core(half, column).wait_recv()
+        number = 2 * column + c
+        r.pack[half, number] = (
+            r.pack[half, number].astype(F32) + r.core_land[half, column].astype(F32)
+        ).astype(BF16)
+
+    def final_rows(half, number):
+        return (2 * number + half) * grad_rows
+
+    def piece_of(owner):
+        return (
+            pl.multiple_of(owner // 4 * piece[0], piece[0]),
+            pl.multiple_of(owner % 4 * piece[1], piece[1]),
+        )
+
+    def piece_in_pack(half, owner):
+        row, lane = piece_of(owner)
+        return r.pack.at[half, quarter, pl.ds(row, piece[0]), pl.ds(lane, piece[1])]
+
+    def piece_in_final(half, owner):
+        row, lane = piece_of(owner)
+        start = pl.multiple_of(final_rows(half, quarter) + row, 16)
+        return r.out.at[pl.ds(start, piece[0]), pl.ds(lane, piece[1])]
+
+    def plane_of(step):
+        return lax.rem(z + step, planes)
+
+    def give(half, step):
+        other = plane_of(step)
+        return remote(
+            piece_in_pack(half, other), r.z_land.at[half, z], r.z_send.at[half, 0, other],
+            r.z_recv.at[half, 0, z], {"ctx": block_of(other, x, c), "ep": ep},
+        )
+
+    def take(half, step):
+        other = plane_of(step)
+        return remote(
+            piece_in_pack(half, 0), r.z_land.at[half, other], r.z_send.at[half, 0, other],
+            r.z_recv.at[half, 0, other], {"ctx": block_of(other, x, c), "ep": ep},
+        )
+
+    def spread(half, step):
+        other = plane_of(step)
+        part = piece_in_final(half, z % owners)
+        return remote(
+            part, part, r.z_send.at[half, 1, other], r.z_recv.at[half, 1, z],
+            {"ctx": block_of(other, x, c), "ep": ep},
+        )
+
+    def gather(half, step):
+        other = plane_of(step)
+        part = piece_in_final(half, other)
+        return remote(
+            part, part, r.z_send.at[half, 1, other], r.z_recv.at[half, 1, other],
+            {"ctx": block_of(other, x, c), "ep": ep},
+        )
+
+    def each_plane(act, among_owners):
+        def step(number, carry):
+            if among_owners and owners < planes:
+
+                @pl.when(plane_of(number) < owners)
+                def _():
+                    act(number)
+
+            else:
+                act(number)
+            return carry
+
+        lax.fori_loop(1, planes, step, 0)
+
+    def if_owner(act):
+        if owners < planes:
+            pl.when(z < owners)(act)
+        else:
+            act()
+
+    def over_final(half, number, way, target):
+        part = r.out.at[pl.ds(pl.multiple_of(final_rows(half, number), 16), grad_rows)]
+        return remote(part, part, r.last_send.at[half, way, number], r.last_recv.at[half, number], target)
+
+    def stage_pieces(half):
+        to_column(half).wait_recv()
+        r.pack[half, quarter] = (
+            r.pack[half, quarter].astype(F32) + r.x_land[half].astype(F32)
+        ).astype(BF16)
+        each_plane(lambda step: give(half, step).start(), True)
+
+    def stage_own(half):
+        def act():
+            each_plane(lambda step: take(half, step).wait_recv(), False)
+            r.z_land[half, z] = piece_in_pack(half, z % owners)[...]
+
+            def add(p, total):
+                return total + r.z_land[half, p].astype(F32)
+
+            total = lax.fori_loop(0, planes, add, jnp.zeros(piece, F32))
+            piece_in_final(half, z % owners)[...] = total.astype(BF16)
+            each_plane(lambda step: spread(half, step).start(), False)
+
+        if_owner(act)
+
+    def stage_column(half):
+        each_plane(lambda step: gather(half, step).wait_recv(), True)
+        over_final(half, quarter, 0, across).start()
+        over_final(half, quarter, 1, beside).start()
+
+    def stage_core(half):
+        over_final(half, 2 * (1 - x) + c, 0, across).wait_recv()
+        over_final(half, 2 * (1 - x) + c, 1, beside).start()
+
+    def stage_end(half):
+        over_final(half, 2 * x + 1 - c, 1, beside).wait_recv()
+        over_final(half, 2 * (1 - x) + 1 - c, 1, beside).wait_recv()
+        each_plane(lambda step: give(half, step).wait_send(), True)
+        if_owner(lambda: each_plane(lambda step: spread(half, step).wait_send(), False))
+        over_final(half, quarter, 0, across).wait_send()
+        over_final(half, quarter, 1, beside).wait_send()
+        over_final(half, 2 * (1 - x) + c, 1, beside).wait_send()
+        to_core(half, 0).wait_send()
+        to_core(half, 1).wait_send()
+        to_column(half).wait_send()
 
     def one(turn, carry):
         slot = turn % slots
         e = expert_at(turn)
+        half, q = turn // 4, quarter_at(turn % 4)
         for copy in expert_loads(turn):
             copy.wait()
         h2, g = r.h2[...], r.g_all[...]
-        mask = r.mask[...]
         gate = jnp.sum(
             jnp.where(iota((block, 2 * experts), 1) == e + ep * experts, r.gates[...], 0.0), axis=1, keepdims=True
         )
-        mid_in = (dot(h2, r.w_in_down[slot], NT) * mask[:, : 2 * SPAN]).astype(BF16)
+        mid_in, lifted = r.mid_in[e], r.lifted[e]
         gate_part = dot(h2, r.w_in[slot, :, :FF]) + dot(mid_in[:, :SPAN], r.w_in_up[slot, 0])
         up_part = dot(h2, r.w_in[slot, :, FF:]) + dot(mid_in[:, SPAN:], r.w_in_up[slot, 1])
+        d_act = dot(g, r.w_out[slot], NT) + dot(lifted, r.w_out_down[slot])
         squash = 1.0 / (1.0 + jnp.exp(-gate_part))
         silu = gate_part * squash
         act = (silu * up_part).astype(BF16)
-        mid_out = dot(act, r.w_out_down[slot], NT) * mask[:, :SPAN]
-        lifted = (dot(g, r.w_out_up[slot], NT) * mask[:, :SPAN]).astype(BF16)
-        d_act = dot(g, r.w_out[slot], NT) + dot(lifted, r.w_out_down[slot])
+        mid_out = dot(act, r.w_out_down[slot], NT) * r.mask[:, :SPAN]
         d_gate = jnp.sum(act.astype(F32) * d_act, axis=1, keepdims=True)
         r.dgates[...] += jnp.where(iota(r.dgates.shape, 1) == e, d_gate, 0.0)
         d_act = d_act * gate
@@ -458,61 +604,52 @@
         d_gp = (d_act * up_part * squash * (1.0 + gate_part * (1.0 - squash))).astype(BF16)
         d_mid_in = (
             jnp.concatenate([dot(d_gp, r.w_in_up[slot, 0], NT), dot(d_up, r.w_in_up[slot, 1], NT)], axis=1)
-            * mask[:, : 2 * SPAN]
+            * r.mask[:, :lanes]
         ).astype(BF16)
         scaled_mid = (mid_out * gate).astype(BF16)
-        r.acc_out[...] += dot((act.astype(F32) * gate).astype(BF16), r.w_out[slot]) + dot(
-            scaled_mid, r.w_out_up[slot]
-        )
-        r.acc_h2[...] += (
-            dot(d_gp, r.w_in[slot, :, :FF], NT)
-            + dot(d_up, r.w_in[slot, :, FF:], NT)
-            + dot(d_mid_in, r.w_in_down[slot])
-        )
-        q = quarter_at(turn // 2)
-        first = 144 * (turn % 2)
-
-        def at(offset, count):
-            return pl.ds(pl.multiple_of(first + offset, 16), count)
-
-        r.pack[q, at(0, 64), :] = dot(d_mid_in, h2, TN).astype(BF16)
-        r.pack[q, at(64, 32), :FF] = dot(mid_in[:, :SPAN], d_gp, TN).astype(BF16)
-        r.pack[q, at(64, 32), FF:] = dot(mid_in[:, SPAN:], d_up, TN).astype(BF16)
-        r.pack[q, at(96, 16), :] = fold(
+        r.d_mid_in[e] = d_mid_in
+        r.mid_out[e] = scaled_mid
+        r.acc_out[...] += dot((act.astype(F32) * gate).astype(BF16), r.w_out[slot])
+        r.acc_h2[...] += dot(d_gp, r.w_in[slot, :, :FF], NT) + dot(d_up, r.w_in[slot, :, FF:], NT)
+        r.pack[half, q, :64, :] = dot(d_mid_in, h2, TN).astype(BF16)
+        r.pack[half, q, 64:96, :FF] = dot(mid_in[:, :SPAN], d_gp, TN).astype(BF16)
+        r.pack[half, q, 64:96, FF:] = dot(mid_in[:, SPAN:], d_up, TN).astype(BF16)
+        r.pack[half, q, 96:112, :] = fold(
             dot((lifted.astype(F32) * gate).astype(BF16), act, TN)
         ).astype(BF16)
-        r.pack[q, at(112, 32), :] = dot(scaled_mid, g, TN).astype(BF16)
+        r.pack[half, q, 112:, :] = dot(scaled_mid, g, TN).astype(BF16)
 
         @pl.when(turn + slots < experts)
         def _():
             for copy in expert_loads(turn + slots):
                 copy.start()
 
-        @pl.when(turn == 1)
-        def _():
-            to_core(1 - x).start()
-
-        @pl.when(turn == 3)
-        def _():
-            to_core(x).start()
-
-        def add_core(column):
-            to_core(column).wait_recv()
-            number = 2 * column + c
-            r.pack[number] = (r.pack[number].astype(F32) + r.core_recv[column].astype(F32)).astype(BF16)
+        @pl.when(turn % 4 == 0)
+        def _():
+            to_core(half, 1 - x).start()
+
+        @pl.when(turn % 4 == 1)
+        def _():
+            to_core(half, x).start()
+
+        @pl.when(turn % 4 == 2)
+        def _():
+            add_core(half, 1 - x)
+            to_column(half).start()
+
+        @pl.when(turn % 4 == 3)
+        def _():
+            add_core(half, x)
 
         @pl.when(turn == 5)
         def _():
-            add_core(1 - x)
-            to_column.start()
-
-        @pl.when(turn == 7)
-        def _():
-            add_core(x)
+            stage_pieces(0)
 
         return carry
 
     lax.fori_loop(0, experts, one, 0)
+    every = range(experts)
+    r.acc_h2[...] += dot(jnp.concatenate([r.d_mid_in[e] for e in every], axis=1), r.in_down[...].reshape(experts * lanes, -1))
 
     r.dg_trade[ep] = r.dgates[...].T[:8]
     send_dg = swap(9, r.dg_trade.at[ep], r.dg_trade.at[ep])
@@ -520,94 +657,18 @@
     r.trade[ep] = r.acc_h2[...].astype(BF16)
     send_h2 = swap(10, r.trade.at[ep], r.trade.at[ep])
     send_h2.start()
+    r.acc_out[...] += dot(jnp.concatenate([r.mid_out[e] for e in every], axis=1), r.out_up[...].reshape(experts * SPAN, -1))
     r.out_trade[0] = r.acc_out[theirs, :].astype(BF16)
     send_out = swap(11, r.out_trade.at[0], r.out_trade.at[1])
     send_out.start()
-
-    to_column.wait_recv()
-    r.pack[quarter] = (r.pack[quarter].astype(F32) + r.x_recv[...].astype(F32)).astype(BF16)
-
-    def plane_of(step):
-        return lax.rem(z + step, planes)
-
-    def give(step):
-        other = plane_of(step)
-        return remote(
-            r.pack.at[quarter, span(other * piece_rows, piece_rows), :], r.z_recv.at[z],
-            r.z_send_sem.at[0, other], r.z_recv_sem.at[0, z], {"ctx": block_of(other, x, c), "ep": ep},
-        )
-
-    def take(step):
-        other = plane_of(step)
-        return remote(
-            r.pack.at[quarter, span(other * piece_rows, piece_rows), :], r.z_recv.at[other],
-            r.z_send_sem.at[0, other], r.z_recv_sem.at[0, other], {"ctx": block_of(other, x, c), "ep": ep},
-        )
-
-    def spread(step):
-        other = plane_of(step)
-        part = r.final.at[quarter, span(z * piece_rows, piece_rows), :]
-        return remote(
-            part, part, r.z_send_sem.at[1, other], r.z_recv_sem.at[1, z], {"ctx": block_of(other, x, c), "ep": ep}
-        )
-
-    def gather(step):
-        other = plane_of(step)
-        part = r.final.at[quarter, span(other * piece_rows, piece_rows), :]
-        return remote(
-            part, part, r.z_send_sem.at[1, other], r.z_recv_sem.at[1, other], {"ctx": block_of(other, x, c), "ep": ep}
-        )
-
-    def each_plane(act):
-        def step(number, carry):
-            act(number)
-            return carry
-
-        lax.fori_loop(1, planes, step, 0)
-
-    each_plane(lambda step: give(step).start())
-
-    def stage_own():
-        each_plane(lambda step: take(step).wait_recv())
-        r.z_recv[z] = r.pack[quarter, span(z * piece_rows, piece_rows), :]
-
-        def add(p, total):
-            return total + r.z_recv[p].astype(F32)
-
-        total = lax.fori_loop(0, planes, add, jnp.zeros(r.z_recv.shape[1:], F32))
-        r.final[quarter, span(z * piece_rows, piece_rows), :] = total.astype(BF16)
-        each_plane(lambda step: spread(step).start())
-
-    def over_final(number, way, target):
-        part = r.final.at[number]
-        return remote(part, part, r.last_send.at[way, number], r.last_recv.at[number], target)
-
-    def stage_column():
-        each_plane(lambda step: gather(step).wait_recv())
-        over_final(quarter, 0, across).start()
-        over_final(quarter, 1, beside).start()
-
-    def stage_core():
-        over_final(2 * (1 - x) + c, 0, across).wait_recv()
-        over_final(2 * (1 - x) + c, 1, beside).start()
-
-    def stage_end():
-        over_final(2 * x + 1 - c, 1, beside).wait_recv()
-        over_final(2 * (1 - x) + 1 - c, 1, beside).wait_recv()
-        each_plane(lambda step: give(step).wait_send())
-        each_plane(lambda step: spread(step).wait_send())
-        over_final(quarter, 0, across).wait_send()
-        over_final(quarter, 1, beside).wait_send()
-        over_final(2 * (1 - x) + c, 1, beside).wait_send()
-        to_core(0).wait_send()
-        to_core(1).wait_send()
-        to_column.wait_send()
+    stage_own(0)
+    stage_pieces(1)
 
     def small_sum(number, source, landing, result):
         tiles = source.shape[0] // 16
         width = landing.shape[2]
         each = source.shape[1] // width
-        owners = tiles * each
+        holders = tiles * each
 
         def region(ref, owner):
             return ref.at[span(owner // each * 16, 16), span(owner % each * width, width)]
@@ -625,13 +686,13 @@
         def from_all(step):
             device = other(step)
             return remote(
-                region(source, me % owners), landing.at[device], r.small_send.at[number, 0, device],
+                region(source, me % holders), landing.at[device], r.small_send.at[number, 0, device],
                 r.small_recv.at[number, 0, device], {"ctx": device, "ep": ep},
             )
 
         def to_all(step):
             device = other(step)
-            part = region(result, me % owners)
+            part = region(result, me % holders)
             return remote(
                 part, part, r.small_send.at[number, 1, device], r.small_recv.at[number, 1, me],
                 {"ctx": device, "ep": ep},
@@ -651,7 +712,7 @@
                     act(index)
                 else:
 
-                    @pl.when(other(index) < owners)
+                    @pl.when(other(index) < holders)
                     def _():
                         act(index)
 
@@ -663,23 +724,23 @@
             loop(lambda step: to_owner(step).start(), False)
 
         def total():
-            @pl.when(me < owners)
+            @pl.when(me < holders)
             def _():
                 loop(lambda step: from_all(step).wait_recv(), True)
-                landing[me] = region(source, me % owners)[...]
+                landing[me] = region(source, me % holders)[...]
 
                 def add(p, sums):
                     return sums + landing[p].astype(F32)
 
                 sums = lax.fori_loop(0, blocks, add, jnp.zeros(landing.shape[1:], F32))
-                region(result, me % owners)[...] = sums.astype(BF16)
+                region(result, me % holders)[...] = sums.astype(BF16)
                 loop(lambda step: to_all(step).start(), True)
 
         def finish():
             loop(lambda step: from_owner(step).wait_recv(), False)
             loop(lambda step: to_owner(step).wait_send(), False)
 
-            @pl.when(me < owners)
+            @pl.when(me < holders)
             def _():
                 loop(lambda step: to_all(step).wait_send(), True)
 
@@ -697,6 +758,7 @@
     gates = r.gates[...]
     d_logits = (gates * (d_gates - jnp.sum(gates * d_gates, axis=1, keepdims=True))).astype(BF16)
     from_router = dot(d_logits, r.router[...])
+    stage_column(0)
     send_h2.wait_recv()
     d_h2 = r.trade[0].astype(F32) + r.trade[1].astype(F32) + from_router
     d_x2 = r.g_all[...].astype(F32) + rms_back(r.x2[...], r.moe_gain[...], d_h2)
@@ -719,6 +781,7 @@
     r.early[32:48, :] = fold(dot(d_mid_o, r.att_all[ep], TN)).astype(BF16)
     r.early[48:, :] = jnp.zeros((16, r.early.shape[1]), BF16)
     early_scatter()
+    stage_own(1)
 
     def block_step(number, masked):
         new_k, new_v = [], []
@@ -816,25 +879,26 @@
             compute(block_of(p, 1 - x, 1 - c))
             claim(p, 0)
             to_beside(p, 1 - x).start()
-            compute(block_of(p, x, 1 - c))
-            to_beside(p, x).start()
-
-            @pl.when(p > 0)
-            def _():
-                finish(p - 1)
-
             compute(block_of(p, 1 - x, c))
             to_beside(p, 1 - x).wait_recv()
             number = block_of(p, 1 - x, c)
             r.kvall[number] = (r.kvall[number].astype(F32) + r.from_beside[p % kept, 1 - x].astype(F32)).astype(BF16)
             claim(p, 1)
             over(p).start()
+            compute(block_of(p, x, 1 - c))
+            to_beside(p, x).start()
+
+            @pl.when(p > 0)
+            def _():
+                finish(p - 1)
+
             compute(block_of(p, x, c))
             to_beside(p, x).wait_recv()
 
         @pl.when(p == 0)
         def _():
-            stage_own()
+            stage_column(1)
+            stage_core(0)
 
         @pl.when(p == 1)
         def _():
@@ -842,11 +906,7 @@
 
         @pl.when(p == 2)
         def _():
-            stage_column()
-
-        @pl.when(p == planes - 1)
-        def _():
-            stage_core()
+            stage_core(1)
 
         return carry
 
@@ -895,7 +955,8 @@
     ).astype(BF16)
     late_total()
     early_finish()
-    stage_end()
+    stage_end(0)
+    stage_end(1)
 
     for copy in (send_x, send_ow, send_od, send_hot, send_g, send_dg, send_h2, send_out, send_mid, send_norm):
         copy.wait_send()
@@ -917,35 +978,71 @@
     late_finish()
 
 
-def unpack_kernel(
-    final, early, late, block_in, grad_in,
-    ein_down, ein_up, eout_down, eout_up, block_out, in_grad, g_down, g_q, g_kv, g_od, g_ou,
-):
-    for number in range(2):
-        part = final[0, 144 * number : 144 * number + 144, :].astype(F32)
-        ein_down[number] = part[:64]
-        ein_up[number, 0] = part[64:96, :FF]
-        ein_up[number, 1] = part[64:96, FF:]
-        eout_down[number, :16] = part[96:112, :FF]
-        eout_down[number, 16:] = part[96:112, FF:]
-        eout_up[number] = part[112:]
-
-    @pl.when(pl.program_id(0) == 0)
-    def _():
-        block_out[...] = block_in[...]
-        in_grad[...] = grad_in[...]
-        g_down[...] = late[:96, :].astype(F32)
-        g_q[:16, :] = late[96:112, :FF].astype(F32)
-        g_q[16:, :] = late[96:112, FF:].astype(F32)
-        both = late[112:, :].astype(F32)
-        kv = FF // 2
-        g_kv[0, :16, :] = both[:, :kv]
-        g_kv[1, :16, :] = both[:, kv : 2 * kv]
-        g_kv[0, 16:, :] = both[:, 2 * kv : 3 * kv]
-        g_kv[1, 16:, :] = both[:, 3 * kv :]
-        g_od[:16, :] = early[32:48, :FF].astype(F32)
-        g_od[16:, :] = early[32:48, FF:].astype(F32)
-        g_ou[...] = early[:32, :].astype(F32)
+RESULTS = (
+    "ein_down", "ein_up", "eout_down", "eout_up", "block_out", "in_grad", "g_down", "g_q", "g_kv", "g_od", "g_ou",
+)
+
+
+def unpack_kernel(packed, *refs):
+    count = len(RESULTS)
+    outs = dict(zip(RESULTS, refs[:count]))
+    held = dict(zip(RESULTS, refs[count : 2 * count]))
+    rows, sem_in, sem_out = refs[2 * count :]
+    experts = outs["ein_down"].shape[0]
+    grad_rows = 144
+    base = experts * grad_rows
+
+    def fetch(start, size, number):
+        return pltpu.make_async_copy(
+            packed.at[pl.ds(start, size)], rows.at[pl.ds(start, size)], sem_in.at[number]
+        )
+
+    fetches = [fetch(grad_rows * e, grad_rows, e) for e in range(experts)]
+    fetches.append(fetch(base, rows.shape[0] - base, experts))
+    for copy in fetches:
+        copy.start()
+    stores = []
+
+    def store(name, number):
+        copy = pltpu.make_async_copy(
+            held[name] if number is None else held[name].at[number],
+            outs[name] if number is None else outs[name].at[number],
+            sem_out.at[len(stores)],
+        )
+        copy.start()
+        stores.append(copy)
+
+    for e in range(experts):
+        fetches[e].wait()
+        part = rows[grad_rows * e : grad_rows * e + grad_rows, :].astype(F32)
+        held["ein_down"][e] = part[:64]
+        held["ein_up"][e, 0] = part[64:96, :FF]
+        held["ein_up"][e, 1] = part[64:96, FF:]
+        held["eout_down"][e, :16] = part[96:112, :FF]
+        held["eout_down"][e, 16:] = part[96:112, FF:]
+        held["eout_up"][e] = part[112:]
+        for name in RESULTS[:4]:
+            store(name, e)
+    fetches[experts].wait()
+    late = rows[base : base + 128, :].astype(F32)
+    early = rows[base + 384 : base + 448, :].astype(F32)
+    held["block_out"][...] = rows[base + 128 : base + 256, :]
+    held["in_grad"][...] = rows[base + 256 : base + 384, :]
+    held["g_down"][...] = late[:96]
+    held["g_q"][:16, :] = late[96:112, :FF]
+    held["g_q"][16:, :] = late[96:112, FF:]
+    kv = FF // 2
+    for side in (0, 1):
+        for half in (0, 1):
+            first = kv * (2 * half + side)
+            held["g_kv"][side, 16 * half : 16 * half + 16, :] = late[112:, first : first + kv]
+    held["g_od"][:16, :] = early[32:48, :FF]
+    held["g_od"][16:, :] = early[32:48, FF:]
+    held["g_ou"][...] = early[:32]
+    for name in RESULTS[4:]:
+        store(name, None)
+    for copy in stores:
+        copy.wait()
 
 
 def per_device(
@@ -962,8 +1059,10 @@
     experts = expert_in.shape[0]
     slots = 4 if planes <= 4 else 2
     kept = planes if planes <= 4 else 2
-    piece_rows = -(-288 // (16 * planes)) * 16
-    quarter_rows = piece_rows * planes
+    grad_rows = 2 * SPAN + SPAN + SPAN // 2 + SPAN
+    base = experts * grad_rows
+    groups = 3 if planes >= 12 else 1
+    piece = (grad_rows // groups, width // 4)
     early_width = max(128, 4 * width // blocks)
     late_width = max(128, 8 * width // blocks)
     freq = np.tile(np.power(10000.0, -2.0 * np.arange(HEAD // 2) / HEAD).astype(np.float32), 4)[None, :]
@@ -988,15 +1087,14 @@
         in_down_hbm=jnp.swapaxes(expert_in_down, 1, 2), in_up_hbm=expert_in_up,
         out_down_hbm=jnp.swapaxes(expert_out_down, 1, 2), out_up_hbm=expert_out_up,
     )
-    results = dict(
-        block_out=shape((rows, width)), in_grad=shape((rows, width)), final=shape((4, quarter_rows, width)),
-        early_out=shape((64, width)), late_out=shape((128, width)),
-    )
+    results = dict(out=shape((base + 448, width)))
     scratch = dict(
         q_w=low(*q_weight.shape), kv_w=low(*key_value_weight.shape), ow_all=low(2, heads, width),
         od_all=low(2, SPAN, heads), w_in=low(slots, *expert_in.shape[1:]), w_out=low(slots, *expert_out.shape[1:]),
-        w_in_down=low(slots, 2 * SPAN, width), w_in_up=low(slots, *expert_in_up.shape[1:]),
-        w_out_down=low(slots, SPAN, FF), w_out_up=low(slots, *expert_out_up.shape[1:]),
+        in_down=low(experts, 2 * SPAN, width), w_in_up=low(slots, *expert_in_up.shape[1:]),
+        w_out_down=low(slots, SPAN, FF), out_up=low(experts, SPAN, width),
+        mid_in=low(experts, block, 2 * SPAN), lifted=low(experts, block, SPAN),
+        d_mid_in=low(experts, block, 2 * SPAN), mid_out=low(experts, block, SPAN),
         x_all=low(block, width), g_all=low(block, width), h1=low(block, width), h2=low(block, width),
         hot_all=low(block, 128), mask=full(block, 128), cosine=full(block, 128), sine=full(block, 128),
         mids=low(block, 3 * SPAN), kvall=low(blocks, 2, block, kv), qt=low(4, 128, 2 * block),
@@ -1006,19 +1104,20 @@
         att=full(block, heads), att_all=low(2, block, heads), halves=full(2, block, width), half_mid=full(2, block, SPAN), mid_o=low(block, SPAN), x2=full(block, width),
         gates=full(block, 2 * experts), dgates=full(block, 128), trade=low(2, block, width), out_trade=low(2, rows, width),
         norm_trade=low(2, rows, width), mid_trade=low(2, block, 3 * SPAN), dg_trade=full(2, 8, block),
-        pack=low(4, quarter_rows, width), core_recv=low(2, quarter_rows, width), x_recv=low(quarter_rows, width),
-        z_recv=low(planes, piece_rows, width), early=low(64, width), late=low(128, width),
+        pack=low(2, 4, grad_rows, width), core_land=low(2, 2, grad_rows, width), x_land=low(2, grad_rows, width),
+        z_land=low(2, planes, *piece), early=low(64, width), late=low(128, width),
         early_land=low(blocks, 16, early_width), late_land=low(blocks, 16, late_width),
         from_beside=low(kept, 2, 2, block, kv), from_across=low(kept, 2, block, kv),
         from_up=low(kept, 2, block, kv), credit=pltpu.SemaphoreType.REGULAR((3,)),
-        load_sem=dma(3), expert_sem=dma(slots, 6), pair_send=dma(14), pair_recv=dma(14),
-        ring_send=dma(3, blocks, 2), ring_recv=dma(blocks, 2), core_send_sem=dma(2), core_recv_sem=dma(2),
-        x_sem=dma(2), z_send_sem=dma(2, planes), z_recv_sem=dma(2, planes), last_send=dma(2, 4), last_recv=dma(4),
+        load_sem=dma(5), expert_sem=dma(slots, 4), pair_send=dma(14), pair_recv=dma(14),
+        ring_send=dma(3, blocks, 2), ring_recv=dma(blocks, 2), core_send=dma(2, 2), core_recv=dma(2, 2),
+        x_send=dma(2), x_recv=dma(2), z_send=dma(2, 2, planes), z_recv=dma(2, 2, planes), last_send=dma(2, 2, 4),
+        last_recv=dma(2, 4),
         small_send=dma(2, 2, blocks), small_recv=dma(2, 2, blocks), beside_send=dma(planes, 2),
         beside_recv=dma(planes, 2), across_send=dma(planes), across_recv=dma(planes), down_send=dma(planes),
         down_recv=dma(planes),
     )
-    block_out, in_grad, final, early, late = pl.pallas_call(
+    (out,) = pl.pallas_call(
         functools.partial(layer_kernel, planes, slots, INPUTS + OUTPUTS + tuple(scratch)),
         out_shape=[results[name] for name in OUTPUTS],
         in_specs=[
@@ -1032,32 +1131,25 @@
         name="layer",
     )(*[operands[name] for name in INPUTS])
 
-    def whole(*dims):
-        return pl.BlockSpec(dims, lambda step: (0,) * len(dims))
-
-    def two(*dims):
-        return pl.BlockSpec((2, *dims), lambda step: (step,) + (0,) * len(dims))
-
-    small = [(96, width), (SPAN, heads), (2, SPAN, kv), (SPAN, heads), (SPAN, width)]
+    unpacked = dict(
+        ein_down=shape((experts, 2 * SPAN, width), F32), ein_up=shape((experts, 2, SPAN, FF), F32),
+        eout_down=shape((experts, SPAN, FF), F32), eout_up=shape((experts, SPAN, width), F32),
+        block_out=shape((rows, width)), in_grad=shape((rows, width)), g_down=shape((3 * SPAN, width), F32),
+        g_q=shape((SPAN, heads), F32), g_kv=shape((2, SPAN, kv), F32), g_od=shape((SPAN, heads), F32),
+        g_ou=shape((SPAN, width), F32),
+    )
     ein_down, ein_up, eout_down, eout_up, block_out, in_grad, g_down, g_q, g_kv, g_od, g_ou = pl.pallas_call(
         unpack_kernel,
-        grid=(4,),
-        out_shape=[
-            shape((experts, 2 * SPAN, width), F32), shape((experts, 2, SPAN, FF), F32),
-            shape((experts, SPAN, FF), F32), shape((experts, SPAN, width), F32),
-            shape((rows, width)), shape((rows, width)), *[shape(dims, F32) for dims in small],
+        out_shape=[unpacked[name] for name in RESULTS],
+        in_specs=[HBM],
+        out_specs=[HBM] * len(RESULTS),
+        scratch_shapes=[
+            *[pltpu.VMEM(unpacked[name].shape, unpacked[name].dtype) for name in RESULTS],
+            pltpu.VMEM(out.shape, BF16), dma(experts + 1), dma(4 * experts + 7),
         ],
-        in_specs=[
-            pl.BlockSpec((1, quarter_rows, width), lambda step: (step, 0, 0)), whole(64, width), whole(128, width),
-            whole(rows, width), whole(rows, width),
-        ],
-        out_specs=[
-            two(2 * SPAN, width), two(2, SPAN, FF), two(SPAN, FF), two(SPAN, width), whole(rows, width),
-            whole(rows, width), *[whole(*dims) for dims in small],
-        ],
-        compiler_params=pltpu.CompilerParams(vmem_limit_bytes=40 << 20),
+        compiler_params=pltpu.CompilerParams(vmem_limit_bytes=62 << 20),
         name="unpack",
-    )(final, early, late, block_out, in_grad)
+    )(out)
     return (
         block_out, in_grad, g_down.T, g_q, g_kv, g_od.T, g_ou, jnp.swapaxes(ein_down, 1, 2), ein_up,
         jnp.swapaxes(eout_down, 1, 2), eout_up,

time: 195 us -> 165 us (0.85)
  the two profiles are of different devices: /device:TPU:0 before, /device:TPU:29 now
where the time goes in v3:
time: 165 us; the launch traced here: 163 us
  Pallas kernels  162 us (98%)
    pallas_call x1, Pallas kernels, per_device(): pl.pallas_call(functools.partial(layer_kernel, planes, slots, INPUTS + OU...  158 us
    pallas_call x1, Pallas kernels, per_device(): pl.pallas_call(unpack_kernel, out_shape=[unpacked[name] for name in RESUL...  3.93 us

profile of v3, /device:TPU:29, one launch (start us, length us, event | category | flops | bytes accessed | tf_op | source)
XLA Modules:
  0.0 162.9 jit_solution(12375366524702645082)
XLA Ops:
  0.7 158.0 %layer.1.packed = bf16[1600,1024]{1,0:T(8,128)(2,1)} custom-call(bf16[128,1024]{1,0:T(8,128)(2,1)} %refs_0_.1, bf16[128,1024]{1,0:T(8,128)(2,1)} %refs_1_.1, s32[8,128]{1,0:T(8,128)} %bitcast.17, s32[8]{0:T(128)} %refs_3_.1, s32[8]{0:T(128)} %refs_4_.1, f32[1,1024]{1,0:T(1,128)} %bitcast.18, f32[1,1024]{1,0:T(1,128)} %bitcast.19, ...), custom_call_target="tpu_custom_call" | custom-call | tf_op jit(solution)/shard_map/layer/pallas_call | solution.py:1120
  158.6 3.9 %unpack.1 = (f32[8,64,1024]{2,1,0:T(8,128)}, f32[8,2,32,512]{3,2,1,0:T(8,128)}, f32[8,32,512]{2,1,0:T(8,128)}, f32[8,32,1024]{2,1,0:T(8,128)}, bf16[128,1024]{1,...) custom-call(bf16[1600,1024]{1,0:T(8,128)(2,1)} %layer.1.packed), custom_call_target="tpu_custom_call" | custom-call | tf_op jit(solution)/shard_map/unpack/pallas_call | solution.py:1141

commit v4 on v3

--- a/solution.py
+++ b/solution.py
@@ -100,31 +100,22 @@
     return pl.ds(pl.multiple_of(start, count), count)
 
 
-def pad_query(rows, target):
-    count = rows.shape[0]
-    upper = iota((count, 128), 1) >= HEAD
-    for group in range(4):
-        tile = rows[:, 128 * group : 128 * group + 128]
-        turned = pltpu.roll(tile, HEAD, 1)
-        keep = upper if group % 2 else jnp.logical_not(upper)
-        low, high = (turned, tile) if group % 2 else (tile, turned)
-        target[group, :count, :] = jnp.where(keep, low, 0.0).astype(BF16)
-        target[group, count:, :] = jnp.where(keep, high, 0.0).astype(BF16)
-
-
-def pad_query_t(columns, target):
-    for group in range(4):
-        both = jnp.concatenate(
-            [
-                columns[128 * group : 128 * group + 64],
-                columns[128 * group + 64 : 128 * group + 128],
-            ],
-            axis=1,
-        ).astype(BF16)
-        blank = jnp.zeros(both.shape, BF16)
-        own = HEAD * (group % 2)
-        target[group, own : own + HEAD, :] = both
-        target[group, HEAD - own : 2 * HEAD - own, :] = blank
+def stack_rows(piece, upper):
+    turned = pltpu.roll(piece, HEAD, 1)
+    keep = iota(piece.shape, 1) >= HEAD if upper else iota(piece.shape, 1) < HEAD
+    first, second = (turned, piece) if upper else (piece, turned)
+    blank = jnp.zeros(piece.shape, piece.dtype)
+    return jnp.concatenate([jnp.where(keep, first, blank), jnp.where(keep, second, blank)], axis=0).astype(BF16)
+
+
+def stack_columns(piece):
+    turned = piece.T
+    return jnp.concatenate([turned[:HEAD], turned[HEAD:]], axis=1)
+
+
+def unstack(columns):
+    count = columns.shape[1] // 2
+    return jnp.concatenate([columns[:, :count], columns[:, count:]], axis=0).T
 
 
 def fold(wide):
@@ -153,6 +144,7 @@
     me, ep, z, x, c = place()
     blocks = 4 * planes
     pair = {"ctx": me, "ep": 1 - ep}
+    head = 2 * x + c
     up = {"ctx": jnp.minimum(me + 4, blocks - 1), "ep": ep}
     down = {"ctx": jnp.maximum(me - 4, 0), "ep": ep}
     across = {"ctx": block_of(z, 1 - x, c), "ep": ep}
@@ -165,7 +157,7 @@
     groups = 3 if planes >= 12 else 1
     owners = 4 * groups
     piece = (grad_rows // groups, r.pack.shape[3] // 4)
-    kept = r.from_across.shape[0]
+    kept = r.from_up.shape[0]
 
     load_q = pltpu.make_async_copy(r.q_hbm, r.q_w, r.load_sem.at[0])
     load_kv = pltpu.make_async_copy(r.kv_hbm, r.kv_w, r.load_sem.at[1])
@@ -201,14 +193,14 @@
 
     lax.fori_loop(0, slots, begin, 0)
 
-    signal(pair)
-
     def greet(step, carry):
         signal({"ctx": lax.rem(me + step, blocks), "ep": ep})
         return carry
 
+    for b in range(4):
+        signal({"ctx": 4 * z + b, "ep": 1 - ep})
     lax.fori_loop(1, blocks, greet, 0)
-    pl.semaphore_wait(pltpu.get_barrier_semaphore(), blocks)
+    pl.semaphore_wait(pltpu.get_barrier_semaphore(), blocks + 3)
 
     def swap(number, src, dst):
         return remote(src, dst, r.pair_send.at[number], r.pair_recv.at[number], pair)
@@ -231,33 +223,57 @@
     angles = (position - own_start).astype(F32) * r.freq[...]
     r.cosine[...] = jnp.cos(angles)
     r.sine[...] = jnp.sin(angles)
-    row_pos = me * block + iota((8, 2 * block), 1) % block
-    row_start, unused = doc_scan(row_pos, r.starts, r.adapters)
-    start_row, pos_row = row_start[:1], row_pos[:1]
-
-    def ring(number, half, way, target):
-        part = r.kvall.at[number, :, mine if half == 0 else theirs, :]
-        return remote(part, part, r.ring_send.at[way, number, half], r.ring_recv.at[number, half], target)
-
-    def forward_own(p, half):
-        number = block_of(p, x, c)
-
+    pos_rows = [((4 * z + b) * block + iota((8, 2 * block), 1) % block)[:1] for b in range(4)]
+    start_rows = [
+        doc_scan((4 * z + b) * block + iota((8, 2 * block), 1) % block, r.starts, r.adapters)[0][:1] for b in range(4)
+    ]
+
+    halves = (mine, theirs)
+
+    def other_head(step):
+        return lax.rem(head + step, 4)
+
+    def device_of(number):
+        return {"ctx": 4 * z + number, "ep": ep}
+
+    def kv_to(step, half):
+        number = other_head(step)
+        return remote(
+            r.kv_out.at[number, halves[half], :], r.kvall.at[z, head, halves[half], :],
+            r.kv_send.at[number, half], r.kv_recv.at[head, half], device_of(number),
+        )
+
+    def kv_from(step, half):
+        number = other_head(step)
+        return remote(
+            r.kv_out.at[number, halves[half], :], r.kvall.at[z, number, halves[half], :],
+            r.kv_send.at[number, half], r.kv_recv.at[number, half], device_of(number),
+        )
+
+    def piece_to(source, landing, sends, recvs, step):
+        number = other_head(step)
+        return remote(source.at[number], landing.at[head], sends.at[number], recvs.at[head], device_of(number))
+
+    def piece_from(source, landing, sends, recvs, step):
+        number = other_head(step)
+        return remote(source.at[number], landing.at[number], sends.at[number], recvs.at[number], device_of(number))
+
+    query_pieces = (r.q_out, r.q_in, r.q_send, r.q_recv)
+    grad_pieces = (r.d_out, r.d_in, r.d_send, r.d_recv)
+
+    def climb(p, half):
+        part = r.kvall.at[p, :, halves[half], :]
+        return remote(part, part, r.up_send.at[p, half], r.up_recv.at[p, half], up)
+
+    def climb_on(p, half):
         @pl.when(z < planes - 1)
         def _():
-            ring(number, half, 0, up).start()
-
-        ring(number, half, 1, across).start()
-        ring(number, half, 2, beside).start()
-
-    def forward_across(p, half):
-        number = block_of(p, 1 - x, c)
-        ring(number, half, 1, across).wait_recv()
-        ring(number, half, 2, beside).start()
-
-    def arrive_beside(p):
-        for column in (0, 1):
-            for half in (0, 1):
-                ring(block_of(p, column, 1 - c), half, 2, beside).wait_recv()
+            climb(p, half).start()
+
+    def collect(half):
+        for step in (1, 2, 3):
+            kv_from(step, half).wait_recv()
+        climb_on(z, half)
 
     def project(here):
         h1 = rms(r.x_all[here, :].astype(F32), r.attn_gain[...]).astype(BF16)
@@ -265,149 +281,198 @@
         mids = (dot(h1, r.qkv_down[...], NT) * r.mask[here, : 3 * SPAN]).astype(BF16)
         r.mids[here, :] = mids
         k_lin = dot(h1, r.kv_w[0]) + dot(mids[:, SPAN : 2 * SPAN], r.kv_up[0])
-        r.kvall[me, 0, here, :] = rotate(k_lin, r.cosine[here, :], r.sine[here, :], 1.0).astype(BF16)
-        r.kvall[me, 1, here, :] = (dot(h1, r.kv_w[1]) + dot(mids[:, 2 * SPAN :], r.kv_up[1])).astype(BF16)
+        keys = rotate(k_lin, r.cosine[here, :], r.sine[here, :], 1.0)
+        values = dot(h1, r.kv_w[1]) + dot(mids[:, 2 * SPAN :], r.kv_up[1])
+        for number in range(4):
+            lanes = slice(HEAD * number, HEAD * number + HEAD)
+            r.kv_out[number, here, :] = jnp.concatenate([keys[:, lanes], values[:, lanes]], axis=1).astype(BF16)
+        r.kvall[z, head, here, :] = r.kv_out[head, here, :]
 
     load_kv.wait()
     project(mine)
-    forward_own(z, 0)
+    for step in (1, 2, 3):
+        kv_to(step, 0).start()
     send_x.wait_recv()
     load_o.wait()
-    send_ow = swap(3, r.ow_all.at[ep], r.ow_all.at[ep])
+
+    def ow_quarter(side, number):
+        return r.ow_all.at[side, pl.ds(pl.multiple_of(128 * number, 128), 128), :]
+
+    def hand_on(number, way, target):
+        part = ow_quarter(1 - ep, number)
+        return remote(part, part, r.ow_send.at[number, way], r.ow_recv.at[number], target)
+
+    sibling = 2 * (1 - x) + c
+
+    def hand_first():
+        send_ow.wait_recv()
+        hand_on(head, 0, across).start()
+        hand_on(head, 1, beside).start()
+
+    def hand_second():
+        hand_on(sibling, 0, across).wait_recv()
+        hand_on(sibling, 1, beside).start()
+
+    def hand_last():
+        hand_on(2 * x + 1 - c, 1, beside).wait_recv()
+        hand_on(2 * (1 - x) + 1 - c, 1, beside).wait_recv()
+
+    send_ow = swap(3, ow_quarter(ep, head), ow_quarter(ep, head))
     send_od = swap(4, r.od_all.at[ep], r.od_all.at[ep])
     send_hot = swap(1, r.hot_all.at[mine], r.hot_all.at[mine])
     send_g = swap(2, r.grad, r.g_all.at[mine])
-    for copy in (send_ow, send_od, send_hot, send_g):
+    for copy in (send_ow, send_od, send_hot):
         copy.start()
     project(theirs)
-    forward_own(z, 1)
+    for step in (1, 2, 3):
+        kv_to(step, 1).start()
     load_q.wait()
     q_lin = dot(r.h1[...], r.q_w[...]) + dot(r.mids[:, :SPAN], r.q_up[...])
-    query = rotate(q_lin, r.cosine[...], r.sine[...], 1.0).astype(BF16).astype(F32)
-    pad_query(query, r.qn)
-    pad_query_t((query * SCALE).T, r.qt)
+    query = rotate(q_lin, r.cosine[...], r.sine[...], 1.0).astype(BF16)
+    for number in range(4):
+        r.q_out[number] = query[:, 128 * number : 128 * number + 128]
+    for step in (1, 2, 3):
+        piece_to(*query_pieces, step).start()
+    collect(0)
+    send_g.start()
+    hand_first()
+    r.q_in[head] = r.q_out[head]
     r.m_s[...] = jnp.full(r.m_s.shape, LOW, F32)
     r.l_s[...] = jnp.zeros(r.l_s.shape, F32)
     r.acc[...] = jnp.zeros(r.acc.shape, F32)
-    forward_across(z, 0)
-    forward_across(z, 1)
-    arrive_beside(z)
-
-    def head_step(p, group, masked):
-        tile = slice(128 * (group // 2), 128 * (group // 2) + 128)
+    r.qt[:, HEAD:, :] = jnp.zeros((4, HEAD, 2 * block), BF16)
+    r.dt[:, :HEAD, :] = jnp.zeros((4, HEAD, 2 * block), BF16)
+    collect(1)
+    for step in (1, 2, 3):
+        piece_from(*query_pieces, step).wait_recv()
+    for b in range(4):
+        scaled = r.q_in[b].astype(F32) * SCALE
+        r.qt[b, :HEAD, :] = stack_columns(scaled).astype(BF16)
+        r.qn[b] = stack_rows(scaled, False)
+
+    def attend_step(p, b, kinds):
         scores, peak = [], None
+        pos_row, start_row = pos_rows[b], start_rows[b]
         sees = start_row <= (4 * p + 1) * block
-        for b in range(4):
-            s = dot(r.kvall[4 * p + b, 0, :, tile], r.qt[group])
-            if masked[b]:
-                key = (4 * p + b) * block + iota(s.shape, 0)
+        for kb, masked in kinds:
+            s = dot(r.kvall[p, kb], r.qt[b])
+            if masked:
+                key = (4 * p + kb) * block + iota(s.shape, 0)
                 s = jnp.where((key <= pos_row) & (key >= start_row), s, LOW)
             scores.append(s)
             highest = jnp.max(s, axis=0, keepdims=True)
-            if not masked[b]:
+            if not masked:
                 highest = jnp.where(sees, highest, LOW)
             peak = highest if peak is None else jnp.maximum(peak, highest)
-        old = r.m_s[group]
+        old = r.m_s[b]
         new = jnp.maximum(old, peak)
-        r.m_s[group] = new
+        r.m_s[b] = new
         blind = jnp.where(sees, new, -LOW)
         decay = jnp.exp(old - new)
-        total = r.l_s[group] * decay
-        grown = r.acc[group] * decay
-        for b in range(4):
-            w = jnp.exp(scores[b] - (new if masked[b] else blind))
+        total = r.l_s[b] * decay
+        grown = r.acc[b] * decay
+        for (kb, masked), s in zip(kinds, scores):
+            w = jnp.exp(s - (new if masked else blind))
             total = total + jnp.sum(w, axis=0, keepdims=True)
-            added = dot(r.kvall[4 * p + b, 1, :, tile], w.astype(BF16), TN)
-            grown = grown + added[HEAD * (group % 2) : HEAD * (group % 2) + HEAD]
-        r.l_s[group] = total
-        r.acc[group] = grown
-
-    def send_att(group):
-        part = r.att_all.at[ep, :, pl.ds(128 * group, 128)]
-        return swap(5 + group, part, part)
-
-    def settle(group):
-        r.lse[group] = r.m_s[group] + jnp.log(r.l_s[group])
-        done = r.acc[group] / r.l_s[group]
-        attended = jnp.concatenate([done[:, :block], done[:, block:]], axis=0).T
-        tile = slice(128 * group, 128 * group + 128)
-        r.att[:, tile] = attended
-        r.att_all[ep, :, tile] = attended.astype(BF16)
-        send_att(group).start()
+            grown = grown + dot(r.kvall[p, kb], w.astype(BF16), TN)[HEAD:]
+        r.l_s[b] = total
+        r.acc[b] = grown
+
+    def att_to(b, side):
+        return remote(
+            r.o_out.at[b], r.att_all.at[ep, :, pl.ds(pl.multiple_of(128 * head, 128), 128)],
+            r.att_send.at[b, side], r.att_recv.at[ep, head], {"ctx": 4 * z + b, "ep": side},
+        )
+
+    def att_from(side, number):
+        return remote(
+            r.o_out.at[0], r.att_all.at[side, :, pl.ds(128 * number, 128)],
+            r.att_send.at[0, 0], r.att_recv.at[side, number], {"ctx": 4 * z + number, "ep": side},
+        )
+
+    def settle(b):
+        r.lse[b] = r.m_s[b] + jnp.log(r.l_s[b])
+        done = r.acc[b] / r.l_s[b]
+        r.acc[b] = done
+        r.o_out[b] = unstack(done).astype(BF16)
+
+        @pl.when(b == head)
+        def _():
+            r.att_all[ep, :, pl.ds(pl.multiple_of(128 * head, 128), 128)] = r.o_out[b]
+
+        @pl.when(b != head)
+        def _():
+            att_to(b, ep).start()
+
+        att_to(b, 1 - ep).start()
 
     def plane_forward(turn, carry):
         p = z - turn
 
-        def heads(group):
+        def steps(b):
             @pl.when(turn == 0)
             def _():
-                head_step(p, group, (True,) * 4)
+                attend_step(p, b, [(kb, kb in (0, b)) for kb in range(b + 1)])
 
             @pl.when((turn > 0) & (p > 0))
             def _():
-                head_step(p, group, (False,) * 4)
+                attend_step(p, b, [(kb, False) for kb in range(4)])
 
             @pl.when((turn > 0) & (p == 0))
             def _():
-                head_step(p, group, (True, False, False, False))
+                attend_step(p, b, [(kb, kb == 0) for kb in range(4)])
 
             @pl.when(p == 0)
             def _():
-                settle(group)
-
-        heads(0)
-
-        @pl.when(p > 0)
-        def _():
-            ring(block_of(p - 1, x, c), 0, 0, up).wait_recv()
-            forward_own(p - 1, 0)
-
-        heads(1)
-
-        @pl.when(p > 0)
-        def _():
-            ring(block_of(p - 1, x, c), 1, 0, up).wait_recv()
-            forward_own(p - 1, 1)
-
-        heads(2)
-
-        @pl.when(p > 0)
-        def _():
-            forward_across(p - 1, 0)
-
-        heads(3)
-
-        @pl.when(p > 0)
-        def _():
-            forward_across(p - 1, 1)
-            arrive_beside(p - 1)
-
+                settle(b)
+
+        def climbing(half):
+            @pl.when(p > 0)
+            def _():
+                climb(p - 1, half).wait_recv()
+                climb_on(p - 1, half)
+
+        steps(3)
+        climbing(0)
+        steps(2)
+        steps(1)
+        climbing(1)
+
+        @pl.when(turn == 0)
+        def _():
+            hand_second()
+
+        steps(0)
         return carry
 
     lax.fori_loop(0, z + 1, plane_forward, 0)
 
-    def ring_drain(p, carry):
-        for side in (0, 1):
-
-            @pl.when(z < planes - 1)
-            def _():
-                ring(block_of(p, x, c), side, 0, up).wait_send()
-
-            ring(block_of(p, x, c), side, 1, across).wait_send()
-            ring(block_of(p, x, c), side, 2, beside).wait_send()
-            ring(block_of(p, 1 - x, c), side, 2, beside).wait_send()
-        return carry
-
-    send_ow.wait_recv()
+    def drain_forward():
+        for step in (1, 2, 3):
+            kv_to(step, 0).wait_send()
+            kv_to(step, 1).wait_send()
+            piece_to(*query_pieces, step).wait_send()
+
+        @pl.when(z < planes - 1)
+        def _():
+            def left(p, carry):
+                climb(p, 0).wait_send()
+                climb(p, 1).wait_send()
+                return carry
+
+            lax.fori_loop(0, z + 1, left, 0)
+
+    hand_last()
     send_od.wait_recv()
 
     def half_product(index, carry):
         which = jnp.where(index == 0, ep, 1 - ep)
 
-        @pl.when(index == 1)
-        def _():
-            for group in range(4):
-                send_att(group).wait_recv()
+        for number in range(4):
+
+            @pl.when((index == 1) | (number != head))
+            def _():
+                att_from(which, number).wait_recv()
 
         r.halves[which] = dot(r.att_all[which], r.ow_all[which])
         r.half_mid[which] = dot(r.att_all[which], r.od_all[which], NT)
@@ -749,7 +814,7 @@
     early_scatter, early_total, early_finish = small_sum(0, r.early, r.early_land, r.early_out)
     late_scatter, late_total, late_finish = small_sum(1, r.late, r.late_land, r.late_out)
 
-    lax.fori_loop(0, z + 1, ring_drain, 0)
+    drain_forward()
 
     send_dg.wait_recv()
     blank = jnp.zeros((112, block), F32)
@@ -766,16 +831,11 @@
     r.acc_h2[...] = d_x2
     d_mid_o = (dot(d_attn, r.o_up[...], NT) * r.mask[:, :SPAN]).astype(BF16)
 
-    d_att = (dot(d_attn, r.ow_all[ep], NT) + dot(d_mid_o, r.od_all[ep])).astype(BF16).astype(F32)
-    pad_query(d_att, r.dn)
-    pad_query_t(d_att.T, r.dt)
-    product = (d_att * r.att[...]).T
-    for group in range(4):
-        for side in (0, 1):
-            first = 128 * group + 64 * side
-            r.delta[group, :, side * block : side * block + block] = jnp.sum(
-                product[first : first + 64], axis=0, keepdims=True
-            )
+    d_att = (dot(d_attn, r.ow_all[ep], NT) + dot(d_mid_o, r.od_all[ep])).astype(BF16)
+    for number in range(4):
+        r.d_out[number] = d_att[:, 128 * number : 128 * number + 128]
+    for step in (1, 2, 3):
+        piece_to(*grad_pieces, step).start()
     r.dqt[...] = jnp.zeros(r.dqt.shape, F32)
     r.early[:32, :] = dot(r.mid_o[...], d_attn, TN).astype(BF16)
     r.early[32:48, :] = fold(dot(d_mid_o, r.att_all[ep], TN)).astype(BF16)
@@ -783,117 +843,116 @@
     early_scatter()
     stage_own(1)
 
-    def block_step(number, masked):
-        new_k, new_v = [], []
-        for group in range(4):
-            tile = slice(128 * (group // 2), 128 * (group // 2) + 128)
-            keys = r.kvall[number, 0, :, tile]
-            s = dot(keys, r.qt[group])
-            base = r.lse[group]
+    r.d_in[head] = r.d_out[head]
+    for step in (1, 2, 3):
+        piece_from(*grad_pieces, step).wait_recv()
+    for b in range(4):
+        received = r.d_in[b].astype(F32)
+        turned = stack_columns(received)
+        r.dt[b, HEAD:, :] = turned.astype(BF16)
+        r.delta[b] = jnp.sum(turned * r.acc[b], axis=0, keepdims=True)
+        r.dn[b] = stack_rows(received, True)
+
+    def back_step(p, kb, kinds):
+        kv = r.kvall[p, kb]
+        grown = None
+        for b, masked in kinds:
+            pos_row, start_row = pos_rows[b], start_rows[b]
+            s = dot(kv, r.qt[b])
+            base = r.lse[b]
             if masked:
-                key = number * block + iota(s.shape, 0)
+                key = (4 * p + kb) * block + iota(s.shape, 0)
                 w = jnp.where((key <= pos_row) & (key >= start_row), jnp.exp(s - base), 0.0)
             else:
-                w = jnp.exp(s - jnp.where(start_row <= number * block, base, -LOW))
-            d_w = dot(r.kvall[number, 1, :, tile], r.dt[group])
-            d_s = (w * (d_w - r.delta[group])).astype(BF16)
-            new_k.append(dot(d_s, r.qn[group]))
-            new_v.append(dot(w.astype(BF16), r.dn[group]))
-            r.dqt[group] += dot(keys, d_s, TN)[HEAD * (group % 2) : HEAD * (group % 2) + HEAD]
-        for side in (0, 1):
-            tile = slice(128 * side, 128 * side + 128)
-            r.kvall[number, 0, :, tile] = ((new_k[2 * side] + new_k[2 * side + 1]) * SCALE).astype(BF16)
-            r.kvall[number, 1, :, tile] = (new_v[2 * side] + new_v[2 * side + 1]).astype(BF16)
-
-    def compute(number):
-        edge = (number == 0) | (number == me)
-
-        @pl.when(edge)
-        def _():
-            block_step(number, True)
-
-        @pl.when((number < me) & jnp.logical_not(edge))
-        def _():
-            block_step(number, False)
-
-        @pl.when(number > me)
-        def _():
-            r.kvall[number] = jnp.zeros(r.kvall.shape[1:], BF16)
-
-    def to_beside(p, column):
-        return remote(
-            r.kvall.at[block_of(p, column, 1 - c)], r.from_beside.at[p % kept, column],
-            r.beside_send.at[p, column], r.beside_recv.at[p, column], beside,
-        )
-
-    def over(p):
-        return remote(
-            r.kvall.at[block_of(p, 1 - x, c)], r.from_across.at[p % kept], r.across_send.at[p], r.across_recv.at[p], across
-        )
+                w = jnp.exp(s - jnp.where(start_row <= (4 * p + 1) * block, base, -LOW))
+            d_w = dot(kv, r.dt[b])
+            d_s = (w * (d_w - r.delta[b])).astype(BF16)
+            added = dot(d_s, r.qn[b]) + dot(w.astype(BF16), r.dn[b])
+            grown = added if grown is None else grown + added
+            r.dqt[b] += dot(kv, d_s, TN)[:HEAD]
+        r.kvall[p, kb] = grown.astype(BF16)
 
     def lower(p):
-        return remote(r.kvall.at[block_of(p, x, c)], r.from_up.at[p % kept], r.down_send.at[p], r.down_recv.at[p], down)
-
-    def claim(p, number):
-        if planes > kept:
-
-            @pl.when(p >= kept)
+        return remote(r.kvall.at[p], r.from_up.at[p % kept], r.down_send.at[p], r.down_recv.at[p], down)
+
+    def finish(p):
+        @pl.when(z < planes - 1)
+        def _():
+            lower(p).wait_recv()
+            r.kvall[p] = (r.kvall[p].astype(F32) + r.from_up[p % kept].astype(F32)).astype(BF16)
+            if planes > kept:
+
+                @pl.when(p + kept <= z)
+                def _():
+                    pl.semaphore_signal(r.credit, inc=1, device_id=up, device_id_type=MESH)
+
+        @pl.when(p < z)
+        def _():
+            if planes > kept:
+
+                @pl.when(p >= kept)
+                def _():
+                    pl.semaphore_wait(r.credit, 1)
+
+            lower(p).start()
+
+    def back_to(source, landing, sends, recvs, b):
+        return remote(source.at[b], landing.at[head], sends.at[b], recvs.at[head], device_of(b))
+
+    def back_from(landing, sends, recvs, number):
+        return remote(landing.at[number], landing.at[number], sends.at[number], recvs.at[number], device_of(number))
+
+    def give_back(source, landing, sends, recvs, b):
+        @pl.when(b == head)
+        def _():
+            landing[b] = source[b]
+
+        @pl.when(b != head)
+        def _():
+            back_to(source, landing, sends, recvs, b).start()
+
+    dq_pieces = (r.dq_out, r.dq_in, r.dq_send, r.dq_recv)
+    dkv_pieces = (r.kvall.at[z], r.dkv_in, r.dkv_send, r.dkv_recv)
+
+    def plane_back(p, carry):
+        @pl.when(p < z)
+        def _():
+            @pl.when(p == 0)
             def _():
-                pl.semaphore_wait(r.credit.at[number], 1)
-
-    def release(p):
-        if planes > kept:
-
-            @pl.when(p + kept <= z)
-            def _():
-                pl.semaphore_signal(r.credit.at[0], inc=1, device_id=beside, device_id_type=MESH)
-                pl.semaphore_signal(r.credit.at[1], inc=1, device_id=across, device_id_type=MESH)
-
-            @pl.when((p + kept <= z) & (z < planes - 1))
-            def _():
-                pl.semaphore_signal(r.credit.at[2], inc=1, device_id=up, device_id_type=MESH)
-
-    def finish(p):
-        number = block_of(p, x, c)
-        over(p).wait_recv()
-        total = (
-            r.kvall[number].astype(F32) + r.from_beside[p % kept, x].astype(F32) + r.from_across[p % kept].astype(F32)
-        )
-        r.kvall[number] = total.astype(BF16)
-
-        @pl.when(z < planes - 1)
-        def _():
-            lower(p).wait_recv()
-            r.kvall[number] = (total + r.from_up[p % kept].astype(F32)).astype(BF16)
-
-        release(p)
-
-        @pl.when(p < z)
-        def _():
-            claim(p, 2)
-            lower(p).start()
-
-    def plane_back(p, carry):
-        @pl.when(p <= z)
-        def _():
-            compute(block_of(p, 1 - x, 1 - c))
-            claim(p, 0)
-            to_beside(p, 1 - x).start()
-            compute(block_of(p, 1 - x, c))
-            to_beside(p, 1 - x).wait_recv()
-            number = block_of(p, 1 - x, c)
-            r.kvall[number] = (r.kvall[number].astype(F32) + r.from_beside[p % kept, 1 - x].astype(F32)).astype(BF16)
-            claim(p, 1)
-            over(p).start()
-            compute(block_of(p, x, 1 - c))
-            to_beside(p, x).start()
-
-            @pl.when(p > 0)
+                back_step(p, 0, [(b, True) for b in range(4)])
+
+            def middle(kb, inner):
+                back_step(p, kb, [(b, False) for b in range(4)])
+                return inner
+
+            lax.fori_loop(jnp.where(p == 0, 1, 0), 2, middle, 0)
+
+            @pl.when((p > 0) & (z < planes - 1))
             def _():
                 finish(p - 1)
 
-            compute(block_of(p, x, c))
-            to_beside(p, x).wait_recv()
+            lax.fori_loop(2, 4, middle, 0)
+
+            @pl.when(z == planes - 1)
+            def _():
+                finish(p)
+
+        @pl.when(p == z)
+        def _():
+            for kb in range(4):
+                back_step(p, kb, [(b, b == kb or kb == 0) for b in range(kb, 4)])
+                r.dq_out[kb] = (unstack(r.dqt[kb]) * SCALE).astype(BF16)
+                give_back(*dq_pieces, kb)
+
+                @pl.when(z == planes - 1)
+                def _():
+                    give_back(*dkv_pieces, kb)
+
+                if kb == 1:
+
+                    @pl.when((p > 0) & (z < planes - 1))
+                    def _():
+                        finish(p - 1)
 
         @pl.when(p == 0)
         def _():
@@ -911,17 +970,26 @@
         return carry
 
     lax.fori_loop(0, planes, plane_back, 0)
-    finish(z)
+
+    @pl.when(z < planes - 1)
+    def _():
+        finish(z)
+        for b in range(4):
+            give_back(*dkv_pieces, b)
 
     cosine, sine = r.cosine[...], r.sine[...]
-    parts = []
-    for group in range(4):
-        both = r.dqt[group]
-        parts += [both[:, :block], both[:, block:]]
-    d_query = jnp.concatenate(parts, axis=0).T * SCALE
-    d_q = rotate(d_query.astype(BF16).astype(F32), cosine, sine, -1.0).astype(BF16)
-    d_k = rotate(r.kvall[me, 0].astype(F32), cosine, sine, -1.0).astype(BF16)
-    d_value = r.kvall[me, 1]
+    for number in range(4):
+
+        @pl.when(number != head)
+        def _():
+            back_from(*dq_pieces[1:], number).wait_recv()
+            back_from(*dkv_pieces[1:], number).wait_recv()
+
+    d_query = jnp.concatenate([r.dq_in[number] for number in range(4)], axis=1)
+    d_q = rotate(d_query.astype(F32), cosine, sine, -1.0).astype(BF16)
+    d_key = jnp.concatenate([r.dkv_in[number, :, :HEAD] for number in range(4)], axis=1)
+    d_k = rotate(d_key.astype(F32), cosine, sine, -1.0).astype(BF16)
+    d_value = jnp.concatenate([r.dkv_in[number, :, HEAD:] for number in range(4)], axis=1)
     r.mid_trade[ep] = jnp.concatenate(
         [dot(d_q, r.q_up[...], NT), dot(d_k, r.kv_up[0], NT), dot(d_value, r.kv_up[1], NT)], axis=1
     ).astype(BF16)
@@ -960,21 +1028,26 @@
 
     for copy in (send_x, send_ow, send_od, send_hot, send_g, send_dg, send_h2, send_out, send_mid, send_norm):
         copy.wait_send()
-    for group in range(4):
-        send_att(group).wait_send()
+    for b in range(4):
+        att_to(b, 1 - ep).wait_send()
+
+        @pl.when(b != head)
+        def _():
+            att_to(b, ep).wait_send()
+            back_to(*dq_pieces, b).wait_send()
+            back_to(*dkv_pieces, b).wait_send()
+
+    for step in (1, 2, 3):
+        piece_to(*grad_pieces, step).wait_send()
+    hand_on(head, 0, across).wait_send()
+    hand_on(head, 1, beside).wait_send()
+    hand_on(sibling, 1, beside).wait_send()
 
     def drain(p, carry):
-        for side in (0, 1):
-            to_beside(p, side).wait_send()
-        over(p).wait_send()
-
-        @pl.when(p < z)
-        def _():
-            lower(p).wait_send()
-
+        lower(p).wait_send()
         return carry
 
-    lax.fori_loop(0, z + 1, drain, 0)
+    lax.fori_loop(0, z, drain, 0)
     late_finish()
 
 
@@ -1057,7 +1130,7 @@
     heads = q_weight.shape[1]
     kv = key_value_weight.shape[2]
     experts = expert_in.shape[0]
-    slots = 4 if planes <= 4 else 2
+    slots = 6 if planes <= 4 else 4
     kept = planes if planes <= 4 else 2
     grad_rows = 2 * SPAN + SPAN + SPAN // 2 + SPAN
     base = experts * grad_rows
@@ -1097,24 +1170,26 @@
         d_mid_in=low(experts, block, 2 * SPAN), mid_out=low(experts, block, SPAN),
         x_all=low(block, width), g_all=low(block, width), h1=low(block, width), h2=low(block, width),
         hot_all=low(block, 128), mask=full(block, 128), cosine=full(block, 128), sine=full(block, 128),
-        mids=low(block, 3 * SPAN), kvall=low(blocks, 2, block, kv), qt=low(4, 128, 2 * block),
+        mids=low(block, 3 * SPAN), kvall=low(planes, 4, block, 128), kv_out=low(4, block, 128), q_out=low(4, block, 128),
+        q_in=low(4, block, 128), d_out=low(4, block, 128), d_in=low(4, block, 128), o_out=low(4, block, 128),
+        dq_out=low(4, block, 128), dq_in=low(4, block, 128), dkv_in=low(4, block, 128), qt=low(4, 128, 2 * block),
         qn=low(4, 2 * block, 128), dt=low(4, 128, 2 * block), dn=low(4, 2 * block, 128),
         m_s=full(4, 1, 2 * block), l_s=full(4, 1, 2 * block), lse=full(4, 1, 2 * block),
         delta=full(4, 1, 2 * block), acc=full(4, HEAD, 2 * block), dqt=full(4, HEAD, 2 * block),
-        att=full(block, heads), att_all=low(2, block, heads), halves=full(2, block, width), half_mid=full(2, block, SPAN), mid_o=low(block, SPAN), x2=full(block, width),
+        att_all=low(2, block, heads), halves=full(2, block, width), half_mid=full(2, block, SPAN), mid_o=low(block, SPAN), x2=full(block, width),
         gates=full(block, 2 * experts), dgates=full(block, 128), trade=low(2, block, width), out_trade=low(2, rows, width),
         norm_trade=low(2, rows, width), mid_trade=low(2, block, 3 * SPAN), dg_trade=full(2, 8, block),
         pack=low(2, 4, grad_rows, width), core_land=low(2, 2, grad_rows, width), x_land=low(2, grad_rows, width),
         z_land=low(2, planes, *piece), early=low(64, width), late=low(128, width),
         early_land=low(blocks, 16, early_width), late_land=low(blocks, 16, late_width),
-        from_beside=low(kept, 2, 2, block, kv), from_across=low(kept, 2, block, kv),
-        from_up=low(kept, 2, block, kv), credit=pltpu.SemaphoreType.REGULAR((3,)),
+        from_up=low(kept, 4, block, 128), credit=pltpu.SemaphoreType.REGULAR,
         load_sem=dma(5), expert_sem=dma(slots, 4), pair_send=dma(14), pair_recv=dma(14),
-        ring_send=dma(3, blocks, 2), ring_recv=dma(blocks, 2), core_send=dma(2, 2), core_recv=dma(2, 2),
+        kv_send=dma(4, 2), kv_recv=dma(4, 2), q_send=dma(4), q_recv=dma(4), d_send=dma(4), d_recv=dma(4),
+        dq_send=dma(4), dq_recv=dma(4), dkv_send=dma(4), dkv_recv=dma(4), up_send=dma(planes, 2),
+        up_recv=dma(planes, 2), ow_send=dma(4, 2), ow_recv=dma(4), att_send=dma(4, 2), att_recv=dma(2, 4), core_send=dma(2, 2), core_recv=dma(2, 2),
         x_send=dma(2), x_recv=dma(2), z_send=dma(2, 2, planes), z_recv=dma(2, 2, planes), last_send=dma(2, 2, 4),
         last_recv=dma(2, 4),
-        small_send=dma(2, 2, blocks), small_recv=dma(2, 2, blocks), beside_send=dma(planes, 2),
-        beside_recv=dma(planes, 2), across_send=dma(planes), across_recv=dma(planes), down_send=dma(planes),
+        small_send=dma(2, 2, blocks), small_recv=dma(2, 2, blocks), down_send=dma(planes),
         down_recv=dma(planes),
     )
     (out,) = pl.pallas_call(

time: 165 us -> 154 us (0.933)
  the two profiles are of different devices: /device:TPU:29 before, /device:TPU:0 now
where the time goes in v4:
time: 154 us
  Pallas kernels  153 us (99%)
    pallas_call x1, Pallas kernels, per_device(): pl.pallas_call(functools.partial(layer_kernel, planes, slots, INPUTS + OU...  149 us
    pallas_call x1, Pallas kernels, per_device(): pl.pallas_call(unpack_kernel, out_shape=[unpacked[name] for name in RESUL...  3.93 us

profile of v4, /device:TPU:0, one launch (start us, length us, event | category | flops | bytes accessed | tf_op | source)
XLA Modules:
  0.0 154.2 jit_solution(2736263094060958270)
XLA Ops:
  0.7 149.4 %layer.1.packed = bf16[1600,1024]{1,0:T(8,128)(2,1)} custom-call(bf16[128,1024]{1,0:T(8,128)(2,1)} %refs_0_.1, bf16[128,1024]{1,0:T(8,128)(2,1)} %refs_1_.1, s32[8,128]{1,0:T(8,128)} %bitcast.17, s32[8]{0:T(128)} %refs_3_.1, s32[8]{0:T(128)} %refs_4_.1, f32[1,1024]{1,0:T(1,128)} %bitcast.18, f32[1,1024]{1,0:T(1,128)} %bitcast.19, ...), custom_call_target="tpu_custom_call" | custom-call | tf_op jit(solution)/shard_map/layer/pallas_call | solution.py:1195
  150.1 3.9 %unpack.1 = (f32[8,64,1024]{2,1,0:T(8,128)}, f32[8,2,32,512]{3,2,1,0:T(8,128)}, f32[8,32,512]{2,1,0:T(8,128)}, f32[8,32,1024]{2,1,0:T(8,128)}, bf16[128,1024]{1,...) custom-call(bf16[1600,1024]{1,0:T(8,128)(2,1)} %layer.1.packed), custom_call_target="tpu_custom_call" | custom-call | tf_op jit(solution)/shard_map/unpack/pallas_call | solution.py:1216

commit v5 on v4

--- a/solution.py
+++ b/solution.py
@@ -137,10 +137,10 @@
     r.acc_out, r.acc_h2 = r.halves.at[0], r.halves.at[1]
     grad_rows = r.pack.shape[2]
     base = r.in_hbm.shape[0] * grad_rows
-    r.late_out = r.out.at[pl.ds(base, 128)]
-    r.block_out = r.out.at[pl.ds(base + 128, 128)]
-    r.in_grad = r.out.at[pl.ds(base + 256, 128)]
-    r.early_out = r.out.at[pl.ds(base + 384, 64)]
+    r.late_out = r.packed.at[pl.ds(base, 128)]
+    r.block_out = r.packed.at[pl.ds(base + 128, 128)]
+    r.in_grad = r.packed.at[pl.ds(base + 256, 128)]
+    r.early_out = r.packed.at[pl.ds(base + 384, 64)]
     me, ep, z, x, c = place()
     blocks = 4 * planes
     pair = {"ctx": me, "ep": 1 - ep}
@@ -195,18 +195,34 @@
 
     def greet(step, carry):
         signal({"ctx": lax.rem(me + step, blocks), "ep": ep})
+        signal({"ctx": lax.rem(me + step, blocks), "ep": 1 - ep})
         return carry
 
-    for b in range(4):
-        signal({"ctx": 4 * z + b, "ep": 1 - ep})
+    signal(pair)
     lax.fori_loop(1, blocks, greet, 0)
-    pl.semaphore_wait(pltpu.get_barrier_semaphore(), blocks + 3)
+    pl.semaphore_wait(pltpu.get_barrier_semaphore(), 2 * blocks - 1)
+
+    def wait_sent(like, sem):
+        remote(like, like, sem, sem, pair).wait_send()
+
+    def wait_received(like, sem):
+        remote(like, like, sem, sem, pair).wait_recv()
 
     def swap(number, src, dst):
         return remote(src, dst, r.pair_send.at[number], r.pair_recv.at[number], pair)
 
-    send_x = swap(0, r.resid, r.x_all.at[mine])
-    send_x.start()
+    small = rows // 2
+    chunks = (
+        (mine, rows),
+        (span(rows - ep * rows, small), small),
+        (span(rows - ep * rows + small, small), small),
+    )
+    send_x = []
+    for number in (0, 1):
+        part = pl.ds(small * number, small)
+        copy = swap(number, r.resid.at[part], r.x_all.at[span(ep * rows + small * number, small)])
+        copy.start()
+        send_x.append(copy)
 
     hot = jnp.zeros((r.ids.shape[0], rows), F32)
     hot = jnp.zeros((128, rows), F32)
@@ -228,41 +244,34 @@
         doc_scan((4 * z + b) * block + iota((8, 2 * block), 1) % block, r.starts, r.adapters)[0][:1] for b in range(4)
     ]
 
-    halves = (mine, theirs)
-
     def other_head(step):
         return lax.rem(head + step, 4)
 
     def device_of(number):
         return {"ctx": 4 * z + number, "ep": ep}
 
-    def kv_to(step, half):
+    def kv_to(step, chunk):
         number = other_head(step)
+        here = chunks[chunk][0]
         return remote(
-            r.kv_out.at[number, halves[half], :], r.kvall.at[z, head, halves[half], :],
-            r.kv_send.at[number, half], r.kv_recv.at[head, half], device_of(number),
+            r.kv_out.at[number, here, :], r.kvall.at[z, head, here, :],
+            r.kv_send.at[chunk], r.kv_recv.at[chunk], device_of(number),
         )
 
-    def kv_from(step, half):
+    def three(chunk):
+        return r.kv_out.at[pl.ds(0, 3), chunks[chunk][0], :]
+
+    def piece_to(source, landing, send, recv, step):
         number = other_head(step)
-        return remote(
-            r.kv_out.at[number, halves[half], :], r.kvall.at[z, number, halves[half], :],
-            r.kv_send.at[number, half], r.kv_recv.at[number, half], device_of(number),
-        )
-
-    def piece_to(source, landing, sends, recvs, step):
-        number = other_head(step)
-        return remote(source.at[number], landing.at[head], sends.at[number], recvs.at[head], device_of(number))
-
-    def piece_from(source, landing, sends, recvs, step):
-        number = other_head(step)
-        return remote(source.at[number], landing.at[number], sends.at[number], recvs.at[number], device_of(number))
-
-    query_pieces = (r.q_out, r.q_in, r.q_send, r.q_recv)
-    grad_pieces = (r.d_out, r.d_in, r.d_send, r.d_recv)
+        return remote(source.at[number], landing.at[head], send, recv, device_of(number))
+
+    three_pieces = r.q_out.at[pl.ds(0, 3)]
+
+    query_pieces = (r.q_out, r.q_in, r.piece_send.at[0], r.piece_recv.at[0])
+    grad_pieces = (r.d_out, r.d_in, r.piece_send.at[1], r.piece_recv.at[1])
 
     def climb(p, half):
-        part = r.kvall.at[p, :, halves[half], :]
+        part = r.kvall.at[p, :, chunks[half][0], :]
         return remote(part, part, r.up_send.at[p, half], r.up_recv.at[p, half], up)
 
     def climb_on(p, half):
@@ -271,8 +280,7 @@
             climb(p, half).start()
 
     def collect(half):
-        for step in (1, 2, 3):
-            kv_from(step, half).wait_recv()
+        wait_received(three(half), r.kv_recv.at[half])
         climb_on(z, half)
 
     def project(here):
@@ -292,7 +300,12 @@
     project(mine)
     for step in (1, 2, 3):
         kv_to(step, 0).start()
-    send_x.wait_recv()
+    send_x[0].wait_recv()
+    project(chunks[1][0])
+    for step in (1, 2, 3):
+        kv_to(step, 1).start()
+    collect(0)
+    send_x[1].wait_recv()
     load_o.wait()
 
     def ow_quarter(side, number):
@@ -317,15 +330,15 @@
         hand_on(2 * x + 1 - c, 1, beside).wait_recv()
         hand_on(2 * (1 - x) + 1 - c, 1, beside).wait_recv()
 
-    send_ow = swap(3, ow_quarter(ep, head), ow_quarter(ep, head))
+    send_ow = swap(12, ow_quarter(ep, head), ow_quarter(ep, head))
     send_od = swap(4, r.od_all.at[ep], r.od_all.at[ep])
-    send_hot = swap(1, r.hot_all.at[mine], r.hot_all.at[mine])
+    send_hot = swap(14, r.hot_all.at[mine], r.hot_all.at[mine])
     send_g = swap(2, r.grad, r.g_all.at[mine])
     for copy in (send_ow, send_od, send_hot):
         copy.start()
-    project(theirs)
+    project(chunks[2][0])
     for step in (1, 2, 3):
-        kv_to(step, 1).start()
+        kv_to(step, 2).start()
     load_q.wait()
     q_lin = dot(r.h1[...], r.q_w[...]) + dot(r.mids[:, :SPAN], r.q_up[...])
     query = rotate(q_lin, r.cosine[...], r.sine[...], 1.0).astype(BF16)
@@ -333,7 +346,7 @@
         r.q_out[number] = query[:, 128 * number : 128 * number + 128]
     for step in (1, 2, 3):
         piece_to(*query_pieces, step).start()
-    collect(0)
+    collect(1)
     send_g.start()
     hand_first()
     r.q_in[head] = r.q_out[head]
@@ -342,22 +355,22 @@
     r.acc[...] = jnp.zeros(r.acc.shape, F32)
     r.qt[:, HEAD:, :] = jnp.zeros((4, HEAD, 2 * block), BF16)
     r.dt[:, :HEAD, :] = jnp.zeros((4, HEAD, 2 * block), BF16)
-    collect(1)
-    for step in (1, 2, 3):
-        piece_from(*query_pieces, step).wait_recv()
+    collect(2)
+    wait_received(three_pieces, r.piece_recv.at[0])
     for b in range(4):
         scaled = r.q_in[b].astype(F32) * SCALE
         r.qt[b, :HEAD, :] = stack_columns(scaled).astype(BF16)
         r.qn[b] = stack_rows(scaled, False)
 
-    def attend_step(p, b, kinds):
-        scores, peak = [], None
+    def attend_step(p, b, keys, kinds):
         pos_row, start_row = pos_rows[b], start_rows[b]
         sees = start_row <= (4 * p + 1) * block
-        for kb, masked in kinds:
-            s = dot(r.kvall[p, kb], r.qt[b])
+        everything = dot(keys, r.qt[b])
+        scores, peak = [], None
+        for first, count, position, masked in kinds:
+            s = everything[first : first + count]
             if masked:
-                key = (4 * p + kb) * block + iota(s.shape, 0)
+                key = position + iota(s.shape, 0)
                 s = jnp.where((key <= pos_row) & (key >= start_row), s, LOW)
             scores.append(s)
             highest = jnp.max(s, axis=0, keepdims=True)
@@ -370,24 +383,19 @@
         blind = jnp.where(sees, new, -LOW)
         decay = jnp.exp(old - new)
         total = r.l_s[b] * decay
-        grown = r.acc[b] * decay
-        for (kb, masked), s in zip(kinds, scores):
+        weights = []
+        for (first, count, position, masked), s in zip(kinds, scores):
             w = jnp.exp(s - (new if masked else blind))
             total = total + jnp.sum(w, axis=0, keepdims=True)
-            grown = grown + dot(r.kvall[p, kb], w.astype(BF16), TN)[HEAD:]
+            weights.append(w.astype(BF16))
+        weights = jnp.concatenate(weights, axis=0) if len(weights) > 1 else weights[0]
         r.l_s[b] = total
-        r.acc[b] = grown
+        r.acc[b] = r.acc[b] * decay + dot(keys, weights, TN)[HEAD:]
 
     def att_to(b, side):
         return remote(
             r.o_out.at[b], r.att_all.at[ep, :, pl.ds(pl.multiple_of(128 * head, 128), 128)],
-            r.att_send.at[b, side], r.att_recv.at[ep, head], {"ctx": 4 * z + b, "ep": side},
-        )
-
-    def att_from(side, number):
-        return remote(
-            r.o_out.at[0], r.att_all.at[side, :, pl.ds(128 * number, 128)],
-            r.att_send.at[0, 0], r.att_recv.at[side, number], {"ctx": 4 * z + number, "ep": side},
+            r.att_send.at[jnp.where(side == ep, 0, 1)], r.att_recv.at[ep], {"ctx": 4 * z + b, "ep": side},
         )
 
     def settle(b):
@@ -406,58 +414,75 @@
 
         att_to(b, 1 - ep).start()
 
+    def take_chunk(p, chunk):
+        @pl.when((p >= 0) & ((p > 0) | (chunk == 0) | (z < planes - 1)))
+        def _():
+            climb(p, chunk).wait_recv()
+            climb_on(p, chunk)
+
+    def whole_plane(p, b, masked):
+        count = len(masked) * block
+        attend_step(
+            p, b, r.kvall[p, : len(masked)].reshape(count, 128),
+            [(kb * block, block, (4 * p + kb) * block, masked[kb]) for kb in range(len(masked))],
+        )
+
+    def half_plane(b, here, first):
+        attend_step(
+            0, b, r.kvall[0, :, here, :].reshape(4 * rows, 128),
+            [(kb * rows, rows, kb * block + first, kb == 0) for kb in range(4)],
+        )
+
     def plane_forward(turn, carry):
         p = z - turn
-
-        def steps(b):
+        for b in (3, 2, 1, 0):
+
             @pl.when(turn == 0)
             def _():
-                attend_step(p, b, [(kb, kb in (0, b)) for kb in range(b + 1)])
+                whole_plane(p, b, [kb in (0, b) for kb in range(b + 1)])
 
             @pl.when((turn > 0) & (p > 0))
             def _():
-                attend_step(p, b, [(kb, False) for kb in range(4)])
+                whole_plane(p, b, [False] * 4)
 
             @pl.when((turn > 0) & (p == 0))
             def _():
-                attend_step(p, b, [(kb, kb == 0) for kb in range(4)])
-
-            @pl.when(p == 0)
-            def _():
-                settle(b)
-
-        def climbing(half):
-            @pl.when(p > 0)
-            def _():
-                climb(p - 1, half).wait_recv()
-                climb_on(p - 1, half)
-
-        steps(3)
-        climbing(0)
-        steps(2)
-        steps(1)
-        climbing(1)
+                half_plane(b, mine, ep * rows)
+
+            if b > 0:
+                take_chunk(p - 1, 3 - b)
 
         @pl.when(turn == 0)
         def _():
             hand_second()
 
-        steps(0)
         return carry
 
     lax.fori_loop(0, z + 1, plane_forward, 0)
 
+    @pl.when((z == planes - 1) & (z > 0))
+    def _():
+        climb(0, 1).wait_recv()
+        climb(0, 2).wait_recv()
+
+    for b in (3, 2, 1, 0):
+
+        @pl.when(z > 0)
+        def _():
+            half_plane(b, theirs, rows - ep * rows)
+
+        settle(b)
+
     def drain_forward():
-        for step in (1, 2, 3):
-            kv_to(step, 0).wait_send()
-            kv_to(step, 1).wait_send()
-            piece_to(*query_pieces, step).wait_send()
+        for chunk in range(3):
+            wait_sent(three(chunk), r.kv_send.at[chunk])
+        wait_sent(three_pieces, r.piece_send.at[0])
 
         @pl.when(z < planes - 1)
         def _():
             def left(p, carry):
-                climb(p, 0).wait_send()
-                climb(p, 1).wait_send()
+                for chunk in range(3):
+                    climb(p, chunk).wait_send()
                 return carry
 
             lax.fori_loop(0, z + 1, left, 0)
@@ -468,11 +493,13 @@
     def half_product(index, carry):
         which = jnp.where(index == 0, ep, 1 - ep)
 
-        for number in range(4):
-
-            @pl.when((index == 1) | (number != head))
-            def _():
-                att_from(which, number).wait_recv()
+        @pl.when(index == 0)
+        def _():
+            wait_received(r.o_out.at[pl.ds(0, 3)], r.att_recv.at[ep])
+
+        @pl.when(index == 1)
+        def _():
+            wait_received(r.o_out, r.att_recv.at[1 - ep])
 
         r.halves[which] = dot(r.att_all[which], r.ow_all[which])
         r.half_mid[which] = dot(r.att_all[which], r.od_all[which], NT)
@@ -543,7 +570,7 @@
     def piece_in_final(half, owner):
         row, lane = piece_of(owner)
         start = pl.multiple_of(final_rows(half, quarter) + row, 16)
-        return r.out.at[pl.ds(start, piece[0]), pl.ds(lane, piece[1])]
+        return r.packed.at[pl.ds(start, piece[0]), pl.ds(lane, piece[1])]
 
     def plane_of(step):
         return lax.rem(z + step, planes)
@@ -551,32 +578,34 @@
     def give(half, step):
         other = plane_of(step)
         return remote(
-            piece_in_pack(half, other), r.z_land.at[half, z], r.z_send.at[half, 0, other],
-            r.z_recv.at[half, 0, z], {"ctx": block_of(other, x, c), "ep": ep},
-        )
-
-    def take(half, step):
-        other = plane_of(step)
-        return remote(
-            piece_in_pack(half, 0), r.z_land.at[half, other], r.z_send.at[half, 0, other],
-            r.z_recv.at[half, 0, other], {"ctx": block_of(other, x, c), "ep": ep},
+            piece_in_pack(half, other), r.z_land.at[half, z], r.z_send.at[half, 0],
+            r.z_recv.at[half, 0], {"ctx": block_of(other, x, c), "ep": ep},
         )
 
     def spread(half, step):
         other = plane_of(step)
         part = piece_in_final(half, z % owners)
         return remote(
-            part, part, r.z_send.at[half, 1, other], r.z_recv.at[half, 1, z],
+            part, part, r.z_send.at[half, 1], r.z_recv.at[half, 1],
             {"ctx": block_of(other, x, c), "ep": ep},
         )
 
-    def gather(half, step):
-        other = plane_of(step)
-        part = piece_in_final(half, other)
-        return remote(
-            part, part, r.z_send.at[half, 1, other], r.z_recv.at[half, 1, other],
-            {"ctx": block_of(other, x, c), "ep": ep},
-        )
+    def pieces(count):
+        return r.z_land.at[0, pl.ds(0, count)]
+
+    def for_pieces(wait, sem):
+        if owners < planes:
+
+            @pl.when(z < owners)
+            def _():
+                wait(pieces(owners - 1), sem)
+
+            @pl.when(z >= owners)
+            def _():
+                wait(pieces(owners), sem)
+
+        else:
+            wait(pieces(owners - 1), sem)
 
     def each_plane(act, among_owners):
         def step(number, carry):
@@ -599,7 +628,7 @@
             act()
 
     def over_final(half, number, way, target):
-        part = r.out.at[pl.ds(pl.multiple_of(final_rows(half, number), 16), grad_rows)]
+        part = r.packed.at[pl.ds(pl.multiple_of(final_rows(half, number), 16), grad_rows)]
         return remote(part, part, r.last_send.at[half, way, number], r.last_recv.at[half, number], target)
 
     def stage_pieces(half):
@@ -611,7 +640,7 @@
 
     def stage_own(half):
         def act():
-            each_plane(lambda step: take(half, step).wait_recv(), False)
+            wait_received(pieces(planes - 1), r.z_recv.at[half, 0])
             r.z_land[half, z] = piece_in_pack(half, z % owners)[...]
 
             def add(p, total):
@@ -624,7 +653,7 @@
         if_owner(act)
 
     def stage_column(half):
-        each_plane(lambda step: gather(half, step).wait_recv(), True)
+        for_pieces(wait_received, r.z_recv.at[half, 1])
         over_final(half, quarter, 0, across).start()
         over_final(half, quarter, 1, beside).start()
 
@@ -635,8 +664,10 @@
     def stage_end(half):
         over_final(half, 2 * x + 1 - c, 1, beside).wait_recv()
         over_final(half, 2 * (1 - x) + 1 - c, 1, beside).wait_recv()
-        each_plane(lambda step: give(half, step).wait_send(), True)
-        if_owner(lambda: each_plane(lambda step: spread(half, step).wait_send(), False))
+
+    def stage_drain(half):
+        for_pieces(wait_sent, r.z_send.at[half, 0])
+        if_owner(lambda: wait_sent(pieces(planes - 1), r.z_send.at[half, 1]))
         over_final(half, quarter, 0, across).wait_send()
         over_final(half, quarter, 1, beside).wait_send()
         over_final(half, 2 * (1 - x) + c, 1, beside).wait_send()
@@ -675,7 +706,16 @@
         r.d_mid_in[e] = d_mid_in
         r.mid_out[e] = scaled_mid
         r.acc_out[...] += dot((act.astype(F32) * gate).astype(BF16), r.w_out[slot])
-        r.acc_h2[...] += dot(d_gp, r.w_in[slot, :, :FF], NT) + dot(d_up, r.w_in[slot, :, FF:], NT)
+
+        @pl.when(turn < experts - 2)
+        def _():
+            r.acc_h2[...] += dot(d_gp, r.w_in[slot, :, :FF], NT) + dot(d_up, r.w_in[slot, :, FF:], NT)
+
+        @pl.when(turn >= experts - 2)
+        def _():
+            r.d_joint[turn - (experts - 2), :, :FF] = d_gp
+            r.d_joint[turn - (experts - 2), :, FF:] = d_up
+
         r.pack[half, q, :64, :] = dot(d_mid_in, h2, TN).astype(BF16)
         r.pack[half, q, 64:96, :FF] = dot(mid_in[:, :SPAN], d_gp, TN).astype(BF16)
         r.pack[half, q, 64:96, FF:] = dot(mid_in[:, SPAN:], d_up, TN).astype(BF16)
@@ -714,14 +754,22 @@
 
     lax.fori_loop(0, experts, one, 0)
     every = range(experts)
-    r.acc_h2[...] += dot(jnp.concatenate([r.d_mid_in[e] for e in every], axis=1), r.in_down[...].reshape(experts * lanes, -1))
-
     r.dg_trade[ep] = r.dgates[...].T[:8]
     send_dg = swap(9, r.dg_trade.at[ep], r.dg_trade.at[ep])
     send_dg.start()
-    r.trade[ep] = r.acc_h2[...].astype(BF16)
-    send_h2 = swap(10, r.trade.at[ep], r.trade.at[ep])
-    send_h2.start()
+    all_d_mids = jnp.concatenate([r.d_mid_in[e] for e in every], axis=1)
+    tile = 256
+    send_h2 = []
+    for number in range(r.acc_h2.shape[1] // tile):
+        columns = slice(tile * number, tile * number + tile)
+        ends = r.acc_h2[:, columns] + dot(all_d_mids, r.in_down[:, :, columns].reshape(experts * lanes, tile))
+        for index in (0, 1):
+            ends = ends + dot(r.d_joint[index], r.w_in[(experts - 2 + index) % slots, columns, :], NT)
+        r.trade[ep, :, columns] = ends.astype(BF16)
+        part = r.trade.at[ep, :, columns]
+        copy = swap((10, 3, 15, 16)[number], part, part)
+        copy.start()
+        send_h2.append(copy)
     r.acc_out[...] += dot(jnp.concatenate([r.mid_out[e] for e in every], axis=1), r.out_up[...].reshape(experts * SPAN, -1))
     r.out_trade[0] = r.acc_out[theirs, :].astype(BF16)
     send_out = swap(11, r.out_trade.at[0], r.out_trade.at[1])
@@ -729,91 +777,104 @@
     stage_own(0)
     stage_pieces(1)
 
-    def small_sum(number, source, landing, result):
+    def small_sum(number, source, landing, result, shared):
         tiles = source.shape[0] // 16
         width = landing.shape[2]
         each = source.shape[1] // width
         holders = tiles * each
+        shared = shared * each
+        private = me >= shared
+        mine_too = (me < holders) & (private | (me % 2 == ep))
+        send_one, send_two = r.small_send.at[number, 0], r.small_send.at[number, 1]
+        recv_one, recv_two = r.small_recv.at[number, 0], r.small_recv.at[number, 1]
+        own_index = me + blocks * ep
 
         def region(ref, owner):
             return ref.at[span(owner // each * 16, 16), span(owner % each * width, width)]
 
-        def other(step):
-            return lax.rem(me + step, blocks)
-
-        def to_owner(step):
-            owner = other(step)
-            return remote(
-                region(source, owner), landing.at[me], r.small_send.at[number, 0, owner],
-                r.small_recv.at[number, 0, me], {"ctx": owner, "ep": ep},
-            )
-
-        def from_all(step):
-            device = other(step)
-            return remote(
-                region(source, me % holders), landing.at[device], r.small_send.at[number, 0, device],
-                r.small_recv.at[number, 0, device], {"ctx": device, "ep": ep},
-            )
-
-        def to_all(step):
-            device = other(step)
+        def several(count):
+            return landing.at[pl.ds(0, count)]
+
+        def scatter():
+            def step(index, carry):
+                owner = lax.rem(me + index, blocks)
+                side = jnp.where(owner < shared, owner % 2, ep)
+
+                @pl.when((owner < holders) & ((index > 0) | (side != ep)))
+                def _():
+                    remote(
+                        region(source, owner), landing.at[own_index], send_one, recv_one, {"ctx": owner, "ep": side}
+                    ).start()
+
+                return carry
+
+            lax.fori_loop(0, blocks, step, 0)
+
+        def add(first, count):
+            def step(p, sums):
+                return sums + landing[p].astype(F32)
+
+            return lax.fori_loop(first, first + count, step, jnp.zeros(landing.shape[1:], F32))
+
+        def tell(side):
             part = region(result, me % holders)
-            return remote(
-                part, part, r.small_send.at[number, 1, device], r.small_recv.at[number, 1, me],
-                {"ctx": device, "ep": ep},
-            )
-
-        def from_owner(step):
-            owner = other(step)
-            part = region(result, owner)
-            return remote(
-                part, part, r.small_send.at[number, 1, owner], r.small_recv.at[number, 1, owner],
-                {"ctx": owner, "ep": ep},
-            )
-
-        def loop(act, mine_too):
+
             def step(index, carry):
-                if mine_too:
-                    act(index)
-                else:
-
-                    @pl.when(other(index) < holders)
-                    def _():
-                        act(index)
+                device = lax.rem(me + index, blocks)
+
+                @pl.when((index > 0) | (side != ep))
+                def _():
+                    remote(part, part, send_two, recv_two, {"ctx": device, "ep": side}).start()
 
                 return carry
 
-            lax.fori_loop(1, blocks, step, 0)
-
-        def scatter():
-            loop(lambda step: to_owner(step).start(), False)
+            lax.fori_loop(0, blocks, step, 0)
 
         def total():
-            @pl.when(me < holders)
+            @pl.when(mine_too)
             def _():
-                loop(lambda step: from_all(step).wait_recv(), True)
-                landing[me] = region(source, me % holders)[...]
-
-                def add(p, sums):
-                    return sums + landing[p].astype(F32)
-
-                sums = lax.fori_loop(0, blocks, add, jnp.zeros(landing.shape[1:], F32))
-                region(result, me % holders)[...] = sums.astype(BF16)
-                loop(lambda step: to_all(step).start(), True)
+                landing[own_index] = region(source, me % holders)[...]
+
+            @pl.when(mine_too & private)
+            def _():
+                wait_received(several(blocks - 1), recv_one)
+                region(result, me % holders)[...] = add(blocks * ep, blocks).astype(BF16)
+                tell(ep)
+
+            if shared:
+
+                @pl.when(mine_too & jnp.logical_not(private))
+                def _():
+                    wait_received(several(2 * blocks - 1), recv_one)
+                    region(result, me % holders)[...] = add(0, 2 * blocks).astype(BF16)
+                    tell(ep)
+                    tell(1 - ep)
 
         def finish():
-            loop(lambda step: from_owner(step).wait_recv(), False)
-            loop(lambda step: to_owner(step).wait_send(), False)
-
-            @pl.when(me < holders)
+            @pl.when(mine_too)
             def _():
-                loop(lambda step: to_all(step).wait_send(), True)
+                wait_received(several(holders - 1), recv_two)
+                wait_sent(several(holders - 1), send_one)
+
+            @pl.when(jnp.logical_not(mine_too))
+            def _():
+                wait_received(several(holders), recv_two)
+                wait_sent(several(holders), send_one)
+
+            @pl.when(mine_too & private)
+            def _():
+                wait_sent(several(blocks - 1), send_two)
+
+            if shared:
+
+                @pl.when(mine_too & jnp.logical_not(private))
+                def _():
+                    wait_sent(several(2 * blocks - 1), send_two)
 
         return scatter, total, finish
 
-    early_scatter, early_total, early_finish = small_sum(0, r.early, r.early_land, r.early_out)
-    late_scatter, late_total, late_finish = small_sum(1, r.late, r.late_land, r.late_out)
-
+    early_scatter, early_total, early_finish = small_sum(0, r.early, r.early_land, r.early_out, 0)
+    late_scatter, late_total, late_finish = small_sum(1, r.late, r.late_land, r.late_out, 6)
     drain_forward()
 
     send_dg.wait_recv()
@@ -824,7 +885,8 @@
     d_logits = (gates * (d_gates - jnp.sum(gates * d_gates, axis=1, keepdims=True))).astype(BF16)
     from_router = dot(d_logits, r.router[...])
     stage_column(0)
-    send_h2.wait_recv()
+    for copy in send_h2:
+        copy.wait_recv()
     d_h2 = r.trade[0].astype(F32) + r.trade[1].astype(F32) + from_router
     d_x2 = r.g_all[...].astype(F32) + rms_back(r.x2[...], r.moe_gain[...], d_h2)
     d_attn = d_x2.astype(BF16)
@@ -844,8 +906,7 @@
     stage_own(1)
 
     r.d_in[head] = r.d_out[head]
-    for step in (1, 2, 3):
-        piece_from(*grad_pieces, step).wait_recv()
+    wait_received(three_pieces, r.piece_recv.at[1])
     for b in range(4):
         received = r.d_in[b].astype(F32)
         turned = stack_columns(received)
@@ -896,23 +957,20 @@
 
             lower(p).start()
 
-    def back_to(source, landing, sends, recvs, b):
-        return remote(source.at[b], landing.at[head], sends.at[b], recvs.at[head], device_of(b))
-
-    def back_from(landing, sends, recvs, number):
-        return remote(landing.at[number], landing.at[number], sends.at[number], recvs.at[number], device_of(number))
-
-    def give_back(source, landing, sends, recvs, b):
+    def back_to(source, landing, send, recv, b):
+        return remote(source.at[b], landing.at[head], send, recv, device_of(b))
+
+    def give_back(source, landing, send, recv, b):
         @pl.when(b == head)
         def _():
             landing[b] = source[b]
 
         @pl.when(b != head)
         def _():
-            back_to(source, landing, sends, recvs, b).start()
-
-    dq_pieces = (r.dq_out, r.dq_in, r.dq_send, r.dq_recv)
-    dkv_pieces = (r.kvall.at[z], r.dkv_in, r.dkv_send, r.dkv_recv)
+            back_to(source, landing, send, recv, b).start()
+
+    dq_pieces = (r.dq_out, r.dq_in, r.piece_send.at[2], r.piece_recv.at[2])
+    dkv_pieces = (r.kvall.at[z], r.dkv_in, r.piece_send.at[3], r.piece_recv.at[3])
 
     def plane_back(p, carry):
         @pl.when(p < z)
@@ -956,16 +1014,15 @@
 
         @pl.when(p == 0)
         def _():
+            stage_core(0)
+
+        @pl.when(p == 1)
+        def _():
             stage_column(1)
-            stage_core(0)
-
-        @pl.when(p == 1)
+
+        @pl.when(p == 2)
         def _():
             early_total()
-
-        @pl.when(p == 2)
-        def _():
-            stage_core(1)
 
         return carry
 
@@ -978,67 +1035,65 @@
             give_back(*dkv_pieces, b)
 
     cosine, sine = r.cosine[...], r.sine[...]
-    for number in range(4):
-
-        @pl.when(number != head)
-        def _():
-            back_from(*dq_pieces[1:], number).wait_recv()
-            back_from(*dkv_pieces[1:], number).wait_recv()
-
+    wait_received(three_pieces, r.piece_recv.at[2])
+    wait_received(three_pieces, r.piece_recv.at[3])
     d_query = jnp.concatenate([r.dq_in[number] for number in range(4)], axis=1)
     d_q = rotate(d_query.astype(F32), cosine, sine, -1.0).astype(BF16)
     d_key = jnp.concatenate([r.dkv_in[number, :, :HEAD] for number in range(4)], axis=1)
     d_k = rotate(d_key.astype(F32), cosine, sine, -1.0).astype(BF16)
     d_value = jnp.concatenate([r.dkv_in[number, :, HEAD:] for number in range(4)], axis=1)
-    r.mid_trade[ep] = jnp.concatenate(
+    d_mids = jnp.concatenate(
         [dot(d_q, r.q_up[...], NT), dot(d_k, r.kv_up[0], NT), dot(d_value, r.kv_up[1], NT)], axis=1
-    ).astype(BF16)
-    send_mid = swap(12, r.mid_trade.at[ep], r.mid_trade.at[ep])
-    send_mid.start()
-    full = dot(d_q, r.q_w[...], NT) + dot(d_k, r.kv_w[0], NT) + dot(d_value, r.kv_w[1], NT)
-    first, second = full[:rows], full[rows:]
-    r.norm_trade[0] = jnp.where(ep == 0, second, first).astype(BF16)
-    send_norm = swap(13, r.norm_trade.at[0], r.norm_trade.at[1])
-    send_norm.start()
+    )
+    d_mids = (d_mids * r.mask[:, : 3 * SPAN]).astype(BF16)
+    r.late[:96, :] = dot(d_mids, r.h1[...], TN).astype(BF16)
     r.late[96:112, :] = fold(dot(r.mids[:, :SPAN], d_q, TN)).astype(BF16)
     r.late[112:, :] = fold(
         jnp.concatenate(
             [dot(r.mids[:, SPAN : 2 * SPAN], d_k, TN), dot(r.mids[:, 2 * SPAN :], d_value, TN)], axis=1
         )
     ).astype(BF16)
-    send_mid.wait_recv()
-    d_mids = (
-        (r.mid_trade[0].astype(F32) + r.mid_trade[1].astype(F32)) * r.mask[:, : 3 * SPAN]
-    ).astype(BF16)
-    r.late[:96, :] = dot(d_mids, r.h1[...], TN).astype(BF16)
     late_scatter()
+    full = (
+        dot(d_q, r.q_w[...], NT) + dot(d_k, r.kv_w[0], NT) + dot(d_value, r.kv_w[1], NT) + dot(d_mids, r.qkv_down[...])
+    )
+    first, second = full[:rows], full[rows:]
+    r.norm_trade[0] = jnp.where(ep == 0, second, first).astype(BF16)
+    send_norm = swap(13, r.norm_trade.at[0], r.norm_trade.at[1])
+    send_norm.start()
+    stage_core(1)
+    stage_end(0)
+    early_finish()
     send_out.wait_recv()
     r.block_out[...] = (r.x2[mine, :] + (r.acc_out[mine, :] + r.out_trade[1].astype(F32))).astype(BF16)
-    from_mids = dot(d_mids, r.qkv_down[...])
-    own = jnp.where(ep == 0, first + from_mids[:rows], second + from_mids[rows:])
+    own = jnp.where(ep == 0, first, second)
+    late_total()
+    stage_end(1)
+
+    def store(number, start, count):
+        return pltpu.make_async_copy(
+            r.packed.at[pl.ds(start, count)], r.out.at[pl.ds(start, count)], r.load_sem.at[number]
+        )
+
+    stores = [store(0, 0, base), store(1, base + 128, 128), store(2, base + 384, 64)]
+    for copy in stores:
+        copy.start()
     send_norm.wait_recv()
     own = own + r.norm_trade[1].astype(F32)
     r.in_grad[...] = (
         r.acc_h2[mine, :] + rms_back(r.x_all[mine, :].astype(F32), r.attn_gain[...], own)
     ).astype(BF16)
-    late_total()
-    early_finish()
-    stage_end(0)
-    stage_end(1)
-
-    for copy in (send_x, send_ow, send_od, send_hot, send_g, send_dg, send_h2, send_out, send_mid, send_norm):
+    stores.append(store(3, base + 256, 128))
+    stores[-1].start()
+    stage_drain(0)
+    stage_drain(1)
+
+    for copy in (*send_x, send_ow, send_od, send_hot, send_g, send_dg, *send_h2, send_out, send_norm):
         copy.wait_send()
-    for b in range(4):
-        att_to(b, 1 - ep).wait_send()
-
-        @pl.when(b != head)
-        def _():
-            att_to(b, ep).wait_send()
-            back_to(*dq_pieces, b).wait_send()
-            back_to(*dkv_pieces, b).wait_send()
-
-    for step in (1, 2, 3):
-        piece_to(*grad_pieces, step).wait_send()
+    wait_sent(r.o_out.at[pl.ds(0, 3)], r.att_send.at[0])
+    wait_sent(r.o_out, r.att_send.at[1])
+    for number in (1, 2, 3):
+        wait_sent(three_pieces, r.piece_send.at[number])
     hand_on(head, 0, across).wait_send()
     hand_on(head, 1, beside).wait_send()
     hand_on(sibling, 1, beside).wait_send()
@@ -1049,6 +1104,10 @@
 
     lax.fori_loop(0, z, drain, 0)
     late_finish()
+    stores.append(store(4, base, 128))
+    stores[-1].start()
+    for copy in stores:
+        copy.wait()
 
 
 RESULTS = (
@@ -1167,7 +1226,7 @@
         in_down=low(experts, 2 * SPAN, width), w_in_up=low(slots, *expert_in_up.shape[1:]),
         w_out_down=low(slots, SPAN, FF), out_up=low(experts, SPAN, width),
         mid_in=low(experts, block, 2 * SPAN), lifted=low(experts, block, SPAN),
-        d_mid_in=low(experts, block, 2 * SPAN), mid_out=low(experts, block, SPAN),
+        d_mid_in=low(experts, block, 2 * SPAN), d_joint=low(2, block, 2 * FF), mid_out=low(experts, block, SPAN),
         x_all=low(block, width), g_all=low(block, width), h1=low(block, width), h2=low(block, width),
         hot_all=low(block, 128), mask=full(block, 128), cosine=full(block, 128), sine=full(block, 128),
         mids=low(block, 3 * SPAN), kvall=low(planes, 4, block, 128), kv_out=low(4, block, 128), q_out=low(4, block, 128),
@@ -1178,18 +1237,17 @@
         delta=full(4, 1, 2 * block), acc=full(4, HEAD, 2 * block), dqt=full(4, HEAD, 2 * block),
         att_all=low(2, block, heads), halves=full(2, block, width), half_mid=full(2, block, SPAN), mid_o=low(block, SPAN), x2=full(block, width),
         gates=full(block, 2 * experts), dgates=full(block, 128), trade=low(2, block, width), out_trade=low(2, rows, width),
-        norm_trade=low(2, rows, width), mid_trade=low(2, block, 3 * SPAN), dg_trade=full(2, 8, block),
+        norm_trade=low(2, rows, width), dg_trade=full(2, 8, block),
         pack=low(2, 4, grad_rows, width), core_land=low(2, 2, grad_rows, width), x_land=low(2, grad_rows, width),
         z_land=low(2, planes, *piece), early=low(64, width), late=low(128, width),
-        early_land=low(blocks, 16, early_width), late_land=low(blocks, 16, late_width),
+        early_land=low(2 * blocks, 16, early_width), late_land=low(2 * blocks, 16, late_width),
         from_up=low(kept, 4, block, 128), credit=pltpu.SemaphoreType.REGULAR,
-        load_sem=dma(5), expert_sem=dma(slots, 4), pair_send=dma(14), pair_recv=dma(14),
-        kv_send=dma(4, 2), kv_recv=dma(4, 2), q_send=dma(4), q_recv=dma(4), d_send=dma(4), d_recv=dma(4),
-        dq_send=dma(4), dq_recv=dma(4), dkv_send=dma(4), dkv_recv=dma(4), up_send=dma(planes, 2),
-        up_recv=dma(planes, 2), ow_send=dma(4, 2), ow_recv=dma(4), att_send=dma(4, 2), att_recv=dma(2, 4), core_send=dma(2, 2), core_recv=dma(2, 2),
-        x_send=dma(2), x_recv=dma(2), z_send=dma(2, 2, planes), z_recv=dma(2, 2, planes), last_send=dma(2, 2, 4),
+        packed=low(base + 448, width), load_sem=dma(5), expert_sem=dma(slots, 4), pair_send=dma(17), pair_recv=dma(17),
+        kv_send=dma(3), kv_recv=dma(3), piece_send=dma(4), piece_recv=dma(4), up_send=dma(planes, 3),
+        up_recv=dma(planes, 3), ow_send=dma(4, 2), ow_recv=dma(4), att_send=dma(2), att_recv=dma(2), core_send=dma(2, 2), core_recv=dma(2, 2),
+        x_send=dma(2), x_recv=dma(2), z_send=dma(2, 2), z_recv=dma(2, 2), last_send=dma(2, 2, 4),
         last_recv=dma(2, 4),
-        small_send=dma(2, 2, blocks), small_recv=dma(2, 2, blocks), down_send=dma(planes),
+        small_send=dma(2, 2), small_recv=dma(2, 2), down_send=dma(planes),
         down_recv=dma(planes),
     )
     (out,) = pl.pallas_call(
@@ -1198,7 +1256,7 @@
         in_specs=[
             SMEM if name in ("starts", "adapters") else HBM if name.endswith("hbm") else VMEM for name in INPUTS
         ],
-        out_specs=[VMEM] * len(OUTPUTS),
+        out_specs=[HBM] * len(OUTPUTS),
         scratch_shapes=list(scratch.values()),
         compiler_params=pltpu.CompilerParams(
             collective_id=1, has_side_effects=True, vmem_limit_bytes=62 << 20

time: 154 us -> 152 us (0.987); the launches traced: 154 us -> 151 us
  Pallas kernels: 153 us -> 150 us
    pallas_call x1, Pallas kernels: 149 us -> 146 us  [per_device(): pl.pallas_call(functools.partial(layer_kernel, planes, slots, INPUTS + OU...]
where the time goes in v5:
time: 152 us; the launch traced here: 151 us
  Pallas kernels  150 us (99%)
    pallas_call x1, Pallas kernels, per_device(): pl.pallas_call(functools.partial(layer_kernel, planes, slots, INPUTS + OU...  146 us
    pallas_call x1, Pallas kernels, per_device(): pl.pallas_call(unpack_kernel, out_shape=[unpacked[name] for name in RESUL...  3.93 us

profile of v5, /device:TPU:0, one launch (start us, length us, event | category | flops | bytes accessed | tf_op | source)
XLA Modules:
  0.0 150.7 jit_solution(4831449786691982807)
XLA Ops:
  0.7 145.9 %layer.1.packed = bf16[1600,1024]{1,0:T(8,128)(2,1)} custom-call(bf16[128,1024]{1,0:T(8,128)(2,1)} %refs_0_.1, bf16[128,1024]{1,0:T(8,128)(2,1)} %refs_1_.1, s32[8,128]{1,0:T(8,128)} %bitcast.17, s32[8]{0:T(128)} %refs_3_.1, s32[8]{0:T(128)} %refs_4_.1, f32[1,1024]{1,0:T(1,128)} %bitcast.18, f32[1,1024]{1,0:T(1,128)} %bitcast.19, ...), custom_call_target="tpu_custom_call" | custom-call | tf_op jit(solution)/shard_map/layer/pallas_call | solution.py:1253
  146.6 3.9 %unpack.1 = (f32[8,64,1024]{2,1,0:T(8,128)}, f32[8,2,32,512]{3,2,1,0:T(8,128)}, f32[8,32,512]{2,1,0:T(8,128)}, f32[8,32,1024]{2,1,0:T(8,128)}, bf16[128,1024]{1,...) custom-call(bf16[1600,1024]{1,0:T(8,128)(2,1)} %layer.1.packed), custom_call_target="tpu_custom_call" | custom-call | tf_op jit(solution)/shard_map/unpack/pallas_call | solution.py:1274

commit v6 on v5

--- a/solution.py
+++ b/solution.py
@@ -707,14 +707,14 @@
         r.mid_out[e] = scaled_mid
         r.acc_out[...] += dot((act.astype(F32) * gate).astype(BF16), r.w_out[slot])
 
-        @pl.when(turn < experts - 2)
+        @pl.when(turn < experts - slots)
         def _():
             r.acc_h2[...] += dot(d_gp, r.w_in[slot, :, :FF], NT) + dot(d_up, r.w_in[slot, :, FF:], NT)
 
-        @pl.when(turn >= experts - 2)
-        def _():
-            r.d_joint[turn - (experts - 2), :, :FF] = d_gp
-            r.d_joint[turn - (experts - 2), :, FF:] = d_up
+        @pl.when(turn >= experts - slots)
+        def _():
+            r.d_joint[slot, :, :FF] = d_gp
+            r.d_joint[slot, :, FF:] = d_up
 
         r.pack[half, q, :64, :] = dot(d_mid_in, h2, TN).astype(BF16)
         r.pack[half, q, 64:96, :FF] = dot(mid_in[:, :SPAN], d_gp, TN).astype(BF16)
@@ -763,8 +763,8 @@
     for number in range(r.acc_h2.shape[1] // tile):
         columns = slice(tile * number, tile * number + tile)
         ends = r.acc_h2[:, columns] + dot(all_d_mids, r.in_down[:, :, columns].reshape(experts * lanes, tile))
-        for index in (0, 1):
-            ends = ends + dot(r.d_joint[index], r.w_in[(experts - 2 + index) % slots, columns, :], NT)
+        for slot in range(slots):
+            ends = ends + dot(r.d_joint[slot], r.w_in[slot, columns, :], NT)
         r.trade[ep, :, columns] = ends.astype(BF16)
         part = r.trade.at[ep, :, columns]
         copy = swap((10, 3, 15, 16)[number], part, part)
@@ -933,17 +933,36 @@
             r.dqt[b] += dot(kv, d_s, TN)[:HEAD]
         r.kvall[p, kb] = grown.astype(BF16)
 
-    def lower(p):
-        return remote(r.kvall.at[p], r.from_up.at[p % kept], r.down_send.at[p], r.down_recv.at[p], down)
-
-    def finish(p):
+    def lower(p, kb):
+        return remote(
+            r.kvall.at[p, kb], r.from_up.at[p % kept, kb], r.down_send.at[p, kb], r.down_recv.at[p, kb], down
+        )
+
+    def back_to(source, landing, send, recv, b):
+        return remote(source.at[b], landing.at[head], send, recv, device_of(b))
+
+    def give_back(source, landing, send, recv, b):
+        @pl.when(b == head)
+        def _():
+            landing[b] = source[b]
+
+        @pl.when(b != head)
+        def _():
+            back_to(source, landing, send, recv, b).start()
+
+    dq_pieces = (r.dq_out, r.dq_in, r.piece_send.at[2], r.piece_recv.at[2])
+    dkv_pieces = (r.kvall.at[z], r.dkv_in, r.piece_send.at[3], r.piece_recv.at[3])
+
+    def pass_on(step):
+        p, kb = step // 4, step % 4
+
         @pl.when(z < planes - 1)
         def _():
-            lower(p).wait_recv()
-            r.kvall[p] = (r.kvall[p].astype(F32) + r.from_up[p % kept].astype(F32)).astype(BF16)
+            lower(p, kb).wait_recv()
+            r.kvall[p, kb] = (r.kvall[p, kb].astype(F32) + r.from_up[p % kept, kb].astype(F32)).astype(BF16)
             if planes > kept:
 
-                @pl.when(p + kept <= z)
+                @pl.when((kb == 3) & (p + kept <= z))
                 def _():
                     pl.semaphore_signal(r.credit, inc=1, device_id=up, device_id_type=MESH)
 
@@ -951,26 +970,24 @@
         def _():
             if planes > kept:
 
-                @pl.when(p >= kept)
+                @pl.when((kb == 0) & (p >= kept))
                 def _():
                     pl.semaphore_wait(r.credit, 1)
 
-            lower(p).start()
-
-    def back_to(source, landing, send, recv, b):
-        return remote(source.at[b], landing.at[head], send, recv, device_of(b))
-
-    def give_back(source, landing, send, recv, b):
-        @pl.when(b == head)
-        def _():
-            landing[b] = source[b]
-
-        @pl.when(b != head)
-        def _():
-            back_to(source, landing, send, recv, b).start()
-
-    dq_pieces = (r.dq_out, r.dq_in, r.piece_send.at[2], r.piece_recv.at[2])
-    dkv_pieces = (r.kvall.at[z], r.dkv_in, r.piece_send.at[3], r.piece_recv.at[3])
+            lower(p, kb).start()
+
+        @pl.when(p == z)
+        def _():
+            give_back(*dkv_pieces, kb)
+
+    def after(step):
+        @pl.when(z == planes - 1)
+        def _():
+            pass_on(step)
+
+        @pl.when((z < planes - 1) & (step >= 2))
+        def _():
+            pass_on(step - 2)
 
     def plane_back(p, carry):
         @pl.when(p < z)
@@ -978,22 +995,14 @@
             @pl.when(p == 0)
             def _():
                 back_step(p, 0, [(b, True) for b in range(4)])
+                after(0)
 
             def middle(kb, inner):
                 back_step(p, kb, [(b, False) for b in range(4)])
+                after(4 * p + kb)
                 return inner
 
-            lax.fori_loop(jnp.where(p == 0, 1, 0), 2, middle, 0)
-
-            @pl.when((p > 0) & (z < planes - 1))
-            def _():
-                finish(p - 1)
-
-            lax.fori_loop(2, 4, middle, 0)
-
-            @pl.when(z == planes - 1)
-            def _():
-                finish(p)
+            lax.fori_loop(jnp.where(p == 0, 1, 0), 4, middle, 0)
 
         @pl.when(p == z)
         def _():
@@ -1001,16 +1010,7 @@
                 back_step(p, kb, [(b, b == kb or kb == 0) for b in range(kb, 4)])
                 r.dq_out[kb] = (unstack(r.dqt[kb]) * SCALE).astype(BF16)
                 give_back(*dq_pieces, kb)
-
-                @pl.when(z == planes - 1)
-                def _():
-                    give_back(*dkv_pieces, kb)
-
-                if kb == 1:
-
-                    @pl.when((p > 0) & (z < planes - 1))
-                    def _():
-                        finish(p - 1)
+                after(4 * p + kb)
 
         @pl.when(p == 0)
         def _():
@@ -1030,9 +1030,8 @@
 
     @pl.when(z < planes - 1)
     def _():
-        finish(z)
-        for b in range(4):
-            give_back(*dkv_pieces, b)
+        pass_on(4 * z + 2)
+        pass_on(4 * z + 3)
 
     cosine, sine = r.cosine[...], r.sine[...]
     wait_received(three_pieces, r.piece_recv.at[2])
@@ -1099,7 +1098,8 @@
     hand_on(sibling, 1, beside).wait_send()
 
     def drain(p, carry):
-        lower(p).wait_send()
+        for kb in range(4):
+            lower(p, kb).wait_send()
         return carry
 
     lax.fori_loop(0, z, drain, 0)
@@ -1226,7 +1226,7 @@
         in_down=low(experts, 2 * SPAN, width), w_in_up=low(slots, *expert_in_up.shape[1:]),
         w_out_down=low(slots, SPAN, FF), out_up=low(experts, SPAN, width),
         mid_in=low(experts, block, 2 * SPAN), lifted=low(experts, block, SPAN),
-        d_mid_in=low(experts, block, 2 * SPAN), d_joint=low(2, block, 2 * FF), mid_out=low(experts, block, SPAN),
+        d_mid_in=low(experts, block, 2 * SPAN), d_joint=low(slots, block, 2 * FF), mid_out=low(experts, block, SPAN),
         x_all=low(block, width), g_all=low(block, width), h1=low(block, width), h2=low(block, width),
         hot_all=low(block, 128), mask=full(block, 128), cosine=full(block, 128), sine=full(block, 128),
         mids=low(block, 3 * SPAN), kvall=low(planes, 4, block, 128), kv_out=low(4, block, 128), q_out=low(4, block, 128),
@@ -1247,8 +1247,8 @@
         up_recv=dma(planes, 3), ow_send=dma(4, 2), ow_recv=dma(4), att_send=dma(2), att_recv=dma(2), core_send=dma(2, 2), core_recv=dma(2, 2),
         x_send=dma(2), x_recv=dma(2), z_send=dma(2, 2), z_recv=dma(2, 2), last_send=dma(2, 2, 4),
         last_recv=dma(2, 4),
-        small_send=dma(2, 2), small_recv=dma(2, 2), down_send=dma(planes),
-        down_recv=dma(planes),
+        small_send=dma(2, 2), small_recv=dma(2, 2), down_send=dma(planes, 4),
+        down_recv=dma(planes, 4),
     )
     (out,) = pl.pallas_call(
         functools.partial(layer_kernel, planes, slots, INPUTS + OUTPUTS + tuple(scratch)),

time: 152 us -> 146 us (0.961)
  Pallas kernels: 150 us -> 145 us
    pallas_call x1, Pallas kernels: 146 us -> 141 us  [per_device(): pl.pallas_call(functools.partial(layer_kernel, planes, slots, INPUTS + OU...]
where the time goes in v6:
time: 146 us
  Pallas kernels  145 us (99%)
    pallas_call x1, Pallas kernels, per_device(): pl.pallas_call(functools.partial(layer_kernel, planes, slots, INPUTS + OU...  141 us
    pallas_call x1, Pallas kernels, per_device(): pl.pallas_call(unpack_kernel, out_shape=[unpacked[name] for name in RESUL...  3.93 us

profile of v6, /device:TPU:0, one launch (start us, length us, event | category | flops | bytes accessed | tf_op | source)
XLA Modules:
  0.0 146.1 jit_solution(11381349249154577820)
XLA Ops:
  0.7 141.3 %layer.1.packed = bf16[1600,1024]{1,0:T(8,128)(2,1)} custom-call(bf16[128,1024]{1,0:T(8,128)(2,1)} %refs_0_.1, bf16[128,1024]{1,0:T(8,128)(2,1)} %refs_1_.1, s32[8,128]{1,0:T(8,128)} %bitcast.17, s32[8]{0:T(128)} %refs_3_.1, s32[8]{0:T(128)} %refs_4_.1, f32[1,1024]{1,0:T(1,128)} %bitcast.18, f32[1,1024]{1,0:T(1,128)} %bitcast.19, ...), custom_call_target="tpu_custom_call" | custom-call | tf_op jit(solution)/shard_map/layer/pallas_call | solution.py:1253
  142.0 3.9 %unpack.1 = (f32[8,64,1024]{2,1,0:T(8,128)}, f32[8,2,32,512]{3,2,1,0:T(8,128)}, f32[8,32,512]{2,1,0:T(8,128)}, f32[8,32,1024]{2,1,0:T(8,128)}, bf16[128,1024]{1,...) custom-call(bf16[1600,1024]{1,0:T(8,128)(2,1)} %layer.1.packed), custom_call_target="tpu_custom_call" | custom-call | tf_op jit(solution)/shard_map/unpack/pallas_call | solution.py:1274

commit v7 on v6

--- a/solution.py
+++ b/solution.py
@@ -158,6 +158,8 @@
     owners = 4 * groups
     piece = (grad_rows // groups, r.pack.shape[3] // 4)
     kept = r.from_up.shape[0]
+    deferred = r.d_joint.shape[0]
+    heads = r.q_hbm.shape[1]
 
     load_q = pltpu.make_async_copy(r.q_hbm, r.q_w, r.load_sem.at[0])
     load_kv = pltpu.make_async_copy(r.kv_hbm, r.kv_w, r.load_sem.at[1])
@@ -268,7 +270,6 @@
     three_pieces = r.q_out.at[pl.ds(0, 3)]
 
     query_pieces = (r.q_out, r.q_in, r.piece_send.at[0], r.piece_recv.at[0])
-    grad_pieces = (r.d_out, r.d_in, r.piece_send.at[1], r.piece_recv.at[1])
 
     def climb(p, half):
         part = r.kvall.at[p, :, chunks[half][0], :]
@@ -643,10 +644,7 @@
             wait_received(pieces(planes - 1), r.z_recv.at[half, 0])
             r.z_land[half, z] = piece_in_pack(half, z % owners)[...]
 
-            def add(p, total):
-                return total + r.z_land[half, p].astype(F32)
-
-            total = lax.fori_loop(0, planes, add, jnp.zeros(piece, F32))
+            total = jnp.sum(r.z_land[half].astype(F32), axis=0)
             piece_in_final(half, z % owners)[...] = total.astype(BF16)
             each_plane(lambda step: spread(half, step).start(), False)
 
@@ -707,14 +705,14 @@
         r.mid_out[e] = scaled_mid
         r.acc_out[...] += dot((act.astype(F32) * gate).astype(BF16), r.w_out[slot])
 
-        @pl.when(turn < experts - slots)
+        @pl.when(turn < experts - deferred)
         def _():
             r.acc_h2[...] += dot(d_gp, r.w_in[slot, :, :FF], NT) + dot(d_up, r.w_in[slot, :, FF:], NT)
 
-        @pl.when(turn >= experts - slots)
-        def _():
-            r.d_joint[slot, :, :FF] = d_gp
-            r.d_joint[slot, :, FF:] = d_up
+        @pl.when(turn >= experts - deferred)
+        def _():
+            r.d_joint[turn - (experts - deferred), :, :FF] = d_gp
+            r.d_joint[turn - (experts - deferred), :, FF:] = d_up
 
         r.pack[half, q, :64, :] = dot(d_mid_in, h2, TN).astype(BF16)
         r.pack[half, q, 64:96, :FF] = dot(mid_in[:, :SPAN], d_gp, TN).astype(BF16)
@@ -763,17 +761,16 @@
     for number in range(r.acc_h2.shape[1] // tile):
         columns = slice(tile * number, tile * number + tile)
         ends = r.acc_h2[:, columns] + dot(all_d_mids, r.in_down[:, :, columns].reshape(experts * lanes, tile))
-        for slot in range(slots):
-            ends = ends + dot(r.d_joint[slot], r.w_in[slot, columns, :], NT)
-        r.trade[ep, :, columns] = ends.astype(BF16)
-        part = r.trade.at[ep, :, columns]
-        copy = swap((10, 3, 15, 16)[number], part, part)
+        for index in range(deferred):
+            ends = ends + dot(r.d_joint[index], r.w_in[(experts - deferred + index) % slots, columns, :], NT)
+        r.trade[0, :, columns] = jnp.where(ep == 0, ends[rows:], ends[:rows]).astype(BF16)
+        r.own_h2[:, columns] = jnp.where(ep == 0, ends[:rows], ends[rows:])
+        copy = swap((10, 3, 15, 16)[number], r.trade.at[0, :, columns], r.trade.at[1, :, columns])
         copy.start()
         send_h2.append(copy)
     r.acc_out[...] += dot(jnp.concatenate([r.mid_out[e] for e in every], axis=1), r.out_up[...].reshape(experts * SPAN, -1))
     r.out_trade[0] = r.acc_out[theirs, :].astype(BF16)
     send_out = swap(11, r.out_trade.at[0], r.out_trade.at[1])
-    send_out.start()
     stage_own(0)
     stage_pieces(1)
 
@@ -796,7 +793,7 @@
             return landing.at[pl.ds(0, count)]
 
         def scatter():
-            def step(index, carry):
+            def act(index):
                 owner = lax.rem(me + index, blocks)
                 side = jnp.where(owner < shared, owner % 2, ep)
 
@@ -806,29 +803,34 @@
                         region(source, owner), landing.at[own_index], send_one, recv_one, {"ctx": owner, "ep": side}
                     ).start()
 
-                return carry
-
-            lax.fori_loop(0, blocks, step, 0)
-
-        def add(first, count):
-            def step(p, sums):
-                return sums + landing[p].astype(F32)
-
-            return lax.fori_loop(first, first + count, step, jnp.zeros(landing.shape[1:], F32))
+            each_block(act)
+
+        def add(pieces):
+            return jnp.sum(pieces.astype(F32), axis=0).astype(BF16)
+
+        def each_block(act):
+            if blocks <= 16:
+                for index in range(blocks):
+                    act(index)
+            else:
+
+                def step(index, carry):
+                    act(index)
+                    return carry
+
+                lax.fori_loop(0, blocks, step, 0)
 
         def tell(side):
             part = region(result, me % holders)
 
-            def step(index, carry):
+            def act(index):
                 device = lax.rem(me + index, blocks)
 
                 @pl.when((index > 0) | (side != ep))
                 def _():
                     remote(part, part, send_two, recv_two, {"ctx": device, "ep": side}).start()
 
-                return carry
-
-            lax.fori_loop(0, blocks, step, 0)
+            each_block(act)
 
         def total():
             @pl.when(mine_too)
@@ -838,7 +840,7 @@
             @pl.when(mine_too & private)
             def _():
                 wait_received(several(blocks - 1), recv_one)
-                region(result, me % holders)[...] = add(blocks * ep, blocks).astype(BF16)
+                region(result, me % holders)[...] = add(landing[pl.ds(blocks * ep, blocks)])
                 tell(ep)
 
             if shared:
@@ -846,7 +848,7 @@
                 @pl.when(mine_too & jnp.logical_not(private))
                 def _():
                     wait_received(several(2 * blocks - 1), recv_one)
-                    region(result, me % holders)[...] = add(0, 2 * blocks).astype(BF16)
+                    region(result, me % holders)[...] = add(landing[...])
                     tell(ep)
                     tell(1 - ep)
 
@@ -873,42 +875,54 @@
 
         return scatter, total, finish
 
-    early_scatter, early_total, early_finish = small_sum(0, r.early, r.early_land, r.early_out, 0)
+    early_scatter, early_total, early_finish = small_sum(0, r.early, r.early_land, r.early_out, 4)
     late_scatter, late_total, late_finish = small_sum(1, r.late, r.late_land, r.late_out, 6)
     drain_forward()
 
     send_dg.wait_recv()
     blank = jnp.zeros((112, block), F32)
     table = jnp.concatenate([r.dg_trade[0], r.dg_trade[1], blank], axis=0).T
-    d_gates = table[:, : 2 * experts]
-    gates = r.gates[...]
+    r.dgates[:, : 2 * experts] = table[:, : 2 * experts]
+    d_gates = r.dgates[mine, : 2 * experts]
+    gates = r.gates[mine, :]
     d_logits = (gates * (d_gates - jnp.sum(gates * d_gates, axis=1, keepdims=True))).astype(BF16)
     from_router = dot(d_logits, r.router[...])
     stage_column(0)
     for copy in send_h2:
         copy.wait_recv()
-    d_h2 = r.trade[0].astype(F32) + r.trade[1].astype(F32) + from_router
-    d_x2 = r.g_all[...].astype(F32) + rms_back(r.x2[...], r.moe_gain[...], d_h2)
+    d_h2 = r.own_h2[...] + r.trade[1].astype(F32) + from_router
+    d_x2 = r.grad[...].astype(F32) + rms_back(r.x2[mine, :], r.moe_gain[...], d_h2)
     d_attn = d_x2.astype(BF16)
-    r.acc_h2[...] = d_x2
-    d_mid_o = (dot(d_attn, r.o_up[...], NT) * r.mask[:, :SPAN]).astype(BF16)
-
-    d_att = (dot(d_attn, r.ow_all[ep], NT) + dot(d_mid_o, r.od_all[ep])).astype(BF16)
-    for number in range(4):
-        r.d_out[number] = d_att[:, 128 * number : 128 * number + 128]
-    for step in (1, 2, 3):
-        piece_to(*grad_pieces, step).start()
+    r.own_h2[...] = d_x2
+    d_mid_o = (dot(d_attn, r.o_up[...], NT) * r.mask[mine, :SPAN]).astype(BF16)
+
+    def grad_to(side, number):
+        return remote(
+            r.d_out.at[side, number], r.d_in.at[2 * head + ep], r.piece_send.at[1], r.piece_recv.at[1],
+            {"ctx": 4 * z + number, "ep": side},
+        )
+
+    for side in (0, 1):
+        d_att = (dot(d_attn, r.ow_all[side], NT) + dot(d_mid_o, r.od_all[side])).astype(BF16)
+        for number in range(4):
+            r.d_out[side, number] = d_att[:, 128 * number : 128 * number + 128]
+
+            @pl.when((side != ep) | (number != head))
+            def _():
+                grad_to(side, number).start()
+
+    send_out.start()
     r.dqt[...] = jnp.zeros(r.dqt.shape, F32)
-    r.early[:32, :] = dot(r.mid_o[...], d_attn, TN).astype(BF16)
-    r.early[32:48, :] = fold(dot(d_mid_o, r.att_all[ep], TN)).astype(BF16)
-    r.early[48:, :] = jnp.zeros((16, r.early.shape[1]), BF16)
+    r.early[:32, :] = dot(r.mid_o[mine, :], d_attn, TN).astype(BF16)
+    for side in (0, 1):
+        r.early[32:, heads * side : heads * side + heads] = dot(d_mid_o, r.att_all[side, mine, :], TN).astype(BF16)
     early_scatter()
     stage_own(1)
 
-    r.d_in[head] = r.d_out[head]
-    wait_received(three_pieces, r.piece_recv.at[1])
+    r.d_in[2 * head + ep] = r.d_out[ep, head]
+    wait_received(r.d_in.at[pl.ds(0, 7)], r.piece_recv.at[1])
     for b in range(4):
-        received = r.d_in[b].astype(F32)
+        received = r.d_in[2 * b : 2 * b + 2].reshape(block, 128).astype(F32)
         turned = stack_columns(received)
         r.dt[b, HEAD:, :] = turned.astype(BF16)
         r.delta[b] = jnp.sum(turned * r.acc[b], axis=0, keepdims=True)
@@ -1063,6 +1077,9 @@
     stage_core(1)
     stage_end(0)
     early_finish()
+    both = r.early_out[32:64, :]
+    own_half = jnp.where(ep == 0, both[:, :heads].astype(F32), both[:, heads:].astype(F32))
+    r.early_out[32:48, :] = fold(own_half).astype(BF16)
     send_out.wait_recv()
     r.block_out[...] = (r.x2[mine, :] + (r.acc_out[mine, :] + r.out_trade[1].astype(F32))).astype(BF16)
     own = jnp.where(ep == 0, first, second)
@@ -1080,7 +1097,7 @@
     send_norm.wait_recv()
     own = own + r.norm_trade[1].astype(F32)
     r.in_grad[...] = (
-        r.acc_h2[mine, :] + rms_back(r.x_all[mine, :].astype(F32), r.attn_gain[...], own)
+        r.own_h2[...] + rms_back(r.x_all[mine, :].astype(F32), r.attn_gain[...], own)
     ).astype(BF16)
     stores.append(store(3, base + 256, 128))
     stores[-1].start()
@@ -1091,7 +1108,8 @@
         copy.wait_send()
     wait_sent(r.o_out.at[pl.ds(0, 3)], r.att_send.at[0])
     wait_sent(r.o_out, r.att_send.at[1])
-    for number in (1, 2, 3):
+    wait_sent(r.d_in.at[pl.ds(0, 7)], r.piece_send.at[1])
+    for number in (2, 3):
         wait_sent(three_pieces, r.piece_send.at[number])
     hand_on(head, 0, across).wait_send()
     hand_on(head, 1, beside).wait_send()
@@ -1226,17 +1244,17 @@
         in_down=low(experts, 2 * SPAN, width), w_in_up=low(slots, *expert_in_up.shape[1:]),
         w_out_down=low(slots, SPAN, FF), out_up=low(experts, SPAN, width),
         mid_in=low(experts, block, 2 * SPAN), lifted=low(experts, block, SPAN),
-        d_mid_in=low(experts, block, 2 * SPAN), d_joint=low(slots, block, 2 * FF), mid_out=low(experts, block, SPAN),
+        d_mid_in=low(experts, block, 2 * SPAN), d_joint=low(2, block, 2 * FF), mid_out=low(experts, block, SPAN),
         x_all=low(block, width), g_all=low(block, width), h1=low(block, width), h2=low(block, width),
         hot_all=low(block, 128), mask=full(block, 128), cosine=full(block, 128), sine=full(block, 128),
         mids=low(block, 3 * SPAN), kvall=low(planes, 4, block, 128), kv_out=low(4, block, 128), q_out=low(4, block, 128),
-        q_in=low(4, block, 128), d_out=low(4, block, 128), d_in=low(4, block, 128), o_out=low(4, block, 128),
+        q_in=low(4, block, 128), d_out=low(2, 4, rows, 128), d_in=low(8, rows, 128), own_h2=full(rows, width), o_out=low(4, block, 128),
         dq_out=low(4, block, 128), dq_in=low(4, block, 128), dkv_in=low(4, block, 128), qt=low(4, 128, 2 * block),
         qn=low(4, 2 * block, 128), dt=low(4, 128, 2 * block), dn=low(4, 2 * block, 128),
         m_s=full(4, 1, 2 * block), l_s=full(4, 1, 2 * block), lse=full(4, 1, 2 * block),
         delta=full(4, 1, 2 * block), acc=full(4, HEAD, 2 * block), dqt=full(4, HEAD, 2 * block),
         att_all=low(2, block, heads), halves=full(2, block, width), half_mid=full(2, block, SPAN), mid_o=low(block, SPAN), x2=full(block, width),
-        gates=full(block, 2 * experts), dgates=full(block, 128), trade=low(2, block, width), out_trade=low(2, rows, width),
+        gates=full(block, 2 * experts), dgates=full(block, 128), trade=low(2, rows, width), out_trade=low(2, rows, width),
         norm_trade=low(2, rows, width), dg_trade=full(2, 8, block),
         pack=low(2, 4, grad_rows, width), core_land=low(2, 2, grad_rows, width), x_land=low(2, grad_rows, width),
         z_land=low(2, planes, *piece), early=low(64, width), late=low(128, width),

time: 146 us -> 143 us (0.979)
  Pallas kernels: 145 us -> 142 us
    pallas_call x1, Pallas kernels: 141 us -> 138 us  [per_device(): pl.pallas_call(functools.partial(layer_kernel, planes, slots, INPUTS + OU...]
where the time goes in v7:
time: 143 us
  Pallas kernels  142 us (99%)
    pallas_call x1, Pallas kernels, per_device(): pl.pallas_call(functools.partial(layer_kernel, planes, slots, INPUTS + OU...  138 us
    pallas_call x1, Pallas kernels, per_device(): pl.pallas_call(unpack_kernel, out_shape=[unpacked[name] for name in RESUL...  3.93 us

profile of v7, /device:TPU:0, one launch (start us, length us, event | category | flops | bytes accessed | tf_op | source)
XLA Modules:
  0.0 143.0 jit_solution(17388198026312162276)
XLA Ops:
  0.7 138.2 %layer.1.packed = bf16[1600,1024]{1,0:T(8,128)(2,1)} custom-call(bf16[128,1024]{1,0:T(8,128)(2,1)} %refs_0_.1, bf16[128,1024]{1,0:T(8,128)(2,1)} %refs_1_.1, s32[8,128]{1,0:T(8,128)} %bitcast.17, s32[8]{0:T(128)} %refs_3_.1, s32[8]{0:T(128)} %refs_4_.1, f32[1,1024]{1,0:T(1,128)} %bitcast.18, f32[1,1024]{1,0:T(1,128)} %bitcast.19, ...), custom_call_target="tpu_custom_call" | custom-call | tf_op jit(solution)/shard_map/layer/pallas_call | solution.py:1271
  138.9 3.9 %unpack.1 = (f32[8,64,1024]{2,1,0:T(8,128)}, f32[8,2,32,512]{3,2,1,0:T(8,128)}, f32[8,32,512]{2,1,0:T(8,128)}, f32[8,32,1024]{2,1,0:T(8,128)}, bf16[128,1024]{1,...) custom-call(bf16[1600,1024]{1,0:T(8,128)(2,1)} %layer.1.packed), custom_call_target="tpu_custom_call" | custom-call | tf_op jit(solution)/shard_map/unpack/pallas_call | solution.py:1292
